TPU v7x, 32 devices: a whole 2x2x4 slice. The times are simulated.
32 devices in a mesh: dp: 8 (over y, x, core), mp: 4 (over z).
Axes of the slice: x: 2, y: 2, z: 4, core: 2. Of those that a mesh axis runs over, the one named last changes fastest.
Arguments:
- tokens: bfloat16 [16384, 768], P('dp'), may hold values from -6 to 6
- seg_ids: int32 [16384], P('dp'), may hold values from 0 to 64, as said below
- qkv_weight: bfloat16 [3, 768, 768], P(None, None, 'mp'), may hold values from -0.21875 to 0.21875
- qkv_bias: float32 [3, 768], P(None, 'mp'), may hold values from -3 to 3
- out_weight: bfloat16 [768, 768], P('mp'), may hold values from -0.875 to 0.875
- out_bias: float32 [768], replicated, may hold values from -2 to 2
- up_weight: bfloat16 [768, 3072], P(None, 'mp'), may hold values from -0.21875 to 0.21875
- up_bias: float32 [3072], P('mp'), may hold values from -3 to 3
- down_weight: bfloat16 [3072, 768], P('mp'), may hold values from -0.109375 to 0.109375
- down_bias: float32 [768], replicated, may hold values from -2 to 2
- norm1_gain: float32 [768], replicated, may hold values from 0.5 to 1.5
- norm1_shift: float32 [768], replicated, may hold values from -2 to 2
- query_gain: float32 [64], replicated, may hold values from 0.5 to 1.5
- query_shift: float32 [64], replicated, may hold values from -2 to 2
- key_gain: float32 [64], replicated, may hold values from 0.5 to 1.5
- norm2_gain: float32 [768], replicated, may hold values from 0.5 to 1.5
- norm2_shift: float32 [768], replicated, may hold values from -2 to 2
- cotangent: bfloat16 [16384, 768], P('dp'), may hold values from -6 to 6
Outputs:
- block_out: bfloat16 [16384, 768], P(('dp', 'mp'))
- input_grad: bfloat16 [16384, 768], P(('dp', 'mp'))
- qkv_weight_grad: float32 [3, 768, 768], P(None, None, 'mp')
- qkv_bias_grad: float32 [3, 768], P(None, 'mp')
- out_weight_grad: float32 [768, 768], P('mp')
- out_bias_grad: float32 [768], replicated
- up_weight_grad: float32 [768, 3072], P(None, 'mp')
- up_bias_grad: float32 [3072], P('mp')
- down_weight_grad: float32 [3072, 768], P('mp')
- down_bias_grad: float32 [768], replicated
- norm1_gain_grad: float32 [768], replicated
- norm1_shift_grad: float32 [768], replicated
- query_gain_grad: float32 [64], replicated
- query_shift_grad: float32 [64], replicated
- key_gain_grad: float32 [64], replicated
- norm2_gain_grad: float32 [768], replicated
- norm2_shift_grad: float32 [768], replicated
Inputs may be any that keep to these rules, and one draw needn't show every extreme that they name: `seg_ids`: within each packed sequence of 1024 slots the ids run 1, 2, 3 and so on over whole images that are square patch grids of 16 or more patches laid end to end, followed by zeros for padding up to the sequence's end.
All inputs are finite; a program needn't handle non-finite values.
Results may differ from a plain program's by a relative error of at most 0.012.
Values sent between devices are 32-bit elements; how exact they have to be, the bound alone decides.
No kernel may reach another device: no remote copies, remote signals or barrier semaphores. Data moves between devices by JAX's collectives and lax.ppermute only.
A program may use at most 192 MiB of HBM per device.

v0:
```python
import functools
import math

import jax
import jax.numpy as jnp
from jax import lax
from jax.experimental import pallas as pl
from jax.experimental.pallas import tpu as pltpu
from jax.sharding import PartitionSpec as P

F32 = jnp.float32
BF16 = jnp.bfloat16
DH = 64
SEQ_LEN = 1024
NORM_EPS = 1e-06
PIECES = 8
SEG_COLS = 128
LOG2E = math.log2(math.e)
SCALE = DH ** (-0.5)
BITS_A = (2, 4, 1)
BITS_B = (4, 2, 1)
MLP_KIND = ("a", "a", "b", "b")
VMEM_LIMIT = 56 * 1024 * 1024


def mm(a, b):
    return lax.dot_general(a, b, (((1,), (0,)), ((), ())), preferred_element_type=F32)


def mm_nt(a, b):
    return lax.dot_general(a, b, (((1,), (1,)), ((), ())), preferred_element_type=F32)


def mm_tn(a, b):
    return lax.dot_general(a, b, (((0,), (0,)), ((), ())), preferred_element_type=F32)


def call(kernel, out_shape, flops=0, bytes_accessed=0, **kw):
    return pl.pallas_call(
        kernel,
        out_shape=out_shape,
        compiler_params=pltpu.CompilerParams(vmem_limit_bytes=VMEM_LIMIT),
        cost_estimate=pl.CostEstimate(
            flops=flops, bytes_accessed=bytes_accessed, transcendentals=0
        ),
        **kw,
    )


def sds(shape, dtype):
    return jax.ShapeDtypeStruct(shape, dtype)


def row_norm(x):
    mean = jnp.mean(x, axis=-1, keepdims=True)
    cen = x - mean
    rstd = lax.rsqrt(jnp.mean(cen * cen, axis=-1, keepdims=True) + NORM_EPS)
    return cen * rstd, rstd


def row_norm_back(f, n, rstd):
    mean_f = jnp.mean(f, axis=-1, keepdims=True)
    mean_fn = jnp.mean(f * n, axis=-1, keepdims=True)
    return (f - mean_f - n * mean_fn) * rstd


def col_norm(x):
    mean = jnp.mean(x, axis=0, keepdims=True)
    cen = x - mean
    rstd = lax.rsqrt(jnp.mean(cen * cen, axis=0, keepdims=True) + NORM_EPS)
    return cen * rstd, rstd


def col_norm_back(f, n, rstd):
    mean_f = jnp.mean(f, axis=0, keepdims=True)
    mean_fn = jnp.mean(f * n, axis=0, keepdims=True)
    return (f - mean_f - n * mean_fn) * rstd


def lane_fold(x):
    out = x[:, :128]
    for t in range(1, x.shape[1] // 128):
        out = out + x[:, t * 128 : (t + 1) * 128]
    return out


def offset_of(s, bits):
    return sum(bit for t, bit in enumerate(bits) if (s >> t) & 1)


def norm1_kernel(blk_ref, x_ref, g_ref, s_ref, out_ref):
    n, _ = row_norm(x_ref[...].astype(F32))
    out_ref[...] = (n * g_ref[...] + s_ref[...]).astype(BF16)


def build_q_aug(q_pre, qg, qs, qaug_ref):
    n, rstd = col_norm(q_pre)
    q_low = (n * qg + qs).astype(BF16)
    scaled = q_low.astype(F32) * (SCALE * LOG2E)
    hi = scaled.astype(BF16)
    lo = (scaled - hi.astype(F32)).astype(BF16)
    qaug_ref[0:DH, :] = hi
    qaug_ref[DH : 2 * DH, :] = lo
    return n, rstd, q_low


def build_k_aug(k_pre, kg, kaug_ref):
    n, rstd = col_norm(k_pre)
    k_low = (n * kg).astype(BF16)
    kaug_ref[:, 0 : 2 * DH] = jnp.concatenate([k_low, k_low], axis=0).T
    return n, rstd, k_low


def bias_col(b_ref, n):
    return b_ref[...].T[0:n, 0:1]


def prep_kernel(
    me_ref, w_ref, o_ref, qb_ref, ub_ref, up_ref, dn_ref,
    att_ref, ob_ref, b_ref, p_ref, u0_ref, u1_ref, d0_ref, d1_ref,
    t_ref, wf_ref,
):
    part = 24
    e = PIECES * part
    me = me_ref[0]
    b_ref[...] = jnp.zeros(b_ref.shape, F32)
    for s in range(3):
        wf_ref[...] = w_ref[s].astype(F32)
        rows = wf_ref[pl.ds(pl.multiple_of(me * part, 8), part), :]
        att_ref[s * part : (s + 1) * part, :] = rows
        b_ref[0:1, s * e : (s + 1) * e] = qb_ref[s : s + 1, :]
    upart = ub_ref.shape[1]
    for s in range(PIECES // 2):
        b_ref[1:2, s * upart : (s + 1) * upart] = ub_ref[pl.ds(me ^ offset_of(s, BITS_A), 1), :]
    wf_ref[...] = o_ref[...].astype(F32)
    rows = wf_ref[pl.ds(pl.multiple_of(me * part, 8), part), :]
    att_ref[3 * part : 4 * part, :] = rows
    ob_ref[0:part, :] = rows
    att_ref[4 * part :, :] = b_ref[...]
    ob_ref[part:, :] = b_ref[...]

    t_ref[...] = up_ref[...].astype(F32).T

    def at_piece(r):
        return pl.ds(pl.multiple_of((me ^ r) * upart, 32), upart)

    p_ref[0:upart, :] = t_ref[at_piece(0), :]
    p_ref[upart:, :] = dn_ref[at_piece(0), :].astype(F32)
    for i, (u_ref, d_ref) in enumerate(((u0_ref, d0_ref), (u1_ref, d1_ref))):
        for j in range(2):
            u_ref[j] = t_ref[at_piece(offset_of(2 * i + j, BITS_A)), :].astype(BF16)
            d_ref[j] = dn_ref[at_piece(offset_of(2 * i + j, BITS_B)), :]


def attend(x_ref, wt_ref, b_ref, hv_ref, kmask_ref, qhot_ref, outs, qaug_ref, kaug_ref):
    qpre_ref, kpre_ref, vt_ref, mixt_ref, mixf_ref, mixs_ref, l_ref = outs
    e = qpre_ref.shape[0]
    full = x_ref.shape[0]
    share = full // 2
    heads = e // DH
    x = x_ref[...]
    bias = bias_col(b_ref, 3 * e)
    qpre_ref[...] = mm_nt(wt_ref[0:e, :], x) + bias[0:e]
    kpre_ref[...] = mm_nt(wt_ref[e : 2 * e, :], x) + bias[e : 2 * e]
    vt_ref[...] = (mm_nt(wt_ref[2 * e : 3 * e, :], x) + bias[2 * e :]).astype(BF16)
    qaug_ref[2 * DH :, :] = qhot_ref[...]
    kaug_ref[:, 2 * DH :] = kmask_ref[...]
    ones = jnp.ones((16, full), BF16)
    for h in range(heads):
        hs = slice(h * DH, (h + 1) * DH)
        build_q_aug(qpre_ref[hs, :], hv_ref[:, 0:1], hv_ref[:, 1:2], qaug_ref)
        build_k_aug(kpre_ref[hs, :], hv_ref[:, 2:3], kaug_ref)
        prob = jnp.exp2(mm(kaug_ref[...], qaug_ref[...])).astype(BF16)
        vaug = jnp.concatenate([vt_ref[hs, :], ones], axis=0)
        o = mm(vaug, prob)
        total = o[DH : DH + 1, :]
        l_ref[h : h + 1, :] = total
        mix = o[0:DH, :] / total
        mixf_ref[hs, :] = mix
        mixt_ref[hs, :] = mix[:, 0:share].astype(BF16)
        at = h * share
        for c in range(0, share, 256):
            block_no, lane = divmod(at + c, x.shape[1])
            mixs_ref[block_no * DH : (block_no + 1) * DH, lane : lane + 256] = mix[
                :, share + c : share + c + 256
            ]


def attn_fwd_own_kernel(x_ref, wt_ref, b_ref, hv_ref, kmask_ref, qhot_ref, *refs):
    attend(x_ref, wt_ref, b_ref, hv_ref, kmask_ref, qhot_ref, refs[:7], *refs[7:])


def attn_fwd_kernel(
    ia_ref, ib_ref, a0_ref, a1_ref, b0_ref, b1_ref, x_ref, b_ref, hv_ref, kmask_ref, qhot_ref,
    wt_ref, ow_ref, ow1_ref, ow3_ref, *refs,
):
    wa_ref, wb_ref = refs[-2:]
    part = 24
    e = PIECES * part
    half = PIECES // 2
    wa_ref[0:half] = a0_ref[...]
    wa_ref[half:] = a1_ref[...]
    wb_ref[0:half] = b0_ref[...]
    wb_ref[half:] = b1_ref[...]

    def rows(w_ref, i_ref, at):
        return jnp.concatenate(
            [w_ref[i_ref[p], at * part : (at + 1) * part, :] for p in range(PIECES)], axis=0
        ).astype(BF16)

    wt_ref[0:e, :] = rows(wa_ref, ia_ref, 0)
    wt_ref[e : 2 * e, :] = rows(wa_ref, ia_ref, 1)
    wt_ref[2 * e : 3 * e, :] = rows(wb_ref, ib_ref, 0)
    ow_ref[...] = rows(wb_ref, ib_ref, 1)
    ow1_ref[...] = rows(wa_ref, ia_ref, 2)
    ow3_ref[...] = rows(wb_ref, ib_ref, 2)
    attend(x_ref, wt_ref, b_ref, hv_ref, kmask_ref, qhot_ref, refs[:7], *refs[7:9])


def unmix(ref, heads, share):
    width = ref.shape[1]
    rows = []
    for h in range(heads):
        cols = []
        for c in range(0, share, 256):
            block_no, lane = divmod(h * share + c, width)
            cols.append(ref[block_no * DH : (block_no + 1) * DH, lane : lane + 256])
        rows.append(jnp.concatenate(cols, axis=1))
    return jnp.concatenate(rows, axis=0).astype(BF16)


def mix_of(ref, share):
    if ref.dtype == BF16:
        return ref[...]
    return unmix(ref, ref.shape[0] * ref.shape[1] // (DH * share), share)


def out_norm2_kernel(nslot, blk_ref, x_ref, *refs):
    mixes = refs[:nslot]
    ws = refs[nslot : 2 * nslot]
    ob_ref, g_ref, s_ref, mid_ref, sec_ref, secf_ref = refs[2 * nslot :]
    acc = x_ref[...].astype(F32) + ob_ref[...]
    for k in range(nslot):
        acc = acc + mm_tn(mix_of(mixes[k], x_ref.shape[0]), ws[k][...])
    mid_ref[...] = acc
    n, _ = row_norm(acc)
    sec = (n * g_ref[...] + s_ref[...]).astype(BF16)
    sec_ref[...] = sec
    secf_ref[...] = sec.astype(F32)


def mlp_kernel(
    kind, keeps, sec_ref, secp_ref, cot_ref, cotp_ref, u0_ref, u1_ref, d0_ref, d1_ref, b_ref, *refs
):
    if keeps:
        p_ref, hid_ref, gp_ref, ub_ref, db_ref, k0_ref, k1_ref, s0_ref, s1_ref, gb_ref = refs
    else:
        hid_ref, gp_ref, ub_ref, db_ref, up_ref, uq_ref, k0_ref, k1_ref, sd_ref, gb_ref = refs
    part = u0_ref.shape[1]
    share = sec_ref.shape[0]
    up = jnp.concatenate([u0_ref[0], u0_ref[1], u1_ref[0], u1_ref[1]], axis=0).astype(BF16)
    down = jnp.concatenate([d0_ref[0], d1_ref[0], d0_ref[1], d1_ref[1]], axis=0).astype(BF16)
    ub_ref[...] = up
    db_ref[...] = down
    bias = b_ref[1:2, 0 : up.shape[0]]
    for r, (s_ref, c_ref) in enumerate(((sec_ref, cot_ref), (secp_ref, cotp_ref))):
        rows = slice(r * share, (r + 1) * share)
        sec = s_ref[...].astype(BF16)
        cot = c_ref[...].astype(BF16)
        pre = mm_nt(sec, up) + bias
        cdf = 0.5 * (1.0 + lax.erf(pre * (1.0 / math.sqrt(2.0))))
        hid = (pre * cdf).astype(BF16)
        pdf = jnp.exp(-0.5 * pre * pre) * (1.0 / math.sqrt(2.0 * math.pi))
        gpre = (mm_nt(cot, down) * (cdf + pre * pdf)).astype(BF16)
        hid_ref[rows, :] = hid
        gp_ref[rows, :] = gpre
        gb_r = jnp.sum(gpre.astype(F32), axis=0, keepdims=True)
        gd_r = mm_tn(hid, cot)
        gu_r = mm_tn(gpre, sec)
        if r == 0:
            gb, gd, gu = gb_r, gd_r, gu_r
        else:
            gb, gd, gu = gb + gb_r, gd + gd_r, gu + gu_r
    gb_ref[...] = gb
    order = (0, 1, 2, 3) if kind == "a" else (0, 2, 1, 3)
    gu_at = [gu[i * part : (i + 1) * part] for i in order]
    gd_at = [gd[i * part : (i + 1) * part] for i in order]
    if keeps:
        gu_at[3] = gu_at[3] + p_ref[0:part, :]
        gu_at[2] = gu_at[2] + p_ref[part:, :]
        for i, ref in enumerate((k0_ref, k1_ref, s0_ref, s1_ref)):
            ref[0:part, :] = gu_at[i]
            ref[part:, :] = gd_at[i]
    else:
        up_ref[0:part, :] = gu_at[3]
        up_ref[part:, :] = gu_at[2]
        uq_ref[0:part, :] = gu_at[0]
        uq_ref[part:, :] = gu_at[1]
        k0_ref[...] = gd_at[0]
        k1_ref[...] = gd_at[1]
        sd_ref[0:part, :] = gd_at[3]
        sd_ref[part:, :] = gd_at[2]


def down_kernel(nslot, *refs):
    hids = refs[:nslot]
    gps = refs[nslot : 2 * nslot]
    ubs = refs[2 * nslot : 3 * nslot]
    dbs = refs[3 * nslot : 4 * nslot]
    out_ref = refs[4 * nslot]
    cat = lambda refs, axis: jnp.concatenate([r[...] for r in refs], axis=axis)
    out_ref[0] = mm(cat(hids, 1), cat(dbs, 0))
    out_ref[1] = mm(cat(gps, 1), cat(ubs, 0))


def mid_kernel(nslot, idx_ref, mid_ref, own_ref, got_ref, cot_ref, db_ref, g_ref, *refs):
    ows = refs[:nslot]
    mixts = refs[nslot : 2 * nslot]
    gmts = refs[2 * nslot : 3 * nslot]
    bo_ref, gm_ref, gow_keep, gow_send, st_ref = refs[3 * nslot :]
    part = 24
    mid = mid_ref[...]
    bo_ref[...] = (mid + (own_ref[0] + got_ref[0]) + db_ref[...]).astype(BF16)
    n, rstd = row_norm(mid)
    e = own_ref[1] + got_ref[1]
    cot = cot_ref[...].astype(F32)
    gm = cot + row_norm_back(e * g_ref[...], n, rstd)
    gm_ref[...] = gm
    gm_low = gm.astype(BF16)
    st_ref[0:1, :] = jnp.sum(e * n, axis=0, keepdims=True)
    st_ref[1:2, :] = jnp.sum(e, axis=0, keepdims=True)
    st_ref[2:3, :] = jnp.sum(gm_low.astype(F32), axis=0, keepdims=True)
    st_ref[3:4, :] = jnp.sum(cot, axis=0, keepdims=True)
    st_ref[4:8, :] = jnp.zeros((4, mid.shape[1]), F32)
    for k in range(nslot):
        gmts[k][...] = mm_nt(ows[k][...], gm_low).astype(gmts[k].dtype)
        g = mm(mix_of(mixts[k], mid.shape[0]), gm_low)
        for p in range(PIECES):
            at = idx_ref[p]
            rows = slice(k * part, (k + 1) * part)

            @pl.when(at < PIECES // 2)
            def _():
                gow_keep[at, rows, :] = g[p * part : (p + 1) * part, :]

            @pl.when(at >= PIECES // 2)
            def _():
                gow_send[at - PIECES // 2, rows, :] = g[p * part : (p + 1) * part, :]


def attn_bwd_kernel(
    first, idx_ref, x_ref, qpre_ref, kpre_ref, vt_ref, wt_ref, gmt_ref, gmtp_ref, mixf_ref, l_ref,
    hv_ref, kmask_ref, qhot_ref, *refs
):
    if first:
        gk_ref, gs_ref, gn_ref, st_ref, gb_ref, qaug_ref, kaug_ref, gpt_ref = refs
    else:
        gn_in, gk_ref, gs_ref, gn_ref, st_ref, gb_ref, qaug_ref, kaug_ref, gpt_ref = refs
    part = 24
    e = PIECES * part
    full = x_ref.shape[0]
    heads = e // DH
    qaug_ref[2 * DH :, :] = qhot_ref[...]
    kaug_ref[:, 2 * DH :] = kmask_ref[...]
    qg, qs, kg = hv_ref[:, 0:1], hv_ref[:, 1:2], hv_ref[:, 2:3]
    qg_sum = jnp.zeros((DH, 128), F32)
    qs_sum = jnp.zeros((DH, 128), F32)
    kg_sum = jnp.zeros((DH, 128), F32)
    row_no = lax.broadcasted_iota(jnp.int32, (DH, full), 0)
    one_rows = (row_no < 3).astype(F32).astype(BF16)
    for h in range(heads):
        hs = slice(h * DH, (h + 1) * DH)
        qn, qr, q_low = build_q_aug(qpre_ref[hs, :], qg, qs, qaug_ref)
        kn, kr, k_low = build_k_aug(kpre_ref[hs, :], kg, kaug_ref)
        inv = 1.0 / l_ref[h : h + 1, :]
        gm = jnp.concatenate(
            [gmt_ref[hs, :].astype(F32), gmtp_ref[hs, :].astype(BF16).astype(F32)], axis=1
        )
        go_low = (gm * inv).astype(BF16)
        delta = -jnp.sum(go_low.astype(F32) * mixf_ref[hs, :], axis=0, keepdims=True)
        d0 = delta.astype(BF16).astype(F32)
        d1 = (delta - d0).astype(BF16).astype(F32)
        d2 = delta - d0 - d1
        extra = jnp.where(
            row_no == 0, d0, jnp.where(row_no == 1, d1, jnp.where(row_no == 2, d2, 0.0))
        ).astype(BF16)
        goaug = jnp.concatenate([go_low, extra], axis=0)
        vaug = jnp.concatenate([vt_ref[hs, :], one_rows], axis=0).T
        prob = jnp.exp2(mm(kaug_ref[...], qaug_ref[...]))
        ds = (prob * mm(vaug, goaug)).astype(BF16)
        gv = mm_nt(go_low, prob.astype(BF16))
        gk = mm_nt(q_low, ds) * SCALE
        gq = mm(k_low, ds) * SCALE
        qg_sum += lane_fold(gq * qn)
        qs_sum += lane_fold(gq)
        kg_sum += lane_fold(gk * kn)
        gpt_ref[h * DH : (h + 1) * DH, :] = col_norm_back(gq * qg, qn, qr).astype(BF16)
        gpt_ref[e + h * DH : e + (h + 1) * DH, :] = col_norm_back(gk * kg, kn, kr).astype(BF16)
        gpt_ref[2 * e + h * DH : 2 * e + (h + 1) * DH, :] = gv.astype(BF16)
    st_ref[0] = qg_sum
    st_ref[1] = qs_sum
    st_ref[2] = kg_sum
    gp = gpt_ref[...]
    gb_ref[...] = lane_fold(gp.astype(F32))
    gw = mm(gp, x_ref[...])

    def put(ref, at, p):
        for s in range(3):
            ref[at, s * part : (s + 1) * part, :] = gw[s * e + p * part : s * e + (p + 1) * part, :]

    for p in range(PIECES):
        at = idx_ref[p]

        @pl.when(at < PIECES // 2)
        def _():
            put(gk_ref, at, p)

        @pl.when(at >= PIECES // 2)
        def _():
            put(gs_ref, at - PIECES // 2, p)

    gn = mm_tn(gp, wt_ref[...])
    gn_ref[...] = gn if first else gn_in[...] + gn


def norm1_stats_kernel(blk_ref, x_ref, gn_ref, out_ref):
    n, _ = row_norm(x_ref[...].astype(F32))
    e = gn_ref[...]

    @pl.when(pl.program_id(0) == 0)
    def _():
        out_ref[...] = jnp.zeros_like(out_ref)

    out_ref[0:1, :] += jnp.sum(e * n, axis=0, keepdims=True)
    out_ref[1:2, :] += jnp.sum(e, axis=0, keepdims=True)


def final_kernel(blk_ref, x_ref, gn_ref, got_ref, gm_ref, g_ref, out_ref):
    n, rstd = row_norm(x_ref[...].astype(F32))
    f = (gn_ref[...] + got_ref[...]) * g_ref[...]
    out_ref[...] = (gm_ref[...] + row_norm_back(f, n, rstd)).astype(BF16)


def both(refs, to_ref):
    half = PIECES // 2
    to_ref[0:half] = refs[0][...]
    to_ref[half:] = refs[1][...]


def lay_out(refs, to_ref):
    part = to_ref.shape[1]
    for i, ref in enumerate(refs):
        for j in range(2):
            to_ref[2 * i + j] = ref[j * part : (j + 1) * part, :]


def unpack_kernel(idx_ref, a_ref, b_ref, c_ref, d_ref, out_ref, s_ref):
    lay_out((a_ref, b_ref, c_ref, d_ref), s_ref)
    whole = jnp.concatenate([s_ref[idx_ref[p]] for p in range(PIECES)], axis=0)
    out_ref[...] = whole.T


def unpack_rows_kernel(idx_ref, a_ref, b_ref, c_ref, d_ref, out_ref, s_ref):
    part = s_ref.shape[1]
    lay_out((a_ref, b_ref, c_ref, d_ref), s_ref)
    for p in range(PIECES):
        out_ref[p * part : (p + 1) * part, :] = s_ref[idx_ref[p]]


def unpack_att_kernel(
    ia_ref, ib_ref, a0_ref, a1_ref, b0_ref, b1_ref, qkv_ref, out_ref, a_ref, b_ref
):
    part = a_ref.shape[1] // 2
    both((a0_ref, a1_ref), a_ref)
    both((b0_ref, b1_ref), b_ref)

    def whole(ref, i_ref, off):
        return jnp.concatenate(
            [ref[i_ref[p], off : off + part, :] for p in range(PIECES)], axis=0
        )

    qkv_ref[0] = whole(a_ref, ia_ref, 0)
    qkv_ref[1] = whole(a_ref, ia_ref, part)
    qkv_ref[2] = whole(b_ref, ib_ref, 0)
    out_ref[...] = whole(b_ref, ib_ref, part)


def swap_mp(a, k, size):
    return lax.ppermute(a, "mp", [(s, s ^ k) for s in range(size)])


def swap_plane(a, bit, size):
    return lax.ppermute(a, "dp", [(d, d ^ bit) for d in range(size)])


def storage_of(r, bits):
    return sum(jnp.where((r & bit) != 0, 1 << t, 0) for t, bit in enumerate(bits))


class Stages:
    def __init__(self):
        self.live = {}

    def __setitem__(self, name, value):
        self.live[name] = value

    def __getitem__(self, name):
        return self.live[name]

    def pop(self, name):
        return self.live.pop(name)

    def fence(self, *still_flying):
        now = {n: a for n, a in self.live.items() if n not in still_flying}
        leaves, tree = jax.tree.flatten(now)
        self.live.update(jax.tree.unflatten(tree, lax.optimization_barrier(leaves)))


def shards(
    tokens,
    seg_ids,
    qkv_weight,
    qkv_bias,
    out_weight,
    out_bias,
    up_weight,
    up_bias,
    down_weight,
    down_bias,
    norm1_gain,
    norm1_shift,
    query_gain,
    query_shift,
    key_gain,
    norm2_gain,
    norm2_shift,
    cotangent,
):
    ndp = lax.axis_size("dp")
    nmp = lax.axis_size("mp")
    dp_no = lax.axis_index("dp")
    mp_no = lax.axis_index("mp")
    me = dp_no % PIECES
    row_count, width = tokens.shape
    share = row_count // nmp
    full = SEQ_LEN
    assert full == 2 * share and nmp == 4 and ndp % PIECES == 0
    e = qkv_weight.shape[2]
    part = e // PIECES
    units = up_weight.shape[1]
    upart = units // PIECES
    half = PIECES // 2
    mine = half * upart
    core, px, py = 1, 2, 4

    vmem = pl.BlockSpec(memory_space=pltpu.VMEM)
    smem = pl.BlockSpec(memory_space=pltpu.SMEM)
    row1 = lambda v: v.reshape(1, -1)
    col = lambda v: v.reshape(-1, 1)
    swap = lambda a, bit: swap_plane(a, bit, ndp)
    zswap = lambda a, k: swap_mp(a, k, nmp)
    v = Stages()

    me1 = me.astype(jnp.int32).reshape(1)
    qkv_t = jnp.swapaxes(qkv_weight, 1, 2)
    wt0 = qkv_t.reshape(3 * e, width)
    att_piece, ob_piece, bias0, mlp_piece, u0, u1, d0, d1 = call(
        prep_kernel,
        (
            sds((4 * part + 8, width), F32),
            sds((part + 8, width), F32),
            sds((8, width), F32),
            sds((2 * upart, width), F32),
            *[sds((2, upart, width), BF16)] * 4,
        ),
        bytes_accessed=9_000_000,
        in_specs=[smem] + [vmem] * 6,
        out_specs=(vmem,) * 8,
        scratch_shapes=[pltpu.VMEM((units, width), F32), pltpu.VMEM((e, width), F32)],
    )(
        me1, qkv_t, out_weight, qkv_bias, up_bias.reshape(PIECES, upart), up_weight, down_weight
    )

    n_gn = (256, 136, 120)
    n_z2 = 56
    numbers = jnp.arange(PIECES, dtype=jnp.int32)
    idx_a = storage_of(numbers ^ me, BITS_A).astype(jnp.int32)
    idx_b = storage_of(numbers ^ me, BITS_B).astype(jnp.int32)

    block = 256
    per = share // block
    steps = 2 * per
    tile_no = jnp.arange(steps, dtype=jnp.int32)
    blk = jnp.where(tile_no < per, mp_no * per + tile_no, (mp_no ^ 1) * per + tile_no - per).astype(
        jnp.int32
    )
    const2 = lambda t, b: (0, 0)
    tok_spec = pl.BlockSpec((block, width), lambda t, b: (b[t], 0))
    run_spec = pl.BlockSpec((block, width), lambda t, b: (t, 0))
    vec_spec = pl.BlockSpec((1, width), const2)

    def run_norm1():
        return call(
            norm1_kernel,
            sds((full, width), BF16),
            flops=full * width * 10,
            bytes_accessed=full * width * 4,
            grid_spec=pltpu.PrefetchScalarGridSpec(
                num_scalar_prefetch=1,
                grid=(steps,),
                in_specs=[tok_spec, vec_spec, vec_spec],
                out_specs=run_spec,
            ),
        )(blk, tokens, row1(norm1_gain), row1(norm1_shift))

    seg_own = lax.dynamic_slice_in_dim(seg_ids, mp_no * share, share, 0)
    seg_other = lax.dynamic_slice_in_dim(seg_ids, (mp_no ^ 1) * share, share, 0)
    seg_keys = jnp.concatenate([seg_own, seg_other])
    qhot = (
        lax.broadcasted_iota(jnp.int32, (SEG_COLS, full), 0) == seg_keys[None, :]
    ).astype(BF16)
    kmask = jnp.where(
        lax.broadcasted_iota(jnp.int32, (full, SEG_COLS), 1) == seg_keys[:, None], 0.0, -1e30
    ).astype(BF16)
    hv = jnp.stack([query_gain, query_shift, key_gain], axis=1)
    scratch = [
        pltpu.VMEM((2 * DH + SEG_COLS, full), BF16),
        pltpu.VMEM((full, 2 * DH + SEG_COLS), BF16),
    ]

    def whole(a):
        return pl.BlockSpec(a.shape, lambda t: (0,) * len(a.shape))

    def bias_at(block_no):
        return pl.BlockSpec((8, width), lambda t: (block_no, 0))

    att_names = ["qpre", "kpre", "vt", "mixt", "mixf", "mixs", "l"]
    att_shapes = [
        sds((e, full), F32),
        sds((e, full), F32),
        sds((e, full), BF16),
        sds((e, share), BF16),
        sds((e, full), F32),
        sds((e * share // width, width), F32),
        sds((8, full), F32),
    ]
    mix_rows = e * share // width

    def run_attn_own():
        outs = call(
            attn_fwd_own_kernel,
            tuple(att_shapes),
            flops=2 * (full * width * e * 3 + full * full * e * 8),
            bytes_accessed=10_000_000,
            in_specs=[vmem] * 6,
            out_specs=(vmem,) * 7,
            scratch_shapes=scratch,
        )(v["normed"], wt0, bias0, hv, kmask, qhot)
        v["st0"] = dict(zip(att_names, outs))
        v["st0"]["wt"] = wt0
        v["st0"]["ow"] = out_weight

    def run_attn_far():
        shapes = [sds((3 * e, width), BF16)] + [sds((e, width), BF16)] * 3 + att_shapes
        args = [
            *v.pop("ta"), *v.pop("tb"), v["normed"], v["t2"], hv, kmask, qhot,
        ]
        specs = [whole(a) for a in args]
        specs[5] = bias_at(4 * part // 8)
        outs = call(
            attn_fwd_kernel,
            tuple(shapes),
            flops=2 * (full * width * e * 3 + full * full * e * 8),
            bytes_accessed=10_000_000,
            grid=(1,),
            in_specs=[smem, smem] + specs,
            out_specs=tuple(whole(a) for a in shapes),
            scratch_shapes=scratch
            + [pltpu.VMEM((PIECES, 3 * part, width), F32)] * 2,
        )(idx_a, idx_b, *args)
        v["st2"] = dict(zip(["wt", "ow", "ow1", "ow3"] + att_names, outs))

    def by_slot():
        st0, st2 = v["st0"], v["st2"]
        mixes = [st0["mixt"], v["mix0"], st2["mixt"], v["mix2"]]
        ows = [st0["ow"], st2["ow1"], st2["ow"], st2["ow3"]]
        return mixes, ows

    def run_out():
        own_spec = pl.BlockSpec((share, width), lambda t, b: (b[0] // per, 0))
        whole2 = lambda shape: pl.BlockSpec(shape, lambda t, b: (0,) * len(shape))
        mixes, ows = by_slot()
        v["middle"], v["second"], v["sec_f"] = call(
            functools.partial(out_norm2_kernel, nmp),
            (sds((share, width), F32), sds((share, width), BF16), sds((share, width), F32)),
            flops=2 * share * width * e * nmp,
            bytes_accessed=8_000_000,
            grid_spec=pltpu.PrefetchScalarGridSpec(
                num_scalar_prefetch=1,
                grid=(1,),
                in_specs=[own_spec]
                + [whole2((e, share)), whole2((mix_rows, width))] * 2
                + [whole2((e, width))] * nmp
                + [whole2((1, width))] * 3,
                out_specs=(whole2((share, width)),) * 3,
            ),
        )(blk, tokens, *mixes, *ows, row1(out_bias), row1(norm2_gain), row1(norm2_shift))

    def run_mlp(k, up, down, bias, block_no):
        keeps = k % 2 == 0
        args = [
            v["second"], v["sec_p"], v["cot"], v["cot_p"], up[0], up[1], down[0], down[1], bias,
        ]
        if keeps:
            args.append(v.pop(f"p{k + 1}"))
        specs = [whole(a) for a in args]
        specs[8] = bias_at(block_no)
        piece = lambda n: sds((n * upart, width), F32)
        shapes = (
            *[sds((full, mine), BF16)] * 2,
            *[sds((mine, width), BF16)] * 2,
            *([piece(2)] * 4 if keeps else [piece(2), piece(2), piece(1), piece(1), piece(2)]),
            sds((1, mine), F32),
        )
        res = call(
            functools.partial(mlp_kernel, MLP_KIND[k], keeps),
            shapes,
            flops=2 * full * width * mine * 4,
            bytes_accessed=12_000_000,
            grid=(1,),
            in_specs=specs,
            out_specs=tuple(whole(a) for a in shapes),
        )(*args)
        v[f"h{k}"] = res[:4]
        v[f"ubg{k}"] = res[-1]
        if keeps:
            v[f"w{k}"] = res[4:8]
        else:
            v[f"p{k}"], v[f"q{k}u"] = res[4], res[5]
            v[f"w{k}"] = res[6:9]

    def run_down(r):
        row_spec = pl.BlockSpec((share, mine), lambda t: (r, 0))
        w_spec = pl.BlockSpec((mine, width), lambda t: (0, 0))
        return call(
            functools.partial(down_kernel, nmp),
            sds((2, share, width), F32),
            flops=4 * share * width * mine * nmp,
            bytes_accessed=11_000_000,
            grid=(1,),
            in_specs=[row_spec] * (2 * nmp) + [w_spec] * (2 * nmp),
            out_specs=pl.BlockSpec((2, share, width), lambda t: (0, 0, 0)),
        )(*[v[f"h{k}"][i] for i in range(4) for k in range(nmp)])

    def run_mid():
        mixes, ows = by_slot()
        shapes = (
            *[sds((e, share), F32 if k % 2 else BF16) for k in range(nmp)],
            sds((share, width), BF16),
            sds((share, width), F32),
            sds((half, nmp * part, width), F32),
            sds((half, nmp * part, width), F32),
            sds((8, width), F32),
        )
        args = [
            v["middle"], v.pop("acc_own"), v.pop("acc_got"), v["cot"], row1(down_bias),
            row1(norm2_gain), *ows, *mixes,
        ]
        specs = [whole(a) for a in args]
        for k in (1, 3):
            specs[6 + nmp + k] = pl.BlockSpec((mix_rows, width), lambda t: (0, 0))
        *gmts, bo, gm, keep, send, mst = call(
            functools.partial(mid_kernel, nmp),
            shapes,
            flops=2 * share * width * e * nmp * 2,
            bytes_accessed=12_000_000,
            grid=(1,),
            in_specs=[smem] + specs,
            out_specs=tuple(whole(a) for a in shapes),
        )(idx_b, *args)
        v["block_out"], v["gm"], v["mst"] = bo, gm, mst
        for k in range(nmp):
            v[f"gmt{k}"] = gmts[k]
        v["o"] = (keep, send)

    def run_attn_bwd(k, got, idx, first):
        st = v.pop(f"st{k}")
        args = [
            idx, v["normed"], st["qpre"], st["kpre"], st["vt"], st["wt"], v.pop(f"gmt{k}"),
            v.pop(got), st["mixf"], st["l"], hv, kmask, qhot,
        ]
        alias = {}
        if not first:
            args.append(v["gn"])
            alias = {len(args) - 1: 2}
        keep, send, gn, hst, gb = call(
            functools.partial(attn_bwd_kernel, first),
            (
                sds((half, 3 * part, width), F32),
                sds((half, 3 * part, width), F32),
                sds((full, width), F32),
                sds((3, DH, 128), F32),
                sds((3 * e, 128), F32),
            ),
            flops=2 * (full * width * e * 6 + full * full * e * 20),
            bytes_accessed=14_000_000,
            in_specs=[smem] + [vmem] * (len(args) - 1),
            out_specs=(vmem,) * 5,
            scratch_shapes=scratch + [pltpu.VMEM((3 * e, full), BF16)],
            input_output_aliases=alias,
        )(*args)
        v[f"q{k}"] = (keep, send)
        v["gn"] = gn
        v[f"hst{k}"] = hst
        v[f"qbg{k}"] = gb

    def g1(n):
        a, b = v[n + "a"], v[n + "b"]
        v[n + "a"] = (a, swap(a, px))
        v[n + "b"] = (b, swap(b, py))

    def g2(n):
        a, b = (jnp.stack(v[n + t]) for t in "ab")
        v[n + "a"] = (a, swap(a, py))
        v[n + "b"] = (b, swap(b, px))

    def g3(n):
        a, b = (jnp.concatenate(v[n + t], axis=0) for t in "ab")
        v[n + "a"] = (a, swap(a, core))
        v[n + "b"] = (b, swap(b, core))

    def r1(n):
        keep, send = v[n]
        v[n] = (keep, swap(send, core))

    def r2(n, kind):
        keep, got = v[n]
        keep_sum = keep[:2] + got[:2]
        v[n] = (keep_sum, swap(keep[2:] + got[2:], py if kind == "a" else px))

    def r3(n, kind):
        keep, got = v[n]
        v[n] = (keep[0] + got[0], swap(keep[1] + got[1], px if kind == "a" else py))

    def r4(n):
        keep, got = v[n]
        v[n] = keep + got

    def first_link(k):
        return py if MLP_KIND[k] == "a" else px

    def second_link(k):
        return px if MLP_KIND[k] == "a" else py

    def c1(k):
        k0, k1, s0, s1 = v[f"w{k}"]
        v[f"w{k}"] = (k0, k1, s0, swap(s1, first_link(k)))

    def c0(k):
        k0, k1, s0, g1 = v[f"w{k}"]
        v[f"w{k}"] = (k0, k1, g1, swap(s0, first_link(k)))

    def c2(k):
        k0, k1, g1, g0 = v[f"w{k}"]
        q = v.pop(f"q{k + 1}u")
        k1 = jnp.concatenate([k1[:upart] + q[upart:], k1[upart:]], axis=0) + g1
        v[f"w{k}"] = (k0, g0, q[:upart], swap(k1, second_link(k)))

    def c3(k):
        k0, g0, q, g = v[f"w{k}"]
        d = v.pop(f"d{k + 1}")
        total = k0 + g0 + g
        v[f"w{k}"] = jnp.concatenate([total[:upart] + q, total[upart:] + d], axis=0)

    def e1(k):
        k0, k1, s = v[f"w{k}"]
        v[f"w{k}"] = (k0, k1, swap(s, first_link(k)))

    def e2(k):
        k0, k1, g = v[f"w{k}"]
        v[f"w{k}"] = (k0 + g[upart:], swap(k1 + g[:upart], second_link(k)))

    def e3(k):
        k0, g = v[f"w{k}"]
        v[f"w{k}"] = k0 + g

    inner = (mp_no == 1) | (mp_no == 2)

    def middle_swap(a):
        return lax.ppermute(a, "mp", [(1, 2), (2, 1)])

    def pass_out(a):
        return lax.ppermute(a, "mp", [(1, 0), (2, 3)])

    def high_bits(a):
        bit = PIECES
        while bit < ndp:
            a = a + swap(a, bit)
            bit *= 2
        return a

    v["cot"] = lax.dynamic_slice_in_dim(cotangent, mp_no * share, share, 0)
    v["piece"] = mlp_piece
    v["o3"] = zswap(ob_piece, 3)
    v["o1"] = zswap(ob_piece, 1)
    v["t2"] = zswap(att_piece, 2)
    v["cot_p"] = swap(v["cot"].astype(F32), core)
    v["normed"] = run_norm1()
    v.fence()
    hp = 2 * part
    t2, o1, o3 = v["t2"], v["o1"], v["o3"]
    v["ta"] = jnp.concatenate([t2[:hp], o1[:part]], axis=0)
    v["tb"] = jnp.concatenate([t2[hp : 2 * hp], o3[:part]], axis=0)
    g1("t")
    v["m1"] = zswap(v["piece"], 1)
    v["mid_a"] = middle_swap(v.pop("piece"))
    v.fence()
    m1 = v["m1"]
    to_y = jnp.concatenate([*v["ta"], m1[upart:]], axis=0)
    to_x = jnp.concatenate([*v["tb"], m1[:upart]], axis=0)
    v["ta"] = (to_y, swap(to_y, py))
    v["tb"] = (to_x, swap(to_x, px))
    v["mid_b"] = middle_swap(v.pop("m1"))
    v["end_a"] = pass_out(v["mid_a"])
    run_attn_own()
    v.fence()
    nt = 2 * 3 * part
    ya, yb = v.pop("ta")
    xa, xb = v.pop("tb")
    v["m1a"], v["m1b"] = (xa[nt:], xb[nt:]), (ya[nt:], yb[nt:])
    v["ta"], v["tb"] = (
        tuple(
            a.reshape(half, 3 * part, width) for a in (both_, swap(both_, core))
        )
        for both_ in (
            jnp.concatenate([ya[:nt], yb[:nt]], axis=0),
            jnp.concatenate([xa[:nt], xb[:nt]], axis=0),
        )
    )
    run_attn_far()
    g2("m1")
    v["mix0"] = zswap(jnp.concatenate([v["st0"].pop("mixs"), v["mid_b"]], axis=0), 1)
    v.fence()
    v["mix2"] = zswap(v["st2"].pop("mixs"), 1)
    run_out()
    m3 = jnp.where(inner, v.pop("mid_a"), v["mix0"][mix_rows:])
    m2 = jnp.where(inner, v.pop("mid_b"), v.pop("end_a"))
    to_x = jnp.concatenate([m3[:upart], m2[:upart]], axis=0)
    to_y = jnp.concatenate([m3[upart:], m2[upart:]], axis=0)
    v["ma"], v["mb"] = (to_x, swap(to_x, px)), (to_y, swap(to_y, py))
    v.fence()
    for t in "ab":
        own, got = v.pop(f"m{t}")
        v[f"m3{t}"] = (own[:upart], got[:upart])
        v[f"m2{t}"] = (own[upart:], got[upart:])
    v["sec_p"] = swap(v.pop("sec_f"), core)
    run_mlp(1, v.pop("m1a"), v.pop("m1b"), v["o1"], part // 8)
    g2("m3")
    v.fence()
    v["p1"] = zswap(v["p1"], 1)
    run_mlp(3, v.pop("m3a"), v.pop("m3b"), v["o3"], part // 8)
    g2("m2")
    v.fence()
    v["p3"] = zswap(v["p3"], 1)
    run_mlp(0, (u0, u1), (d0, d1), bias0, 0)
    e1(1)
    e1(3)
    v.fence()
    run_mlp(2, v.pop("m2a"), v.pop("m2b"), v["t2"], 4 * part // 8)
    e2(1)
    e2(3)
    v["q1u"] = zswap(v["q1u"], 1)
    v.fence()
    e3(1)
    e3(3)
    v["d13"] = jnp.concatenate([v.pop("w1"), v.pop("w3")], axis=0)
    v["q3u"] = zswap(v["q3u"], 1)
    c1(0)
    c1(2)
    v["send"] = run_down(1)
    v.fence()
    c0(0)
    c0(2)
    v["d13"] = zswap(v["d13"], 1)
    v["acc_got"] = swap(v.pop("send"), core)
    v["acc_own"] = run_down(0)
    v.fence()
    d13 = v.pop("d13")
    v["d1"], v["d3"] = d13[:upart], d13[upart:]
    c2(0)
    c2(2)
    run_mid()
    v.fence()
    c3(0)
    c3(2)
    w2 = v.pop("w2")
    v["z2x"] = zswap(w2[:n_z2], 2)
    v["z2s"] = w2[n_z2:]
    v["gp2"] = zswap(v.pop("gmt3"), 1)
    r1("o")
    v.fence()
    v["gp0"] = zswap(v.pop("gmt1"), 1)
    v["z2y"] = zswap(v.pop("z2s"), 2)
    r2("o", "b")
    run_attn_bwd(2, "gp2", idx_b, True)
    v.fence()
    r1("q2")
    v.fence()
    mlp_sum = high_bits(
        v.pop("w0") + jnp.concatenate([v.pop("z2x"), v.pop("z2y")], axis=0)
    )
    ma, mb = mlp_sum[:upart], mlp_sum[upart:]
    keep, got = v["q2"]
    to_x = jnp.concatenate([(keep[2:] + got[2:]).reshape(-1, width), ma], axis=0)
    v["q2"] = keep[:2] + got[:2]
    keep, got = v["o"]
    to_y = jnp.concatenate([keep[1] + got[1], mb], axis=0)
    v["o"] = keep[0] + got[0]
    v["gx"], v["gy"] = (to_x, swap(to_x, px)), (to_y, swap(to_y, py))
    run_attn_bwd(0, "gp0", idx_b, False)
    v.fence()
    nq = 2 * 3 * part
    (xa, xb), (ya, yb) = v.pop("gx"), v.pop("gy")
    r1("q0")
    q2 = v["q2"] + xb[:nq].reshape(2, 3 * part, width)
    v["q2"] = q2[0]
    to_y = jnp.concatenate([xa[nq:], xb[nq:], q2[1]], axis=0)
    to_x = jnp.concatenate([ya[nmp * part :], yb[nmp * part :]], axis=0)
    v["gx"], v["gy"] = (to_x, swap(to_x, px)), (to_y, swap(to_y, py))
    o = v.pop("o") + yb[: nmp * part]
    v["gn0"] = zswap(
        jnp.concatenate([v["gn"][share : share + n_gn[0]], o[part : 2 * part], o[3 * part :]], axis=0), 1
    )
    v["o0"], v["o2"] = o[:part], o[2 * part : 3 * part]
    n1_stats = call(
        norm1_stats_kernel,
        sds((8, width), F32),
        flops=full * width * 10,
        bytes_accessed=full * width * 6,
        grid_spec=pltpu.PrefetchScalarGridSpec(
            num_scalar_prefetch=1,
            grid=(steps,),
            in_specs=[tok_spec, run_spec],
            out_specs=pl.BlockSpec((8, width), const2),
        ),
    )(blk, tokens, v["gn"])
    head_sum = jnp.sum(v.pop("hst0") + v.pop("hst2"), axis=-1)
    copied = jnp.concatenate(
        [v.pop("mst")[:4].reshape(-1), n1_stats[:2].reshape(-1), head_sum.reshape(-1)]
    )
    own_parts = []
    for k in range(nmp):
        qb = jnp.zeros((3 * e,), F32) if k % 2 else jnp.sum(v.pop(f"qbg{k}"), axis=1)
        ubg = jnp.pad(v.pop(f"ubg{k}").reshape(half, upart), ((0, half), (0, 0)))
        own_parts.append(jnp.concatenate([qb, jnp.take(ubg, idx_a, axis=0).reshape(-1)]))
    nc = copied.shape[0]
    no = own_parts[0].shape[0]
    v["small"] = jnp.concatenate([copied] + own_parts)
    v.fence()
    r2("q0", "b")
    (xa, xb), (ya, yb) = v["gx"], v["gy"]
    gn0 = v.pop("gn0")
    v["gn0"] = gn0[: n_gn[0]]
    v["o0"] = v["o0"] + gn0[n_gn[0] : n_gn[0] + part]
    o2 = v.pop("o2") + gn0[n_gn[0] + part :]
    q2 = v.pop("q2") + yb[2 * upart :]
    v["y2"] = zswap(jnp.concatenate([q2, o2], axis=0), 2)
    at = share + n_gn[0]
    v["gn1"] = zswap(v["gn"][at : at + n_gn[1]], 1)
    v["small"] = v["small"] + swap(v["small"], core)
    v.fence()
    r3("q0", "b")
    v["gn2"] = zswap(v["gn"][share + n_gn[0] + n_gn[1] :], 1)
    v["small"] = v["small"] + swap(v["small"], px)
    ya, yb = v.pop("gy")
    v["gu"] = (ya, yb, swap(ya, core), swap(yb, core))
    v.fence()
    r4("q0")
    att_sum = high_bits(
        jnp.concatenate([v.pop("q0"), v.pop("o0")], axis=0) + v.pop("y2")
    )
    v["wa"], v["wb"] = att_sum[:hp], att_sum[hp:]
    g1("w")
    xa, xb = v.pop("gx")
    v["gd"] = (xa, xb, swap(xa, core), swap(xb, core))
    v["small"] = v["small"] + swap(v["small"], py)
    v["input_grad"] = call(
        final_kernel,
        sds((share, width), BF16),
        flops=share * width * 20,
        bytes_accessed=share * width * 16,
        grid_spec=pltpu.PrefetchScalarGridSpec(
            num_scalar_prefetch=1,
            grid=(per,),
            in_specs=[tok_spec, run_spec, run_spec, run_spec, vec_spec],
            out_specs=run_spec,
        ),
    )(
        blk,
        tokens,
        v["gn"],
        jnp.concatenate([v.pop("gn0"), v.pop("gn1"), v.pop("gn2")], axis=0),
        v["gm"],
        row1(norm1_gain),
    )
    v.fence()

    def unpack(kernel, arrays, idx, shape):
        pieces_spec = pl.BlockSpec((2 * upart, width), lambda t: (0, 0))
        return call(
            kernel,
            sds(shape, F32),
            bytes_accessed=2 * 4 * math.prod(shape),
            grid=(1,),
            in_specs=[smem] + [pieces_spec] * 4,
            out_specs=pl.BlockSpec(shape, lambda t: (0, 0)),
            scratch_shapes=[pltpu.VMEM((PIECES, upart, width), F32)],
        )(idx, *arrays)

    g2("w")
    small = high_bits(v.pop("small"))
    parts = [small[nc + k * no : nc + (k + 1) * no] for k in range(nmp)]
    sent = jnp.concatenate([small[:nc], parts[1], parts[3]])
    got = zswap(sent, 1)
    v["small"] = jnp.concatenate([small[:nc], parts[0], parts[2]]) + got
    v["up_g"] = unpack(unpack_kernel, v.pop("gu"), idx_a, (width, units))
    v["down_g"] = unpack(unpack_rows_kernel, v.pop("gd"), idx_b, (units, width))
    v.fence()
    wa, wb = (jnp.concatenate(v.pop("w" + t), axis=0) for t in "ab")
    small = v.pop("small")
    got = zswap(jnp.concatenate([small[:nc], small[nc + no :]]), 2)
    v["small_sum"] = small[: nc + no] + got
    qkv_weight_grad, out_weight_grad = call(
        unpack_att_kernel,
        (sds((3, e, width), F32), sds((e, width), F32)),
        bytes_accessed=2 * 4 * 4 * width * e,
        in_specs=[smem, smem] + [vmem] * 4,
        out_specs=(vmem, vmem),
        scratch_shapes=[pltpu.VMEM((PIECES, hp, width), F32)] * 2,
    )(idx_a, idx_b, wa, swap(wa, core), wb, swap(wb, core))
    qkv_weight_grad = jnp.swapaxes(qkv_weight_grad, 1, 2)

    small_sum = v["small_sum"]
    rows_of = small_sum[: 6 * width].reshape(6, width)
    heads_of = small_sum[6 * width : nc].reshape(3, DH)
    qkv_bias_grad = small_sum[nc : nc + 3 * e].reshape(3, e)
    up_bias_grad = small_sum[nc + 3 * e :]
    return (
        v["block_out"],
        v["input_grad"],
        qkv_weight_grad,
        qkv_bias_grad,
        out_weight_grad,
        rows_of[2],
        v["up_g"],
        up_bias_grad,
        v["down_g"],
        rows_of[3],
        rows_of[4],
        rows_of[5],
        heads_of[0],
        heads_of[1],
        heads_of[2],
        rows_of[0],
        rows_of[1],
    )


def solution(mesh):
    in_specs = (
        P("dp", None),
        P("dp"),
        P(None, None, "mp"),
        P(None, "mp"),
        P("mp", None),
        P(),
        P(None, "mp"),
        P("mp"),
        P("mp", None),
        P(),
        P(),
        P(),
        P(),
        P(),
        P(),
        P(),
        P(),
        P("dp", None),
    )
    out_specs = (
        P(("dp", "mp"), None),
        P(("dp", "mp"), None),
        P(None, None, "mp"),
        P(None, "mp"),
        P("mp", None),
        P(),
        P(None, "mp"),
        P("mp"),
        P("mp", None),
        P(),
        P(),
        P(),
        P(),
        P(),
        P(),
        P(),
        P(),
    )
    return jax.shard_map(shards, mesh=mesh, in_specs=in_specs, out_specs=out_specs, check_vma=False)
```

profile of v0, /device:TPU:0, one launch (start us, length us, event | category | flops | bytes accessed | tf_op | source)
XLA Modules:
  0.0 372.8 jit_solution(12258431356378569587)
XLA Ops:
  4.0 4.0 %shard_map.306 = (f32[104,768]{1,0:T(8,128)}, f32[32,768]{1,0:T(8,128)}, f32[8,768]{1,0:T(8,128)}, f32[192,768]{1,0:T(8,128)}, bf16[2,96,768]{2,1,0:T(8,128)(2,1...) custom-call(s32[1]{0:T(128)} %bitcast.me_ref, ...), custom_call_target="tpu_custom_call" | custom-call | bytes 9000000 | tf_op jit(solution)/shard_map/pallas_call | solution.py:567
  8.0 3.6 collective-permute-start.3
  15.6 5.0 %shard_map.305.x_ref = bf16[1024,768]{1,0:T(8,128)(2,1)} custom-call(s32[4]{0:T(128)} %compare_select_fusion.1.blk_ref, bf16[2048,768]{1,0:T(8,128)(2,1)} %x_ref.7, f32[1,768]{1,0:T(1,128)} %reshape.154.g_ref, f32[1,768]{1,0:T(1,128)} %reshape.155.s_ref), custom_call_target="tpu_custom_call" | custom-call | flops 7864320 | bytes 3145728 | tf_op jit(solution)/shard_map/pallas_call | solution.py:603
  21.9 3.5 collective-permute-done.2.b_ref
  25.4 3.7 collective-permute-done.3.b_ref
  36.0 3.9 %collective-permute-done.6 = f32[72,768]{1,0:T(8,128)S(1)} collective-permute-done((f32[72,768]{1,0:T(8,128)S(1)}, f32[72,768]{1,0:T(8,128)S(1)}, u32[]{:S(2)}, u32[]{:S(2)}) %collective-permute-start.6) | collective-permute-done | bytes 221216 | tf_op jit(solution)/shard_map/ppermute | solution.py:493
  41.2 4.3 %collective-permute-done.4 = f32[192,768]{1,0:T(8,128)S(1)} collective-permute-done((f32[192,768]{1,0:T(8,128)S(1)}, f32[192,768]{1,0:T(8,128)S(1)}, u32[]{:S(2)}, u32[]{:S(2)}) %collective-permute-start.4) | collective-permute-done | bytes 589856 | tf_op jit(solution)/shard_map/ppermute | solution.py:489
  52.7 7.7 %shard_map.307 = (f32[192,1024]{1,0:T(8,128)}, f32[192,1024]{1,0:T(8,128)}, bf16[192,1024]{1,0:T(8,128)(2,1)}, bf16[192,512]{1,0:T(8,128)(2,1)}, f32[192,1024]{1...) custom-call(bf16[1024,768]{1,0:T(8,128)(2,1)} %shard_map.305.x_ref, bf16[576,768]{1,0:T(8,128)(2,1)} %bitcast.58, ...), custom_call_target="tpu_custom_call" | custom-call | flops 4127195136 | bytes 10000000 | tf_op jit(solution)/shard_map/pallas_call | solution.py:650
  60.4 10.5 %collective-permute-done.8 = f32[192,768]{1,0:T(8,128)S(1)} collective-permute-done((f32[192,768]{1,0:T(8,128)S(1)}, f32[192,768]{1,0:T(8,128)S(1)}, u32[]{:S(2)}, u32[]{:S(2)}) %collective-permute-start.8) | collective-permute-done | bytes 589856 | tf_op jit(solution)/shard_map/ppermute | solution.py:893
  78.1 9.9 %shard_map.308 = (bf16[576,768]{1,0:T(8,128)(2,1)}, bf16[192,768]{1,0:T(8,128)(2,1)}, bf16[192,768]{1,0:T(8,128)(2,1)}, bf16[192,768]{1,0:T(8,128)(2,1)}, f32[19...) custom-call(s32[8]{0:T(128)} %get-tuple-element.1524.ia_ref.idx_ref,, ...), custom_call_target="tpu_custom_call" | custom-call | flops 4127195136 | bytes 10000000 | tf_op jit(solution)/shard_map/pallas_call | solution.py:670
  88.0 3.2 collective-permute-done.12.u1_ref
  99.3 5.9 %collective-permute-done.19.refs_3_.refs_7_ = f32[128,768]{1,0:T(8,128)S(1)} collective-permute-done((f32[128,768]{1,0:T(8,128)S(1)}, f32[128,768]{1,0:T(8,128)S(1)}, u32[]{:S(2)}, u32[]{:S(2)}) %collective-permute-start.19) | collective-permute-done | bytes 393248 | tf_op jit(solution)/shard_map/ppermute | solution.py:489
  106.0 5.6 %shard_map.309 = (f32[512,768]{1,0:T(8,128)}, bf16[512,768]{1,0:T(8,128)(2,1)}, f32[512,768]{1,0:T(8,128)}) custom-call(s32[4]{0:T(128)} %compare_select_fusion.1.blk_ref, bf16[2048,768]{1,0:T(8,128)(2,1)} %x_ref.7, bf16[192,512]{1,0:T(8,128)(2,1)} %get-tuple-element.1187.refs_0_.refs_4_, f32[320,768]{1,0:T(8,128)} %copy-done, ...), custom_call_target="tpu_custom_call" | custom-call | flops 603979776 | bytes 8000000 | tf_op jit(solution)/shard_map/pallas_call | solution.py:693
  116.4 7.5 %shard_map.310 = (bf16[1024,384]{1,0:T(8,128)(2,1)}, bf16[1024,384]{1,0:T(8,128)(2,1)}, bf16[384,768]{1,0:T(8,128)(2,1)}, bf16[384,768]{1,0:T(8,128)(2,1)}, f32[...) custom-call(bf16[512,768]{1,0:T(8,128)(2,1)} %get-tuple-element.1009, ...), custom_call_target="tpu_custom_call" | custom-call | flops 2415919104 | bytes 12000000 | tf_op jit(solution)/shard_map/pallas_call | solution.py:725
  124.0 3.7 collective-permute-done.21.u1_ref
  133.1 7.3 %shard_map.311 = (bf16[1024,384]{1,0:T(8,128)(2,1)}, bf16[1024,384]{1,0:T(8,128)(2,1)}, bf16[384,768]{1,0:T(8,128)(2,1)}, bf16[384,768]{1,0:T(8,128)(2,1)}, f32[...) custom-call(bf16[512,768]{1,0:T(8,128)(2,1)} %get-tuple-element.1009, ...), custom_call_target="tpu_custom_call" | custom-call | flops 2415919104 | bytes 12000000 | tf_op jit(solution)/shard_map/pallas_call | solution.py:725
  148.7 7.4 %shard_map.312 = (bf16[1024,384]{1,0:T(8,128)(2,1)}, bf16[1024,384]{1,0:T(8,128)(2,1)}, bf16[384,768]{1,0:T(8,128)(2,1)}, bf16[384,768]{1,0:T(8,128)(2,1)}, f32[...) custom-call(bf16[512,768]{1,0:T(8,128)(2,1)} %get-tuple-element.1009.sec, ...), custom_call_target="tpu_custom_call" | custom-call | flops 2415919104 | bytes 12000000 | tf_op jit(solution)/shard_map/pallas_call | solution.py:725
  163.3 8.0 %shard_map.313 = (bf16[1024,384]{1,0:T(8,128)(2,1)}, bf16[1024,384]{1,0:T(8,128)(2,1)}, bf16[384,768]{1,0:T(8,128)(2,1)}, bf16[384,768]{1,0:T(8,128)(2,1)}, f32[...) custom-call(bf16[512,768]{1,0:T(8,128)(2,1)} %get-tuple-element.1009.sec, ...), custom_call_target="tpu_custom_call" | custom-call | flops 2415919104 | bytes 12000000 | tf_op jit(solution)/shard_map/pallas_call | solution.py:725
  171.3 3.9 %collective-permute-done.29 = f32[192,768]{1,0:T(8,128)S(1)} collective-permute-done((f32[192,768]{1,0:T(8,128)S(1)}, f32[192,768]{1,0:T(8,128)S(1)}, u32[]{:S(2)}, u32[]{:S(2)}) %collective-permute-start.29) | collective-permute-done | bytes 589856 | tf_op jit(solution)/shard_map/ppermute | solution.py:489
  176.6 7.6 %shard_map.314 = f32[2,512,768]{2,1,0:T(8,128)} custom-call(bf16[1024,384]{1,0:T(8,128)(2,1)} %get-tuple-element.1125.refs_0_, bf16[1024,384]{1,0:T(8,128)(2,1)} %get-tuple-element.1126.refs_1_, bf16[1024,384]{1,0:T(8,128)(2,1)} %get-tuple-element.1127.refs_2_, bf16[1024,384]{1,0:T(8,128)(2,1)} %get-tuple-element.1128.refs_3_, ...), custom_call_target="tpu_custom_call" | custom-call | flops 2415919104 | bytes 11000000 | tf_op jit(solution)/shard_map/pallas_call | solution.py:745
  189.8 7.5 %shard_map.315.own_ref = f32[2,512,768]{2,1,0:T(8,128)} custom-call(bf16[1024,384]{1,0:T(8,128)(2,1)} %get-tuple-element.1125.refs_0_, bf16[1024,384]{1,0:T(8,128)(2,1)} %get-tuple-element.1126.refs_1_, bf16[1024,384]{1,0:T(8,128)(2,1)} %get-tuple-element.1127.refs_2_, bf16[1024,384]{1,0:T(8,128)(2,1)} %get-tuple-element.1128.refs_3_, ...), custom_call_target="tpu_custom_call" | custom-call | flops 2415919104 | bytes 11000000 | tf_op jit(solution)/shard_map/pallas_call | solution.py:745
  197.3 5.2 %collective-permute-done.36 = f32[192,768]{1,0:T(8,128)S(1)} collective-permute-done((f32[192,768]{1,0:T(8,128)S(1)}, f32[192,768]{1,0:T(8,128)S(1)}, u32[]{:S(2)}, u32[]{:S(2)}) %collective-permute-start.36) | collective-permute-done | bytes 589856 | tf_op jit(solution)/shard_map/ppermute | solution.py:489
  208.2 11.0 %shard_map.316 = (bf16[192,512]{1,0:T(8,128)(2,1)}, f32[192,512]{1,0:T(8,128)}, bf16[192,512]{1,0:T(8,128)(2,1)}, f32[192,512]{1,0:T(8,128)}, bf16[512,768]{1,0:...) custom-call(s32[8]{0:T(128)} %get-tuple-element.1523.ib_ref.idx_ref, ...), custom_call_target="tpu_custom_call" | custom-call | flops 1207959552 | bytes 12000000 | tf_op jit(solution)/shard_map/pallas_call | solution.py:772
  223.8 8.8 %collective-permute-done.43 = f32[56,768]{1,0:T(8,128)S(1)} collective-permute-done((f32[56,768]{1,0:T(8,128)S(1)}, f32[56,768]{1,0:T(8,128)S(1)}, u32[]{:S(2)}, u32[]{:S(2)}) %collective-permute-start.43) | collective-permute-done | bytes 172064 | tf_op jit(solution)/shard_map/ppermute | solution.py:489
  238.4 16.0 %shard_map.317 = (f32[4,72,768]{2,1,0:T(8,128)}, f32[4,72,768]{2,1,0:T(8,128)}, f32[1024,768]{1,0:T(8,128)}, f32[3,64,128]{2,1,0:T(8,128)}, f32[576,128]{1,0:T(8,128)}) custom-call(s32[8]{0:T(128)} %get-tuple-element.1523.ib_ref.idx_ref, bf16[1024,768]{1,0:T(8,128)(2,1)} %shard_map.305.x_ref, f32[192,1024]{1,0:T(8,128)} %get-tuple-element.1268.qpre_ref, ...), custom_call_target="tpu_custom_call" | custom-call | flops 9865003008 | bytes 14000000 | tf_op jit(solution)/shard_map/pallas_call | solution.py:796
  259.9 17.1 %shard_map.318 = (f32[4,72,768]{2,1,0:T(8,128)}, f32[4,72,768]{2,1,0:T(8,128)}, f32[1024,768]{1,0:T(8,128)}, f32[3,64,128]{2,1,0:T(8,128)}, f32[576,128]{1,0:T(8,128)}) custom-call(s32[8]{0:T(128)} %get-tuple-element.1523.ib_ref.idx_ref, bf16[1024,768]{1,0:T(8,128)(2,1)} %shard_map.305.x_ref, ...), custom_call_target="tpu_custom_call", output_to_operand_aliasing={{2}: (13, {})} | custom-call | flops 9865003008 | bytes 14000000 | tf_op jit(solution)/shard_map/pallas_call | solution.py:796
  284.6 5.5 %shard_map.319 = f32[8,768]{1,0:T(8,128)} custom-call(s32[4]{0:T(128)} %compare_select_fusion.1.blk_ref, bf16[2048,768]{1,0:T(8,128)(2,1)} %x_ref.7, f32[1024,768]{1,0:T(8,128)} %get-tuple-element.1407.gn_ref), custom_call_target="tpu_custom_call" | custom-call | flops 7864320 | bytes 4718592 | tf_op jit(solution)/shard_map/pallas_call | solution.py:1035
  314.5 10.5 %collective-permute-done.57 = f32[96,768]{1,0:T(8,128)S(1)} collective-permute-done((f32[96,768]{1,0:T(8,128)S(1)}, f32[96,768]{1,0:T(8,128)S(1)}, u32[]{:S(2)}, u32[]{:S(2)}) %collective-permute-start.57) | collective-permute-done | bytes 294944 | tf_op jit(solution)/shard_map/ppermute | solution.py:489
  345.5 4.5 %shard_map.320 = bf16[512,768]{1,0:T(8,128)(2,1)} custom-call(s32[4]{0:T(128)} %compare_select_fusion.1.blk_ref, bf16[2048,768]{1,0:T(8,128)(2,1)} %x_ref.7, f32[1024,768]{1,0:T(8,128)} %get-tuple-element.1407.gn_ref, f32[512,768]{1,0:T(8,128)} %pad_maximum_fusion.got_ref, f32[512,768]{1,0:T(8,128)} %get-tuple-element.1406.gm_ref, f32[1,768]{1,0:T(1,128)} %reshape.154.g_ref), custom_call_target="tpu_custom_call" | custom-call | flops 7864320 | bytes 6291456 | tf_op jit(solution)/shard_map/pallas_call | solution.py:1087
  352.8 3.3 shard_map.321
  356.1 3.8 %shard_map.322 = f32[768,768]{1,0:T(8,128)} custom-call(s32[8]{0:T(128)} %get-tuple-element.1524.ia_ref.idx_ref, f32[264,768]{1,0:T(8,128)} %copy-done.1, f32[264,768]{1,0:T(8,128)} %copy-done.9, f32[264,768]{1,0:T(8,128)} %copy-done.13, f32[264,768]{1,0:T(8,128)} %copy-done.14), custom_call_target="tpu_custom_call" | custom-call | bytes 4718592 | tf_op jit(solution)/shard_map/pallas_call | solution.py:1110
  369.2 3.3 shard_map.323
  (439 shorter events, 157.8 us)
Async XLA Ops:
  2.9 26.3 %collective-permute-start = (f32[512,768]{1,0:T(8,128)S(1)}, f32[512,768]{1,0:T(8,128)}, u32[]{:S(2)}, u32[]{:S(2)}) collective-permute-start(f32[512,768]{1,0:T(8,128)S(1)} %get-tuple-element.1446), channel_id=1, source_target_pairs={{0,4},{4,0},{8,12},{12,8},{16,20},{20,16},{24,28},{28,24},{1,5},{5... | collective-permute-start | bytes 4718600 | tf_op jit(solution)/shard_map/ppermute | solution.py:493
  8.0 21.1 %collective-permute-start.3 = (f32[104,768]{1,0:T(8,128)}, f32[104,768]{1,0:T(8,128)S(1)}, u32[]{:S(2)}, u32[]{:S(2)}) collective-permute-start(f32[104,768]{1,0:T(8,128)} %get-tuple-element.734), channel_id=1, source_target_pairs={{0,2},{1,3},{2,0},{3,1},{4,6},{5,7},{6,4},{7,5},{8,10},{9,11},{10,... | collective-permute-start | bytes 958472 | tf_op jit(solution)/shard_map/ppermute | solution.py:489
  29.1 16.4 %collective-permute-start.4 = (f32[192,768]{1,0:T(8,128)S(1)}, f32[192,768]{1,0:T(8,128)S(1)}, u32[]{:S(2)}, u32[]{:S(2)}) collective-permute-start(f32[192,768]{1,0:T(8,128)S(1)} %copy-done.63), channel_id=1, source_target_pairs={{0,1},{1,0},{2,3},{3,2},{4,5},{5,4},{6,7},{7,6},{8,9},{9,8},{10,11... | collective-permute-start | bytes 1769480 | tf_op jit(solution)/shard_map/ppermute | solution.py:489
  45.7 25.2 %collective-permute-start.10 = (f32[240,768]{1,0:T(8,128)S(1)}, f32[240,768]{1,0:T(8,128)S(1)}, u32[]{:S(2)}, u32[]{:S(2)}) collective-permute-start(f32[240,768]{1,0:T(8,128)S(1)} %pad_maximum_fusion.6), channel_id=1, source_target_pairs={{0,16},{4,20},{8,24},{12,28},{16,0},{20,4},{24,8},{28,12},{1,17},{... | collective-permute-start | bytes 2211848 | tf_op jit(solution)/shard_map/ppermute | solution.py:493
  47.3 23.6 %collective-permute-start.11 = (f32[240,768]{1,0:T(8,128)S(1)}, f32[240,768]{1,0:T(8,128)S(1)}, u32[]{:S(2)}, u32[]{:S(2)}) collective-permute-start(f32[240,768]{1,0:T(8,128)S(1)} %pad_maximum_fusion.7), channel_id=1, source_target_pairs={{0,8},{4,12},{8,0},{12,4},{16,24},{20,28},{24,16},{28,20},{1,9},{5... | collective-permute-start | bytes 2211848 | tf_op jit(solution)/shard_map/ppermute | solution.py:493
  49.8 21.1 %collective-permute-start.9 = (f32[192,768]{1,0:T(8,128)S(1)}, f32[192,768]{1,0:T(8,128)S(1)}, u32[]{:S(2)}, u32[]{:S(2)}) collective-permute-start(f32[192,768]{1,0:T(8,128)S(1)} %collective-permute-done.4), channel_id=1, source_target_pairs={{1,2},{2,1},{5,6},{6,5},{9,10},{10,9},{13,14},{14,13},{17,18},{18,... | collective-permute-start | bytes 1769480 | tf_op jit(solution)/shard_map/ppermute | solution.py:890
  50.5 20.4 %collective-permute-start.8 = (f32[192,768]{1,0:T(8,128)S(1)}, f32[192,768]{1,0:T(8,128)S(1)}, u32[]{:S(2)}, u32[]{:S(2)}) collective-permute-start(f32[192,768]{1,0:T(8,128)S(1)} %collective-permute-done.5), channel_id=1, source_target_pairs={{1,0},{2,3},{5,4},{6,7},{9,8},{10,11},{13,12},{14,15},{17,16},{18,... | collective-permute-start | bytes 1769480 | tf_op jit(solution)/shard_map/ppermute | solution.py:893
  72.7 21.5 %collective-permute-start.14 = (f32[320,768]{1,0:T(8,128)S(1)}, f32[320,768]{1,0:T(8,128)S(1)}, u32[]{:S(2)}, u32[]{:S(2)}) collective-permute-start(f32[320,768]{1,0:T(8,128)S(1)} %pad_maximum_fusion.1), channel_id=1, source_target_pairs={{0,1},{1,0},{2,3},{3,2},{4,5},{5,4},{6,7},{7,6},{8,9},{9,8},{10,11... | collective-permute-start | bytes 2949128 | tf_op jit(solution)/shard_map/ppermute | solution.py:489
  75.5 15.6 %collective-permute-start.12 = (f32[2,96,768]{2,1,0:T(8,128)}, f32[2,96,768]{2,1,0:T(8,128)}, u32[]{:S(2)}, u32[]{:S(2)}) collective-permute-start(f32[2,96,768]{2,1,0:T(8,128)} %pad_maximum_fusion.9.u0_ref), channel_id=1, source_target_pairs={{0,16},{4,20},{8,24},{12,28},{16,0},{20,4},{24,8},{28,12},{1,17},{... | collective-permute-start | bytes 1769480 | tf_op jit(solution)/shard_map/ppermute | solution.py:493
  76.9 15.4 %collective-permute-start.13 = (f32[2,96,768]{2,1,0:T(8,128)}, f32[2,96,768]{2,1,0:T(8,128)}, u32[]{:S(2)}, u32[]{:S(2)}) collective-permute-start(f32[2,96,768]{2,1,0:T(8,128)} %pad_maximum_fusion.10.d0_ref), channel_id=1, source_target_pairs={{0,8},{4,12},{8,0},{12,4},{16,24},{20,28},{24,16},{28,20},{1,9},{5... | collective-permute-start | bytes 1769480 | tf_op jit(solution)/shard_map/ppermute | solution.py:493
  95.3 16.3 %collective-permute-start.17 = (f32[192,768]{1,0:T(8,128)S(1)}, f32[192,768]{1,0:T(8,128)S(1)}, u32[]{:S(2)}, u32[]{:S(2)}) collective-permute-start(f32[192,768]{1,0:T(8,128)S(1)} %pad_maximum_fusion.11), channel_id=1, source_target_pairs={{0,8},{4,12},{8,0},{12,4},{16,24},{20,28},{24,16},{28,20},{1,9},{5... | collective-permute-start | bytes 1769480 | tf_op jit(solution)/shard_map/ppermute | solution.py:493
  95.9 15.7 %collective-permute-start.18 = (f32[192,768]{1,0:T(8,128)S(1)}, f32[192,768]{1,0:T(8,128)S(1)}, u32[]{:S(2)}, u32[]{:S(2)}) collective-permute-start(f32[192,768]{1,0:T(8,128)S(1)} %pad_maximum_fusion.12), channel_id=1, source_target_pairs={{0,16},{4,20},{8,24},{12,28},{16,0},{20,4},{24,8},{28,12},{1,17},{... | collective-permute-start | bytes 1769480 | tf_op jit(solution)/shard_map/ppermute | solution.py:493
  111.8 15.8 %collective-permute-start.21 = (f32[2,96,768]{2,1,0:T(8,128)S(1)}, f32[2,96,768]{2,1,0:T(8,128)S(1)}, u32[]{:S(2)}, u32[]{:S(2)}) collective-permute-start(f32[2,96,768]{2,1,0:T(8,128)S(1)} %pad_maximum_fusion.13.u0_ref), channel_id=1, source_target_pairs={{0,16},{4,20},{8,24},{12,28},{16,0},{20,4},{24,8},{28,12},{1,17},{... | collective-permute-start | bytes 1769480 | tf_op jit(solution)/shard_map/ppermute | solution.py:493
  112.8 15.6 %collective-permute-start.22 = (f32[2,96,768]{2,1,0:T(8,128)S(1)}, f32[2,96,768]{2,1,0:T(8,128)S(1)}, u32[]{:S(2)}, u32[]{:S(2)}) collective-permute-start(f32[2,96,768]{2,1,0:T(8,128)S(1)} %pad_maximum_fusion.14.d0_ref), channel_id=1, source_target_pairs={{0,8},{4,12},{8,0},{12,4},{16,24},{20,28},{24,16},{28,20},{1,9},{5... | collective-permute-start | bytes 1769480 | tf_op jit(solution)/shard_map/ppermute | solution.py:493
  128.4 14.8 %collective-permute-start.23 = (f32[2,96,768]{2,1,0:T(8,128)S(1)}, f32[2,96,768]{2,1,0:T(8,128)S(1)}, u32[]{:S(2)}, u32[]{:S(2)}) collective-permute-start(f32[2,96,768]{2,1,0:T(8,128)S(1)} %pad_maximum_fusion.15.u0_ref), channel_id=1, source_target_pairs={{0,16},{4,20},{8,24},{12,28},{16,0},{20,4},{24,8},{28,12},{1,17},{... | collective-permute-start | bytes 1769480 | tf_op jit(solution)/shard_map/ppermute | solution.py:493
  129.8 14.4 %collective-permute-start.24 = (f32[2,96,768]{2,1,0:T(8,128)S(1)}, f32[2,96,768]{2,1,0:T(8,128)S(1)}, u32[]{:S(2)}, u32[]{:S(2)}) collective-permute-start(f32[2,96,768]{2,1,0:T(8,128)S(1)} %pad_maximum_fusion.16.d0_ref), channel_id=1, source_target_pairs={{0,8},{4,12},{8,0},{12,4},{16,24},{20,28},{24,16},{28,20},{1,9},{5... | collective-permute-start | bytes 1769480 | tf_op jit(solution)/shard_map/ppermute | solution.py:493
  186.8 17.9 %collective-permute-start.35 = (f32[2,512,768]{2,1,0:T(8,128)}, f32[2,512,768]{2,1,0:T(8,128)S(1)}, u32[]{:S(2)}, u32[]{:S(2)}) collective-permute-start(f32[2,512,768]{2,1,0:T(8,128)} %shard_map.314), channel_id=1, source_target_pairs={{0,4},{4,0},{8,12},{12,8},{16,20},{20,16},{24,28},{28,24},{1,5},{5... | collective-permute-start | bytes 9437192 | tf_op jit(solution)/shard_map/ppermute | solution.py:493
  186.8 15.7 %collective-permute-start.36 = (f32[192,768]{1,0:T(8,128)S(1)}, f32[192,768]{1,0:T(8,128)S(1)}, u32[]{:S(2)}, u32[]{:S(2)}) collective-permute-start(f32[192,768]{1,0:T(8,128)S(1)} %pad_maximum_fusion.17), channel_id=1, source_target_pairs={{0,1},{1,0},{2,3},{3,2},{4,5},{5,4},{6,7},{7,6},{8,9},{9,8},{10,11... | collective-permute-start | bytes 1769480 | tf_op jit(solution)/shard_map/ppermute | solution.py:489
  187.7 15.7 %collective-permute-start.37 = (f32[192,768]{1,0:T(8,128)}, f32[192,768]{1,0:T(8,128)S(1)}, u32[]{:S(2)}, u32[]{:S(2)}) collective-permute-start(f32[192,768]{1,0:T(8,128)} %get-tuple-element.1174), channel_id=1, source_target_pairs={{0,16},{4,20},{8,24},{12,28},{16,0},{20,4},{24,8},{28,12},{1,17},{... | collective-permute-start | bytes 1769480 | tf_op jit(solution)/shard_map/ppermute | solution.py:493
  189.4 15.4 %collective-permute-start.38 = (f32[192,768]{1,0:T(8,128)}, f32[192,768]{1,0:T(8,128)S(1)}, u32[]{:S(2)}, u32[]{:S(2)}) collective-permute-start(f32[192,768]{1,0:T(8,128)} %get-tuple-element.1178), channel_id=1, source_target_pairs={{0,8},{4,12},{8,0},{12,4},{16,24},{20,28},{24,16},{28,20},{1,9},{5... | collective-permute-start | bytes 1769480 | tf_op jit(solution)/shard_map/ppermute | solution.py:493
  206.5 14.3 %collective-permute-start.39 = (f32[192,768]{1,0:T(8,128)S(1)}, f32[192,768]{1,0:T(8,128)S(1)}, u32[]{:S(2)}, u32[]{:S(2)}) collective-permute-start(f32[192,768]{1,0:T(8,128)S(1)} %maximum_add_fusion), channel_id=1, source_target_pairs={{0,8},{4,12},{8,0},{12,4},{16,24},{20,28},{24,16},{28,20},{1,9},{5... | collective-permute-start | bytes 1769480 | tf_op jit(solution)/shard_map/ppermute | solution.py:493
  234.1 20.4 %collective-permute-start.44 = (f32[192,512]{1,0:T(8,128)S(1)}, f32[192,512]{1,0:T(8,128)S(1)}, u32[]{:S(2)}, u32[]{:S(2)}) collective-permute-start(f32[192,512]{1,0:T(8,128)S(1)} %copy-done.70), channel_id=1, source_target_pairs={{0,1},{1,0},{2,3},{3,2},{4,5},{5,4},{6,7},{7,6},{8,9},{9,8},{10,11... | collective-permute-start | bytes 1179656 | tf_op jit(solution)/shard_map/ppermute | solution.py:489
  235.1 19.6 %collective-permute-start.45 = (f32[2,96,768]{2,1,0:T(8,128)S(1)}, f32[2,96,768]{2,1,0:T(8,128)S(1)}, u32[]{:S(2)}, u32[]{:S(2)}) collective-permute-start(f32[2,96,768]{2,1,0:T(8,128)S(1)} %get-tuple-element.1448), channel_id=1, source_target_pairs={{0,8},{4,12},{8,0},{12,4},{16,24},{20,28},{24,16},{28,20},{1,9},{5... | collective-permute-start | bytes 1769480 | tf_op jit(solution)/shard_map/ppermute | solution.py:493
  236.7 18.0 %collective-permute-start.46 = (f32[136,768]{1,0:T(8,128)S(1)}, f32[136,768]{1,0:T(8,128)S(1)}, u32[]{:S(2)}, u32[]{:S(2)}) collective-permute-start(f32[136,768]{1,0:T(8,128)S(1)} %pad_maximum_fusion.21), channel_id=1, source_target_pairs={{0,2},{1,3},{2,0},{3,1},{4,6},{5,7},{6,4},{7,5},{8,10},{9,11},{10,... | collective-permute-start | bytes 1253384 | tf_op jit(solution)/shard_map/ppermute | solution.py:489
  257.6 19.4 %collective-permute-start.48 = (f32[240,768]{1,0:T(8,128)S(1)}, f32[240,768]{1,0:T(8,128)S(1)}, u32[]{:S(2)}, u32[]{:S(2)}) collective-permute-start(f32[240,768]{1,0:T(8,128)S(1)} %pad_maximum_fusion.8), channel_id=1, source_target_pairs={{0,8},{4,12},{8,0},{12,4},{16,24},{20,28},{24,16},{28,20},{1,9},{5... | collective-permute-start | bytes 2211848 | tf_op jit(solution)/shard_map/ppermute | solution.py:493
  258.2 18.8 %collective-permute-start.49 = (f32[192,768]{1,0:T(8,128)S(1)}, f32[192,768]{1,0:T(8,128)S(1)}, u32[]{:S(2)}, u32[]{:S(2)}) collective-permute-start(f32[192,768]{1,0:T(8,128)S(1)} %pad_maximum_fusion.19), channel_id=1, source_target_pairs={{0,16},{4,20},{8,24},{12,28},{16,0},{20,4},{24,8},{28,12},{1,17},{... | collective-permute-start | bytes 1769480 | tf_op jit(solution)/shard_map/ppermute | solution.py:493
  280.1 27.4 %collective-permute-start.50 = (f32[304,768]{1,0:T(8,128)}, f32[304,768]{1,0:T(8,128)S(1)}, u32[]{:S(2)}, u32[]{:S(2)}) collective-permute-start(f32[304,768]{1,0:T(8,128)} %pad_maximum_fusion.2), channel_id=1, source_target_pairs={{0,1},{1,0},{2,3},{3,2},{4,5},{5,4},{6,7},{7,6},{8,9},{9,8},{10,11... | collective-permute-start | bytes 2801672 | tf_op jit(solution)/shard_map/ppermute | solution.py:489
  281.1 26.4 %collective-permute-start.53 = (f32[4,72,768]{2,1,0:T(8,128)}, f32[4,72,768]{2,1,0:T(8,128)}, u32[]{:S(2)}, u32[]{:S(2)}) collective-permute-start(f32[4,72,768]{2,1,0:T(8,128)} %get-tuple-element.1365), channel_id=1, source_target_pairs={{0,4},{4,0},{8,12},{12,8},{16,20},{20,16},{24,28},{28,24},{1,5},{5... | collective-permute-start | bytes 2654216 | tf_op jit(solution)/shard_map/ppermute | solution.py:493
  281.3 26.2 %collective-permute-start.52 = (f32[264,768]{1,0:T(8,128)S(1)}, f32[264,768]{1,0:T(8,128)S(1)}, u32[]{:S(2)}, u32[]{:S(2)}) collective-permute-start(f32[264,768]{1,0:T(8,128)S(1)} %pad_maximum_fusion.5.a_ref), channel_id=1, source_target_pairs={{0,16},{4,20},{8,24},{12,28},{16,0},{20,4},{24,8},{28,12},{1,17},{... | collective-permute-start | bytes 2433032 | tf_op jit(solution)/shard_map/ppermute | solution.py:493
  282.4 25.1 %collective-permute-start.51 = (f32[192,768]{1,0:T(8,128)S(1)}, f32[192,768]{1,0:T(8,128)}, u32[]{:S(2)}, u32[]{:S(2)}) collective-permute-start(f32[192,768]{1,0:T(8,128)S(1)} %pad_maximum_fusion.20.a_ref), channel_id=1, source_target_pairs={{0,8},{4,12},{8,0},{12,4},{16,24},{20,28},{24,16},{28,20},{1,9},{5... | collective-permute-start | bytes 1769480 | tf_op jit(solution)/shard_map/ppermute | solution.py:493
  308.8 17.8 %collective-permute-start.54 = (f32[136,768]{1,0:T(8,128)S(1)}, f32[136,768]{1,0:T(8,128)S(1)}, u32[]{:S(2)}, u32[]{:S(2)}) collective-permute-start(f32[136,768]{1,0:T(8,128)S(1)} %slice.442), channel_id=1, source_target_pairs={{0,1},{1,0},{2,3},{3,2},{4,5},{5,4},{6,7},{7,6},{8,9},{9,8},{10,11... | collective-permute-start | bytes 1253384 | tf_op jit(solution)/shard_map/ppermute | solution.py:489
  311.2 15.5 %collective-permute-start.55 = (f32[2,72,768]{2,1,0:T(8,128)S(1)}, f32[2,72,768]{2,1,0:T(8,128)S(1)}, u32[]{:S(2)}, u32[]{:S(2)}) collective-permute-start(f32[2,72,768]{2,1,0:T(8,128)S(1)} %get-tuple-element.1450), channel_id=1, source_target_pairs={{0,8},{4,12},{8,0},{12,4},{16,24},{20,28},{24,16},{28,20},{1,9},{5... | collective-permute-start | bytes 1327112 | tf_op jit(solution)/shard_map/ppermute | solution.py:493
  (119 other events, 1039.1 us)
where the time goes:
time: 377 us; the launch traced here: 373 us
  Pallas kernels  142 us (38%)
  waiting for transfers between devices  108 us (29%)
  starting transfers between devices  65.6 us (17%)
  local copies, waits for them, and re-layouts  33 us (9%)
  other arithmetic  21.7 us (6%)
    ppermute x21, waiting for transfers between devices, swap_mp(): return lax.ppermute(a, 'mp', [(s, s ^ k) for s in range(size)])  62.6 us
    ppermute x50, starting transfers between devices, swap_plane(): return lax.ppermute(a, 'dp', [(d, d ^ bit) for d in range(size)])  38.6 us
    ppermute x50, waiting for transfers between devices, swap_plane(): return lax.ppermute(a, 'dp', [(d, d ^ bit) for d in range(size)])  34.9 us
    pallas_call x2, Pallas kernels, run_attn_bwd(): call(functools.partial(attn_bwd_kernel, first), (sds((half, 3 * part, wid...  33.2 us
    pallas_call x4, Pallas kernels, run_mlp(): call(functools.partial(mlp_kernel, MLP_KIND[k], keeps), shapes, flops=2 *...  30.3 us
    ppermute x21, starting transfers between devices, swap_mp(): return lax.ppermute(a, 'mp', [(s, s ^ k) for s in range(size)])  24.1 us
    pallas_call x2, Pallas kernels, run_down(): call(functools.partial(down_kernel, nmp), sds((2, share, width), F32), fl...  15.1 us
    pallas_call x1, Pallas kernels, run_mid(): call(functools.partial(mid_kernel, nmp), shapes, flops=2 * share * width...  11 us
  transfers between devices with their start and end apart: 74, of which 38 were waited for; matrix products, arithmetic and copies ran while one was open for 10% of the time, Pallas kernels for 37%

commit v1 on v0

--- a/solution.py
+++ b/solution.py
@@ -129,9 +129,14 @@
         rows = wf_ref[pl.ds(pl.multiple_of(me * part, 8), part), :]
         att_ref[s * part : (s + 1) * part, :] = rows
         b_ref[0:1, s * e : (s + 1) * e] = qb_ref[s : s + 1, :]
-    upart = ub_ref.shape[1]
+    upart = up_ref.shape[1] // PIECES
+    ub = ub_ref[...].reshape(1, PIECES * upart)
     for s in range(PIECES // 2):
-        b_ref[1:2, s * upart : (s + 1) * upart] = ub_ref[pl.ds(me ^ offset_of(s, BITS_A), 1), :]
+        piece = jnp.zeros((1, upart), F32)
+        for p in range(PIECES):
+            here = (me ^ offset_of(s, BITS_A)) == p
+            piece = piece + jnp.where(here, ub[:, p * upart : (p + 1) * upart], 0.0)
+        b_ref[1:2, s * upart : (s + 1) * upart] = piece
     wf_ref[...] = o_ref[...].astype(F32)
     rows = wf_ref[pl.ds(pl.multiple_of(me * part, 8), part), :]
     att_ref[3 * part : 4 * part, :] = rows
@@ -313,28 +318,35 @@
     out_ref[1] = mm(cat(gps, 1), cat(ubs, 0))
 
 
-def mid_kernel(nslot, idx_ref, mid_ref, own_ref, got_ref, cot_ref, db_ref, g_ref, *refs):
+def mid_kernel(nslot, mid_ref, own_ref, got_ref, cot_ref, db_ref, g_ref, *refs):
     ows = refs[:nslot]
-    mixts = refs[nslot : 2 * nslot]
-    gmts = refs[2 * nslot : 3 * nslot]
-    bo_ref, gm_ref, gow_keep, gow_send, st_ref = refs[3 * nslot :]
-    part = 24
+    gmts = refs[nslot : 2 * nslot]
+    bo_ref, gm_ref, low_ref, st_ref = refs[2 * nslot :]
     mid = mid_ref[...]
-    bo_ref[...] = (mid + (own_ref[0] + got_ref[0]) + db_ref[...]).astype(BF16)
     n, rstd = row_norm(mid)
     e = own_ref[1] + got_ref[1]
     cot = cot_ref[...].astype(F32)
     gm = cot + row_norm_back(e * g_ref[...], n, rstd)
     gm_ref[...] = gm
     gm_low = gm.astype(BF16)
+    low_ref[...] = gm_low
+    for k in range(nslot):
+        gmts[k][...] = mm_nt(ows[k][...], gm_low).astype(gmts[k].dtype)
+    bo_ref[...] = (mid + (own_ref[0] + got_ref[0]) + db_ref[...]).astype(BF16)
     st_ref[0:1, :] = jnp.sum(e * n, axis=0, keepdims=True)
     st_ref[1:2, :] = jnp.sum(e, axis=0, keepdims=True)
     st_ref[2:3, :] = jnp.sum(gm_low.astype(F32), axis=0, keepdims=True)
     st_ref[3:4, :] = jnp.sum(cot, axis=0, keepdims=True)
     st_ref[4:8, :] = jnp.zeros((4, mid.shape[1]), F32)
+
+
+def out_grad_kernel(nslot, idx_ref, low_ref, *refs):
+    mixts = refs[:nslot]
+    gow_keep, gow_send = refs[nslot:]
+    part = 24
+    gm_low = low_ref[...]
     for k in range(nslot):
-        gmts[k][...] = mm_nt(ows[k][...], gm_low).astype(gmts[k].dtype)
-        g = mm(mix_of(mixts[k], mid.shape[0]), gm_low)
+        g = mm(mix_of(mixts[k], gm_low.shape[0]), gm_low)
         for p in range(PIECES):
             at = idx_ref[p]
             rows = slice(k * part, (k + 1) * part)
@@ -423,28 +435,58 @@
     gn_ref[...] = gn if first else gn_in[...] + gn
 
 
-def norm1_stats_kernel(blk_ref, x_ref, gn_ref, out_ref):
+def sums_kernel(
+    nslot, blk_ref, me_ref, x_ref, gn_ref, mst_ref, h0_ref, h2_ref, b0_ref, b2_ref, *refs
+):
+    ubs = refs[:nslot]
+    out_ref = refs[nslot]
     n, _ = row_norm(x_ref[...].astype(F32))
     e = gn_ref[...]
 
     @pl.when(pl.program_id(0) == 0)
     def _():
         out_ref[...] = jnp.zeros_like(out_ref)
-
-    out_ref[0:1, :] += jnp.sum(e * n, axis=0, keepdims=True)
-    out_ref[1:2, :] += jnp.sum(e, axis=0, keepdims=True)
-
-
-def final_kernel(blk_ref, x_ref, gn_ref, got_ref, gm_ref, g_ref, out_ref):
-    n, rstd = row_norm(x_ref[...].astype(F32))
-    f = (gn_ref[...] + got_ref[...]) * g_ref[...]
-    out_ref[...] = (gm_ref[...] + row_norm_back(f, n, rstd)).astype(BF16)
-
-
-def both(refs, to_ref):
-    half = PIECES // 2
-    to_ref[0:half] = refs[0][...]
-    to_ref[half:] = refs[1][...]
+        out_ref[0:4, :] = mst_ref[0:4, :]
+        heads = jnp.concatenate([h0_ref[i] + h2_ref[i] for i in range(3)], axis=0).T
+        out_ref[6:7, 0 : heads.shape[1]] = jnp.sum(heads, axis=0, keepdims=True)
+        me = me_ref[0]
+        upart = out_ref.shape[1] // PIECES
+        for row, k in zip((8, 10, 12, 14), (0, 2, 1, 3)):
+            if k % 2 == 0:
+                cols = (b0_ref if k == 0 else b2_ref)[...].T
+                out_ref[row : row + 1, 0 : cols.shape[1]] = jnp.sum(cols, axis=0, keepdims=True)
+            mine = ubs[k][...]
+            for p in range(PIECES):
+                piece = jnp.zeros((1, upart), F32)
+                for t in range(PIECES // 2):
+                    here = (me ^ offset_of(t, BITS_A)) == p
+                    piece = piece + jnp.where(here, mine[:, t * upart : (t + 1) * upart], 0.0)
+                out_ref[row + 1 : row + 2, p * upart : (p + 1) * upart] = piece
+
+    out_ref[4:5, :] += jnp.sum(e * n, axis=0, keepdims=True)
+    out_ref[5:6, :] += jnp.sum(e, axis=0, keepdims=True)
+
+
+def small_out_kernel(a_ref, b_ref, qb_ref, h0_ref, h1_ref, h2_ref, *rows):
+    total = a_ref[...] + b_ref[...]
+    for row, ref in zip((0, 1, 2, 3, 4, 5, 9), rows):
+        ref[...] = total[row]
+    for i, ref in enumerate((h0_ref, h1_ref, h2_ref)):
+        ref[...] = total[6, i * DH : (i + 1) * DH]
+        n = qb_ref.shape[1]
+        qb_ref[i : i + 1, :] = total[8:9, i * n : (i + 1) * n]
+
+
+def final_kernel(blk_ref, x_ref, gn_ref, *refs):
+    gots = refs[:-3]
+    gm_ref, g_ref, out_ref = refs[-3:]
+    at = 0
+    for ref in gots:
+        rows = slice(at, at + ref.shape[0])
+        n, rstd = row_norm(x_ref[rows, :].astype(F32))
+        f = (gn_ref[rows, :] + ref[...]) * g_ref[...]
+        out_ref[rows, :] = (gm_ref[rows, :] + row_norm_back(f, n, rstd)).astype(BF16)
+        at += ref.shape[0]
 
 
 def lay_out(refs, to_ref):
@@ -467,22 +509,16 @@
         out_ref[p * part : (p + 1) * part, :] = s_ref[idx_ref[p]]
 
 
-def unpack_att_kernel(
-    ia_ref, ib_ref, a0_ref, a1_ref, b0_ref, b1_ref, qkv_ref, out_ref, a_ref, b_ref
-):
-    part = a_ref.shape[1] // 2
-    both((a0_ref, a1_ref), a_ref)
-    both((b0_ref, b1_ref), b_ref)
-
-    def whole(ref, i_ref, off):
-        return jnp.concatenate(
-            [ref[i_ref[p], off : off + part, :] for p in range(PIECES)], axis=0
-        )
-
-    qkv_ref[0] = whole(a_ref, ia_ref, 0)
-    qkv_ref[1] = whole(a_ref, ia_ref, part)
-    qkv_ref[2] = whole(b_ref, ib_ref, 0)
-    out_ref[...] = whole(b_ref, ib_ref, part)
+def unpack_att_kernel(i_ref, a_ref, b_ref, qkv_ref, out_ref, s_ref):
+    rows = s_ref.shape[1]
+    part = rows // 4
+    half = PIECES // 2
+    for j in range(half):
+        s_ref[j] = a_ref[j * rows : (j + 1) * rows, :]
+        s_ref[half + j] = b_ref[j * rows : (j + 1) * rows, :]
+    for s, ref in enumerate((qkv_ref.at[0], qkv_ref.at[1], qkv_ref.at[2], out_ref)):
+        for p in range(PIECES):
+            ref[p * part : (p + 1) * part, :] = s_ref[i_ref[p], s * part : (s + 1) * part, :]
 
 
 def swap_mp(a, k, size):
@@ -578,11 +614,11 @@
         out_specs=(vmem,) * 8,
         scratch_shapes=[pltpu.VMEM((units, width), F32), pltpu.VMEM((e, width), F32)],
     )(
-        me1, qkv_t, out_weight, qkv_bias, up_bias.reshape(PIECES, upart), up_weight, down_weight
+        me1, qkv_t, out_weight, qkv_bias, up_bias, up_weight, down_weight
     )
 
-    n_gn = (256, 136, 120)
-    n_z2 = 56
+    n_gn = (256, 88, 80, 88)
+    n_z2 = 64
     numbers = jnp.arange(PIECES, dtype=jnp.int32)
     idx_a = storage_of(numbers ^ me, BITS_A).astype(jnp.int32)
     idx_b = storage_of(numbers ^ me, BITS_B).astype(jnp.int32)
@@ -758,30 +794,41 @@
             *[sds((e, share), F32 if k % 2 else BF16) for k in range(nmp)],
             sds((share, width), BF16),
             sds((share, width), F32),
-            sds((half, nmp * part, width), F32),
-            sds((half, nmp * part, width), F32),
+            sds((share, width), BF16),
             sds((8, width), F32),
         )
-        args = [
+        *gmts, bo, gm, low, mst = call(
+            functools.partial(mid_kernel, nmp),
+            shapes,
+            flops=2 * share * width * e * nmp,
+            bytes_accessed=12_000_000,
+            in_specs=[vmem] * (6 + nmp),
+            out_specs=(vmem,) * (4 + nmp),
+        )(
             v["middle"], v.pop("acc_own"), v.pop("acc_got"), v["cot"], row1(down_bias),
-            row1(norm2_gain), *ows, *mixes,
-        ]
+            row1(norm2_gain), *ows,
+        )
+        v["block_out"], v["gm"], v["mst"] = bo, gm, mst
+        for k in range(nmp):
+            v[f"gmt{k}"] = gmts[k]
+        return low
+
+    def run_out_grad(low):
+        mixes, ows = by_slot()
+        args = [low, *mixes]
         specs = [whole(a) for a in args]
         for k in (1, 3):
-            specs[6 + nmp + k] = pl.BlockSpec((mix_rows, width), lambda t: (0, 0))
-        *gmts, bo, gm, keep, send, mst = call(
-            functools.partial(mid_kernel, nmp),
+            specs[1 + k] = pl.BlockSpec((mix_rows, width), lambda t: (0, 0))
+        shapes = (sds((half, nmp * part, width), F32),) * 2
+        v["o"] = call(
+            functools.partial(out_grad_kernel, nmp),
             shapes,
-            flops=2 * share * width * e * nmp * 2,
-            bytes_accessed=12_000_000,
+            flops=2 * share * width * e * nmp,
+            bytes_accessed=5_000_000,
             grid=(1,),
             in_specs=[smem] + specs,
             out_specs=tuple(whole(a) for a in shapes),
         )(idx_b, *args)
-        v["block_out"], v["gm"], v["mst"] = bo, gm, mst
-        for k in range(nmp):
-            v[f"gmt{k}"] = gmts[k]
-        v["o"] = (keep, send)
 
     def run_attn_bwd(k, got, idx, first):
         st = v.pop(f"st{k}")
@@ -860,17 +907,21 @@
         k0, k1, s0, g1 = v[f"w{k}"]
         v[f"w{k}"] = (k0, k1, g1, swap(s0, first_link(k)))
 
-    def c2(k):
+    def c2u(k):
         k0, k1, g1, g0 = v[f"w{k}"]
         q = v.pop(f"q{k + 1}u")
-        k1 = jnp.concatenate([k1[:upart] + q[upart:], k1[upart:]], axis=0) + g1
-        v[f"w{k}"] = (k0, g0, q[:upart], swap(k1, second_link(k)))
+        sent = k1[:upart] + q[upart:] + g1[:upart]
+        v[f"w{k}"] = (k0, k1, g1, g0, q, swap(sent, second_link(k)))
+
+    def c2d(k):
+        k0, k1, g1, g0, q, gu = v[f"w{k}"]
+        up_sum = k0[:upart] + g0[:upart] + q[:upart] + gu
+        sent = k1[upart:] + g1[upart:]
+        v[f"w{k}"] = (up_sum, k0[upart:], g0[upart:], swap(sent, second_link(k)))
 
     def c3(k):
-        k0, g0, q, g = v[f"w{k}"]
-        d = v.pop(f"d{k + 1}")
-        total = k0 + g0 + g
-        v[f"w{k}"] = jnp.concatenate([total[:upart] + q, total[upart:] + d], axis=0)
+        up_sum, kd, g0, gd = v[f"w{k}"]
+        v[f"w{k}"] = (up_sum, kd + g0 + gd + v.pop(f"d{k + 1}"))
 
     def e1(k):
         k0, k1, s = v[f"w{k}"]
@@ -899,12 +950,15 @@
             bit *= 2
         return a
 
-    v["cot"] = lax.dynamic_slice_in_dim(cotangent, mp_no * share, share, 0)
+    cot_all, att_piece, ob_piece, mlp_piece = lax.optimization_barrier(
+        (cotangent, att_piece, ob_piece, mlp_piece)
+    )
+    v["cot"] = lax.dynamic_slice_in_dim(cot_all, mp_no * share, share, 0)
+    v["cot_f"] = v["cot"].astype(F32)
     v["piece"] = mlp_piece
     v["o3"] = zswap(ob_piece, 3)
     v["o1"] = zswap(ob_piece, 1)
     v["t2"] = zswap(att_piece, 2)
-    v["cot_p"] = swap(v["cot"].astype(F32), core)
     v["normed"] = run_norm1()
     v.fence()
     hp = 2 * part
@@ -912,6 +966,7 @@
     v["ta"] = jnp.concatenate([t2[:hp], o1[:part]], axis=0)
     v["tb"] = jnp.concatenate([t2[hp : 2 * hp], o3[:part]], axis=0)
     g1("t")
+    v["cot_p"] = swap(v.pop("cot_f"), core)
     v["m1"] = zswap(v["piece"], 1)
     v["mid_a"] = middle_swap(v.pop("piece"))
     v.fence()
@@ -987,27 +1042,30 @@
     v.fence()
     d13 = v.pop("d13")
     v["d1"], v["d3"] = d13[:upart], d13[upart:]
-    c2(0)
-    c2(2)
-    run_mid()
+    c2u(0)
+    c2u(2)
+    v["low"] = run_mid()
+    v.fence()
+    c2d(0)
+    c2d(2)
+    v["gp2"] = zswap(v.pop("gmt3"), 1)
+    v["z2x"] = zswap(v["w2"][0][:n_z2], 2)
+    run_out_grad(v.pop("low"))
     v.fence()
     c3(0)
     c3(2)
-    w2 = v.pop("w2")
-    v["z2x"] = zswap(w2[:n_z2], 2)
-    v["z2s"] = w2[n_z2:]
-    v["gp2"] = zswap(v.pop("gmt3"), 1)
+    up_sum, down_sum = v.pop("w2")
+    v["z2y"] = zswap(jnp.concatenate([up_sum[n_z2:], down_sum], axis=0), 2)
+    v["gp0"] = zswap(v.pop("gmt1"), 1)
     r1("o")
-    v.fence()
-    v["gp0"] = zswap(v.pop("gmt1"), 1)
-    v["z2y"] = zswap(v.pop("z2s"), 2)
     r2("o", "b")
     run_attn_bwd(2, "gp2", idx_b, True)
     v.fence()
     r1("q2")
     v.fence()
     mlp_sum = high_bits(
-        v.pop("w0") + jnp.concatenate([v.pop("z2x"), v.pop("z2y")], axis=0)
+        jnp.concatenate(v.pop("w0"), axis=0)
+        + jnp.concatenate([v.pop("z2x"), v.pop("z2y")], axis=0)
     )
     ma, mb = mlp_sum[:upart], mlp_sum[upart:]
     keep, got = v["q2"]
@@ -1032,46 +1090,46 @@
         jnp.concatenate([v["gn"][share : share + n_gn[0]], o[part : 2 * part], o[3 * part :]], axis=0), 1
     )
     v["o0"], v["o2"] = o[:part], o[2 * part : 3 * part]
-    n1_stats = call(
-        norm1_stats_kernel,
-        sds((8, width), F32),
+    v["small"] = call(
+        functools.partial(sums_kernel, nmp),
+        sds((16, width), F32),
         flops=full * width * 10,
         bytes_accessed=full * width * 6,
         grid_spec=pltpu.PrefetchScalarGridSpec(
-            num_scalar_prefetch=1,
+            num_scalar_prefetch=2,
             grid=(steps,),
-            in_specs=[tok_spec, run_spec],
-            out_specs=pl.BlockSpec((8, width), const2),
+            in_specs=[
+                pl.BlockSpec((block, width), lambda t, b, m: (b[t], 0)),
+                pl.BlockSpec((block, width), lambda t, b, m: (t, 0)),
+                pl.BlockSpec((8, width), lambda t, b, m: (0, 0)),
+                *[pl.BlockSpec((3, DH, 128), lambda t, b, m: (0, 0, 0))] * 2,
+                *[pl.BlockSpec((3 * e, 128), lambda t, b, m: (0, 0))] * 2,
+                *[pl.BlockSpec((1, mine), lambda t, b, m: (0, 0))] * nmp,
+            ],
+            out_specs=pl.BlockSpec((16, width), lambda t, b, m: (0, 0)),
         ),
-    )(blk, tokens, v["gn"])
-    head_sum = jnp.sum(v.pop("hst0") + v.pop("hst2"), axis=-1)
-    copied = jnp.concatenate(
-        [v.pop("mst")[:4].reshape(-1), n1_stats[:2].reshape(-1), head_sum.reshape(-1)]
+    )(
+        blk, me1, tokens, v["gn"], v.pop("mst"), v.pop("hst0"), v.pop("hst2"), v.pop("qbg0"),
+        v.pop("qbg2"), *[v.pop(f"ubg{k}") for k in range(nmp)],
     )
-    own_parts = []
-    for k in range(nmp):
-        qb = jnp.zeros((3 * e,), F32) if k % 2 else jnp.sum(v.pop(f"qbg{k}"), axis=1)
-        ubg = jnp.pad(v.pop(f"ubg{k}").reshape(half, upart), ((0, half), (0, 0)))
-        own_parts.append(jnp.concatenate([qb, jnp.take(ubg, idx_a, axis=0).reshape(-1)]))
-    nc = copied.shape[0]
-    no = own_parts[0].shape[0]
-    v["small"] = jnp.concatenate([copied] + own_parts)
     v.fence()
     r2("q0", "b")
     (xa, xb), (ya, yb) = v["gx"], v["gy"]
     gn0 = v.pop("gn0")
-    v["gn0"] = gn0[: n_gn[0]]
+    v["gn0"] = gn0
     v["o0"] = v["o0"] + gn0[n_gn[0] : n_gn[0] + part]
     o2 = v.pop("o2") + gn0[n_gn[0] + part :]
     q2 = v.pop("q2") + yb[2 * upart :]
     v["y2"] = zswap(jnp.concatenate([q2, o2], axis=0), 2)
     at = share + n_gn[0]
     v["gn1"] = zswap(v["gn"][at : at + n_gn[1]], 1)
-    v["small"] = v["small"] + swap(v["small"], core)
+    small = v["small"] + swap(v["small"], core)
+    v["small"] = small + swap(small, px)
     v.fence()
     r3("q0", "b")
-    v["gn2"] = zswap(v["gn"][share + n_gn[0] + n_gn[1] :], 1)
-    v["small"] = v["small"] + swap(v["small"], px)
+    at = share + n_gn[0] + n_gn[1]
+    v["gn2"] = zswap(v["gn"][at : at + n_gn[2]], 1)
+    v["small"] = v["small"] + swap(v["small"], py)
     ya, yb = v.pop("gy")
     v["gu"] = (ya, yb, swap(ya, core), swap(yb, core))
     v.fence()
@@ -1079,31 +1137,12 @@
     att_sum = high_bits(
         jnp.concatenate([v.pop("q0"), v.pop("o0")], axis=0) + v.pop("y2")
     )
-    v["wa"], v["wb"] = att_sum[:hp], att_sum[hp:]
-    g1("w")
+    v["w"] = (att_sum, swap(att_sum, px), swap(att_sum, py), swap(att_sum, px | py))
     xa, xb = v.pop("gx")
-    v["gd"] = (xa, xb, swap(xa, core), swap(xb, core))
-    v["small"] = v["small"] + swap(v["small"], py)
-    v["input_grad"] = call(
-        final_kernel,
-        sds((share, width), BF16),
-        flops=share * width * 20,
-        bytes_accessed=share * width * 16,
-        grid_spec=pltpu.PrefetchScalarGridSpec(
-            num_scalar_prefetch=1,
-            grid=(per,),
-            in_specs=[tok_spec, run_spec, run_spec, run_spec, vec_spec],
-            out_specs=run_spec,
-        ),
-    )(
-        blk,
-        tokens,
-        v["gn"],
-        jnp.concatenate([v.pop("gn0"), v.pop("gn1"), v.pop("gn2")], axis=0),
-        v["gm"],
-        row1(norm1_gain),
-    )
-    v.fence()
+    gd = (xa, xb, swap(xa, core), swap(xb, core))
+    small = high_bits(v.pop("small"))
+    got = zswap(jnp.concatenate([small[:8], small[12:]], axis=0), 1)
+    v["small"] = small[:12] + got
 
     def unpack(kernel, arrays, idx, shape):
         pieces_spec = pl.BlockSpec((2 * upart, width), lambda t: (0, 0))
@@ -1117,43 +1156,57 @@
             scratch_shapes=[pltpu.VMEM((PIECES, upart, width), F32)],
         )(idx, *arrays)
 
-    g2("w")
-    small = high_bits(v.pop("small"))
-    parts = [small[nc + k * no : nc + (k + 1) * no] for k in range(nmp)]
-    sent = jnp.concatenate([small[:nc], parts[1], parts[3]])
-    got = zswap(sent, 1)
-    v["small"] = jnp.concatenate([small[:nc], parts[0], parts[2]]) + got
     v["up_g"] = unpack(unpack_kernel, v.pop("gu"), idx_a, (width, units))
-    v["down_g"] = unpack(unpack_rows_kernel, v.pop("gd"), idx_b, (units, width))
-    v.fence()
-    wa, wb = (jnp.concatenate(v.pop("w" + t), axis=0) for t in "ab")
+    v["down_g"] = unpack(unpack_rows_kernel, gd, idx_b, (units, width))
+    v["gn3"] = zswap(v["gn"][full - n_gn[3] :], 1)
+    v.fence()
+    input_grad = call(
+        final_kernel,
+        sds((share, width), BF16),
+        flops=share * width * 20,
+        bytes_accessed=share * width * 16,
+        grid_spec=pltpu.PrefetchScalarGridSpec(
+            num_scalar_prefetch=1,
+            grid=(1,),
+            in_specs=[
+                pl.BlockSpec((share, width), lambda t, b: (b[0] // per, 0)),
+                pl.BlockSpec((share, width), const2),
+                *[pl.BlockSpec((n, width), const2) for n in n_gn],
+                pl.BlockSpec((share, width), const2),
+                vec_spec,
+            ],
+            out_specs=pl.BlockSpec((share, width), const2),
+        ),
+    )(blk, tokens, v["gn"], *[v[f"gn{i}"] for i in range(4)], v["gm"], row1(norm1_gain))
+    w = jnp.concatenate(v.pop("w"), axis=0)
     small = v.pop("small")
-    got = zswap(jnp.concatenate([small[:nc], small[nc + no :]]), 2)
-    v["small_sum"] = small[: nc + no] + got
+    small_got = zswap(jnp.concatenate([small[:8], small[10:]], axis=0), 2)
     qkv_weight_grad, out_weight_grad = call(
         unpack_att_kernel,
         (sds((3, e, width), F32), sds((e, width), F32)),
         bytes_accessed=2 * 4 * 4 * width * e,
-        in_specs=[smem, smem] + [vmem] * 4,
+        in_specs=[smem] + [vmem] * 2,
         out_specs=(vmem, vmem),
-        scratch_shapes=[pltpu.VMEM((PIECES, hp, width), F32)] * 2,
-    )(idx_a, idx_b, wa, swap(wa, core), wb, swap(wb, core))
+        scratch_shapes=[pltpu.VMEM((PIECES, 4 * part, width), F32)],
+    )(idx_a, w, swap(w, core))
     qkv_weight_grad = jnp.swapaxes(qkv_weight_grad, 1, 2)
-
-    small_sum = v["small_sum"]
-    rows_of = small_sum[: 6 * width].reshape(6, width)
-    heads_of = small_sum[6 * width : nc].reshape(3, DH)
-    qkv_bias_grad = small_sum[nc : nc + 3 * e].reshape(3, e)
-    up_bias_grad = small_sum[nc + 3 * e :]
+    qkv_bias_grad, *rows_of = call(
+        small_out_kernel,
+        (sds((3, e), F32), *[sds((DH,), F32)] * 3, *[sds((width,), F32)] * 7),
+        bytes_accessed=100_000,
+        in_specs=[vmem, vmem],
+        out_specs=(vmem,) * 11,
+    )(small[:10], small_got)
+    heads_of, rows_of = rows_of[:3], rows_of[3:]
     return (
         v["block_out"],
-        v["input_grad"],
+        input_grad,
         qkv_weight_grad,
         qkv_bias_grad,
         out_weight_grad,
         rows_of[2],
         v["up_g"],
-        up_bias_grad,
+        rows_of[6],
         v["down_g"],
         rows_of[3],
         rows_of[4],

time: 377 us -> 361 us (0.958)
  local copies, waits for them, and re-layouts: 33 us -> 20 us
  other arithmetic: 21.7 us -> 14.6 us
  Pallas kernels: 142 us -> 147 us
    ppermute x21 -> x22, waiting for transfers between devices: 62.6 us -> 39.2 us  [swap_mp(): return lax.ppermute(a, 'mp', [(s, s ^ k) for s in range(size)])]
    ppermute x50, waiting for transfers between devices: 34.9 us -> 54.9 us  [swap_plane(): return lax.ppermute(a, 'dp', [(d, d ^ bit) for d in range(size)])]
    pallas_call x1 -> x3, Pallas kernels: 5.51 us -> 12.8 us  [the longest x1 6.26 us: shards(): call(functools.partial(sums_kernel, nmp), sds((16, width), F32), flops=fu...]
    reshape x12 -> x0, local copies, waits for them, and re-layouts: 5.79 us -> none  [the longest x4 3.54 us: shards(): jnp.take(ubg, idx_a, axis=0).reshape(-1)]
    ppermute x21 -> x22, starting transfers between devices: 24.1 us -> 25.7 us  [swap_mp(): return lax.ppermute(a, 'mp', [(s, s ^ k) for s in range(size)])]
    unnamed x150 -> x155, local copies, waits for them, and re-layouts: 9.5 us -> 9.35 us
  transfers between devices with their start and end apart: 74 -> 75, of which waited for: 38 -> 37; matrix products, arithmetic and copies ran while one was open for 10% -> 6% of each run, Pallas kernels for 37% -> 39%
where the time goes in v1:
time: 361 us; the launch traced here: 357 us
  Pallas kernels  147 us (41%)
  waiting for transfers between devices  105 us (29%)
  starting transfers between devices  68.6 us (19%)
  local copies, waits for them, and re-layouts  20 us (6%)
  other arithmetic  14.6 us (4%)
    ppermute x50, waiting for transfers between devices, swap_plane(): return lax.ppermute(a, 'dp', [(d, d ^ bit) for d in range(size)])  54.9 us
    ppermute x50, starting transfers between devices, swap_plane(): return lax.ppermute(a, 'dp', [(d, d ^ bit) for d in range(size)])  39.9 us
    ppermute x22, waiting for transfers between devices, swap_mp(): return lax.ppermute(a, 'mp', [(s, s ^ k) for s in range(size)])  39.2 us
    pallas_call x2, Pallas kernels, run_attn_bwd(): call(functools.partial(attn_bwd_kernel, first), (sds((half, 3 * part, wid...  33.2 us
    pallas_call x4, Pallas kernels, run_mlp(): call(functools.partial(mlp_kernel, MLP_KIND[k], keeps), shapes, flops=2 *...  30.4 us
    ppermute x22, starting transfers between devices, swap_mp(): return lax.ppermute(a, 'mp', [(s, s ^ k) for s in range(size)])  25.7 us
    pallas_call x2, Pallas kernels, run_down(): call(functools.partial(down_kernel, nmp), sds((2, share, width), F32), fl...  15.1 us
    ppermute x1, waiting for transfers between devices, pass_out(): return lax.ppermute(a, 'mp', [(1, 0), (2, 3)])  10.8 us
  transfers between devices with their start and end apart: 75, of which 37 were waited for; matrix products, arithmetic and copies ran while one was open for 6% of the time, Pallas kernels for 39%

profile of v1, /device:TPU:0, one launch (start us, length us, event | category | flops | bytes accessed | tf_op | source)
XLA Modules:
  0.0 357.1 jit_solution(6610901027452310730)
XLA Ops:
  0.7 4.1 %shard_map.305 = (f32[104,768]{1,0:T(8,128)}, f32[32,768]{1,0:T(8,128)}, f32[8,768]{1,0:T(8,128)}, f32[192,768]{1,0:T(8,128)}, bf16[2,96,768]{2,1,0:T(8,128)(2,1...) custom-call(s32[1]{0:T(128)} %bitcast.me_ref, ...), custom_call_target="tpu_custom_call" | custom-call | bytes 9000000 | tf_op jit(solution)/shard_map/pallas_call | solution.py:603
  4.7 4.0 %collective-permute-start.2 = (f32[104,768]{1,0:T(8,128)}, f32[104,768]{1,0:T(8,128)S(1)}, u32[]{:S(2)}, u32[]{:S(2)}) collective-permute-start(f32[104,768]{1,0:T(8,128)} %get-tuple-element.759), channel_id=1, source_target_pairs={{0,2},{1,3},{2,0},{3,1},{4,6},{5,7},{6,4},{7,5},{8,10},{9,11},{10,... | collective-permute-start | bytes 958472 | tf_op jit(solution)/shard_map/ppermute | solution.py:525
  12.0 4.8 %shard_map.306.x_ref = bf16[1024,768]{1,0:T(8,128)(2,1)} custom-call(s32[4]{0:T(128)} %compare_select_fusion.1.blk_ref, bf16[2048,768]{1,0:T(8,128)(2,1)} %x_ref.7, f32[1,768]{1,0:T(1,128)} %reshape.85.g_ref.refs_5_, f32[1,768]{1,0:T(1,128)} %reshape.86.s_ref), custom_call_target="tpu_custom_call" | custom-call | flops 7864320 | bytes 3145728 | tf_op jit(solution)/shard_map/pallas_call | solution.py:639
  21.9 4.5 %collective-permute-done.2.b_ref = f32[104,768]{1,0:T(8,128)S(1)} collective-permute-done((f32[104,768]{1,0:T(8,128)}, f32[104,768]{1,0:T(8,128)S(1)}, u32[]{:S(2)}, u32[]{:S(2)}) %collective-permute-start.2) | collective-permute-done | bytes 319520 | tf_op jit(solution)/shard_map/ppermute | solution.py:525
  33.2 4.3 %collective-permute-done.6 = f32[72,768]{1,0:T(8,128)S(1)} collective-permute-done((f32[72,768]{1,0:T(8,128)S(1)}, f32[72,768]{1,0:T(8,128)S(1)}, u32[]{:S(2)}, u32[]{:S(2)}) %collective-permute-start.6) | collective-permute-done | bytes 221216 | tf_op jit(solution)/shard_map/ppermute | solution.py:529
  38.8 4.3 %collective-permute-done.4 = f32[192,768]{1,0:T(8,128)S(1)} collective-permute-done((f32[192,768]{1,0:T(8,128)S(1)}, f32[192,768]{1,0:T(8,128)S(1)}, u32[]{:S(2)}, u32[]{:S(2)}) %collective-permute-start.4) | collective-permute-done | bytes 589856 | tf_op jit(solution)/shard_map/ppermute | solution.py:525
  50.5 7.7 %shard_map.307 = (f32[192,1024]{1,0:T(8,128)}, f32[192,1024]{1,0:T(8,128)}, bf16[192,1024]{1,0:T(8,128)(2,1)}, bf16[192,512]{1,0:T(8,128)(2,1)}, f32[192,1024]{1...) custom-call(bf16[1024,768]{1,0:T(8,128)(2,1)} %shard_map.306.x_ref, bf16[576,768]{1,0:T(8,128)(2,1)} %bitcast.55, ...), custom_call_target="tpu_custom_call" | custom-call | flops 4127195136 | bytes 10000000 | tf_op jit(solution)/shard_map/pallas_call | solution.py:686
  58.2 10.8 %collective-permute-done.8 = f32[192,768]{1,0:T(8,128)S(1)} collective-permute-done((f32[192,768]{1,0:T(8,128)S(1)}, f32[192,768]{1,0:T(8,128)S(1)}, u32[]{:S(2)}, u32[]{:S(2)}) %collective-permute-start.8) | collective-permute-done | bytes 589856 | tf_op jit(solution)/shard_map/ppermute | solution.py:944
  77.1 9.9 %shard_map.308 = (bf16[576,768]{1,0:T(8,128)(2,1)}, bf16[192,768]{1,0:T(8,128)(2,1)}, bf16[192,768]{1,0:T(8,128)(2,1)}, bf16[192,768]{1,0:T(8,128)(2,1)}, f32[19...) custom-call(s32[8]{0:T(128)} %get-tuple-element.1543.ia_ref.idx_ref., ...), custom_call_target="tpu_custom_call" | custom-call | flops 4127195136 | bytes 10000000 | tf_op jit(solution)/shard_map/pallas_call | solution.py:706
  99.2 6.1 %collective-permute-done.19.refs_3_ = f32[128,768]{1,0:T(8,128)S(1)} collective-permute-done((f32[128,768]{1,0:T(8,128)S(1)}, f32[128,768]{1,0:T(8,128)S(1)}, u32[]{:S(2)}, u32[]{:S(2)}) %collective-permute-start.19) | collective-permute-done | bytes 393248 | tf_op jit(solution)/shard_map/ppermute | solution.py:525
  106.0 5.6 %shard_map.309 = (f32[512,768]{1,0:T(8,128)}, bf16[512,768]{1,0:T(8,128)(2,1)}, f32[512,768]{1,0:T(8,128)}) custom-call(s32[4]{0:T(128)} %compare_select_fusion.1.blk_ref, bf16[2048,768]{1,0:T(8,128)(2,1)} %x_ref.7, bf16[192,512]{1,0:T(8,128)(2,1)} %get-tuple-element.1264.refs_0_, f32[320,768]{1,0:T(8,128)} %copy-done, ...), custom_call_target="tpu_custom_call" | custom-call | flops 603979776 | bytes 8000000 | tf_op jit(solution)/shard_map/pallas_call | solution.py:729
  116.5 7.8 %shard_map.310 = (bf16[1024,384]{1,0:T(8,128)(2,1)}, bf16[1024,384]{1,0:T(8,128)(2,1)}, bf16[384,768]{1,0:T(8,128)(2,1)}, bf16[384,768]{1,0:T(8,128)(2,1)}, f32[...) custom-call(bf16[512,768]{1,0:T(8,128)(2,1)} %get-tuple-element.1033, ...), custom_call_target="tpu_custom_call" | custom-call | flops 2415919104 | bytes 12000000 | tf_op jit(solution)/shard_map/pallas_call | solution.py:761
  124.3 3.4 collective-permute-done.21.u1_ref
  133.1 7.3 %shard_map.311 = (bf16[1024,384]{1,0:T(8,128)(2,1)}, bf16[1024,384]{1,0:T(8,128)(2,1)}, bf16[384,768]{1,0:T(8,128)(2,1)}, bf16[384,768]{1,0:T(8,128)(2,1)}, f32[...) custom-call(bf16[512,768]{1,0:T(8,128)(2,1)} %get-tuple-element.1033, ...), custom_call_target="tpu_custom_call" | custom-call | flops 2415919104 | bytes 12000000 | tf_op jit(solution)/shard_map/pallas_call | solution.py:761
  149.0 7.4 %shard_map.312 = (bf16[1024,384]{1,0:T(8,128)(2,1)}, bf16[1024,384]{1,0:T(8,128)(2,1)}, bf16[384,768]{1,0:T(8,128)(2,1)}, bf16[384,768]{1,0:T(8,128)(2,1)}, f32[...) custom-call(bf16[512,768]{1,0:T(8,128)(2,1)} %get-tuple-element.1033.sec, ...), custom_call_target="tpu_custom_call" | custom-call | flops 2415919104 | bytes 12000000 | tf_op jit(solution)/shard_map/pallas_call | solution.py:761
  164.1 7.9 %shard_map.313 = (bf16[1024,384]{1,0:T(8,128)(2,1)}, bf16[1024,384]{1,0:T(8,128)(2,1)}, bf16[384,768]{1,0:T(8,128)(2,1)}, bf16[384,768]{1,0:T(8,128)(2,1)}, f32[...) custom-call(bf16[512,768]{1,0:T(8,128)(2,1)} %get-tuple-element.1033.sec, ...), custom_call_target="tpu_custom_call" | custom-call | flops 2415919104 | bytes 12000000 | tf_op jit(solution)/shard_map/pallas_call | solution.py:761
  172.0 3.4 collective-permute-done.29
  177.4 7.5 %shard_map.314 = f32[2,512,768]{2,1,0:T(8,128)} custom-call(bf16[1024,384]{1,0:T(8,128)(2,1)} %get-tuple-element.1149.refs_0_, bf16[1024,384]{1,0:T(8,128)(2,1)} %get-tuple-element.1150.refs_1_, bf16[1024,384]{1,0:T(8,128)(2,1)} %get-tuple-element.1151.refs_2_, bf16[1024,384]{1,0:T(8,128)(2,1)} %get-tuple-element.1152.refs_3_, ...), custom_call_target="tpu_custom_call" | custom-call | flops 2415919104 | bytes 11000000 | tf_op jit(solution)/shard_map/pallas_call | solution.py:781
  190.6 7.6 %shard_map.315.own_ref = f32[2,512,768]{2,1,0:T(8,128)} custom-call(bf16[1024,384]{1,0:T(8,128)(2,1)} %get-tuple-element.1149.refs_0_, bf16[1024,384]{1,0:T(8,128)(2,1)} %get-tuple-element.1150.refs_1_, bf16[1024,384]{1,0:T(8,128)(2,1)} %get-tuple-element.1151.refs_2_, bf16[1024,384]{1,0:T(8,128)(2,1)} %get-tuple-element.1152.refs_3_, ...), custom_call_target="tpu_custom_call" | custom-call | flops 2415919104 | bytes 11000000 | tf_op jit(solution)/shard_map/pallas_call | solution.py:781
  198.2 3.8 %collective-permute-done.36 = f32[192,768]{1,0:T(8,128)S(1)} collective-permute-done((f32[192,768]{1,0:T(8,128)S(1)}, f32[192,768]{1,0:T(8,128)S(1)}, u32[]{:S(2)}, u32[]{:S(2)}) %collective-permute-start.36) | collective-permute-done | bytes 589856 | tf_op jit(solution)/shard_map/ppermute | solution.py:525
  207.7 7.5 %shard_map.316 = (bf16[192,512]{1,0:T(8,128)(2,1)}, f32[192,512]{1,0:T(8,128)}, bf16[192,512]{1,0:T(8,128)(2,1)}, f32[192,512]{1,0:T(8,128)}, bf16[512,768]{1,0:...) custom-call(f32[512,768]{1,0:T(8,128)} %get-tuple-element.1203.mid_ref, ...), custom_call_target="tpu_custom_call" | custom-call | flops 603979776 | bytes 12000000 | tf_op jit(solution)/shard_map/pallas_call | solution.py:800
  221.0 5.1 %shard_map.317 = (f32[4,96,768]{2,1,0:T(8,128)}, f32[4,96,768]{2,1,0:T(8,128)}) custom-call(s32[8]{0:T(128)} %get-tuple-element.1544.ib_ref.idx_ref, bf16[512,768]{1,0:T(8,128)(2,1)} %get-tuple-element.1263.low_ref, bf16[192,512]{1,0:T(8,128)(2,1)} %get-tuple-element.1264.refs_0_, f32[320,768]{1,0:T(8,128)} %copy-done, ...), custom_call_target="tpu_custom_call" | custom-call | flops 603979776 | bytes 5000000 | tf_op jit(solution)/shard_map/pallas_call | solution.py:823
  233.8 16.2 %shard_map.318 = (f32[4,72,768]{2,1,0:T(8,128)}, f32[4,72,768]{2,1,0:T(8,128)}, f32[1024,768]{1,0:T(8,128)}, f32[3,64,128]{2,1,0:T(8,128)}, f32[576,128]{1,0:T(8,128)}) custom-call(s32[8]{0:T(128)} %get-tuple-element.1544.ib_ref.idx_ref, bf16[1024,768]{1,0:T(8,128)(2,1)} %shard_map.306.x_ref, f32[192,1024]{1,0:T(8,128)} %get-tuple-element.1300.qpre_ref, ...), custom_call_target="tpu_custom_call" | custom-call | flops 9865003008 | bytes 14000000 | tf_op jit(solution)/shard_map/pallas_call | solution.py:843
  256.1 17.0 %shard_map.319 = (f32[4,72,768]{2,1,0:T(8,128)}, f32[4,72,768]{2,1,0:T(8,128)}, f32[1024,768]{1,0:T(8,128)}, f32[3,64,128]{2,1,0:T(8,128)}, f32[576,128]{1,0:T(8,128)}) custom-call(s32[8]{0:T(128)} %get-tuple-element.1544.ib_ref.idx_ref, bf16[1024,768]{1,0:T(8,128)(2,1)} %shard_map.306.x_ref, ...), custom_call_target="tpu_custom_call", output_to_operand_aliasing={{2}: (13, {})} | custom-call | flops 9865003008 | bytes 14000000 | tf_op jit(solution)/shard_map/pallas_call | solution.py:843
  280.0 6.3 %shard_map.320 = f32[16,768]{1,0:T(8,128)} custom-call(s32[4]{0:T(128)} %compare_select_fusion.1.blk_ref, s32[1]{0:T(128)} %bitcast.me_ref, bf16[2048,768]{1,0:T(8,128)(2,1)} %x_ref.7, f32[1024,768]{1,0:T(8,128)} %get-tuple-element.1463.gn_ref, f32[8,768]{1,0:T(8,128)} %get-tuple-element.1408.mst_ref, f32[3,64,128]{2,1,0:T(8,128)} %get-tuple-element.1409.h0_ref, ...), custom_call_target="tpu_custom_call" | custom-call | flops 7864320 | bytes 4718592 | tf_op jit(solution)/shard_map/pallas_call | solution.py:1093
  286.3 8.1 %collective-permute-done.53.b_ref = f32[192,768]{1,0:T(8,128)S(1)} collective-permute-done((f32[192,768]{1,0:T(8,128)S(1)}, f32[192,768]{1,0:T(8,128)S(1)}, u32[]{:S(2)}, u32[]{:S(2)}) %collective-permute-start.53) | collective-permute-done | bytes 589856 | tf_op jit(solution)/shard_map/ppermute | solution.py:529
  294.4 3.7 %collective-permute-done.54.b_ref = f32[264,768]{1,0:T(8,128)S(1)} collective-permute-done((f32[264,768]{1,0:T(8,128)S(1)}, f32[264,768]{1,0:T(8,128)S(1)}, u32[]{:S(2)}, u32[]{:S(2)}) %collective-permute-start.54) | collective-permute-done | bytes 811040 | tf_op jit(solution)/shard_map/ppermute | solution.py:529
  305.7 5.4 %collective-permute-done.59 = f32[16,768]{1,0:T(8,128)S(1)} collective-permute-done((f32[16,768]{1,0:T(8,128)S(1)}, f32[16,768]{1,0:T(8,128)S(1)}, u32[]{:S(2)}, u32[]{:S(2)}) %collective-permute-start.59) | collective-permute-done | bytes 49184 | tf_op jit(solution)/shard_map/ppermute | solution.py:529
  311.1 4.6 %collective-permute-done.56.refs_1_ = f32[88,768]{1,0:T(8,128)S(1)} collective-permute-done((f32[88,768]{1,0:T(8,128)S(1)}, f32[88,768]{1,0:T(8,128)S(1)}, u32[]{:S(2)}, u32[]{:S(2)}) %collective-permute-start.56) | collective-permute-done | bytes 270368 | tf_op jit(solution)/shard_map/ppermute | solution.py:525
  319.5 6.4 %collective-permute-done.65 = f32[16,768]{1,0:T(8,128)S(1)} collective-permute-done((f32[16,768]{1,0:T(8,128)S(1)}, f32[16,768]{1,0:T(8,128)S(1)}, u32[]{:S(2)}, u32[]{:S(2)}) %collective-permute-start.65) | collective-permute-done | bytes 49184 | tf_op jit(solution)/shard_map/ppermute | solution.py:529
  334.8 3.8 %shard_map.322 = f32[768,768]{1,0:T(8,128)} custom-call(s32[8]{0:T(128)} %get-tuple-element.1543.ia_ref.idx_ref.i_ref, f32[264,768]{1,0:T(8,128)} %copy-done.1, f32[264,768]{1,0:T(8,128)} %copy-done.9, f32[264,768]{1,0:T(8,128)} %copy-done.16, f32[264,768]{1,0:T(8,128)} %copy-done.17), custom_call_target="tpu_custom_call" | custom-call | bytes 4718592 | tf_op jit(solution)/shard_map/pallas_call | solution.py:1149
  345.0 5.1 %shard_map.323 = bf16[512,768]{1,0:T(8,128)(2,1)} custom-call(s32[4]{0:T(128)} %compare_select_fusion.1.blk_ref, bf16[2048,768]{1,0:T(8,128)(2,1)} %x_ref.7, f32[1024,768]{1,0:T(8,128)} %get-tuple-element.1463.gn_ref, f32[304,768]{1,0:T(8,128)} %copy-done.10, f32[88,768]{1,0:T(8,128)} %copy-done.39, f32[80,768]{1,0:T(8,128)} %copy-done.41, ...), custom_call_target="tpu_custom_call" | custom-call | flops 7864320 | bytes 6291456 | tf_op jit(solution)/shard_map/pallas_call | solution.py:1163
  (402 shorter events, 143.5 us)
Async XLA Ops:
  4.7 21.6 %collective-permute-start.2 = (f32[104,768]{1,0:T(8,128)}, f32[104,768]{1,0:T(8,128)S(1)}, u32[]{:S(2)}, u32[]{:S(2)}) collective-permute-start(f32[104,768]{1,0:T(8,128)} %get-tuple-element.759), channel_id=1, source_target_pairs={{0,2},{1,3},{2,0},{3,1},{4,6},{5,7},{6,4},{7,5},{8,10},{9,11},{10,... | collective-permute-start | bytes 958472 | tf_op jit(solution)/shard_map/ppermute | solution.py:525
  26.3 16.9 %collective-permute-start.3 = (f32[512,768]{1,0:T(8,128)S(1)}, f32[512,768]{1,0:T(8,128)}, u32[]{:S(2)}, u32[]{:S(2)}) collective-permute-start(f32[512,768]{1,0:T(8,128)S(1)} %get-tuple-element.761), channel_id=1, source_target_pairs={{0,4},{4,0},{8,12},{12,8},{16,20},{20,16},{24,28},{28,24},{1,5},{5... | collective-permute-start | bytes 4718600 | tf_op jit(solution)/shard_map/ppermute | solution.py:529
  27.1 16.1 %collective-permute-start.4 = (f32[192,768]{1,0:T(8,128)S(1)}, f32[192,768]{1,0:T(8,128)S(1)}, u32[]{:S(2)}, u32[]{:S(2)}) collective-permute-start(f32[192,768]{1,0:T(8,128)S(1)} %copy-done.62), channel_id=1, source_target_pairs={{0,1},{1,0},{2,3},{3,2},{4,5},{5,4},{6,7},{7,6},{8,9},{9,8},{10,11... | collective-permute-start | bytes 1769480 | tf_op jit(solution)/shard_map/ppermute | solution.py:525
  43.3 25.7 %collective-permute-start.10 = (f32[240,768]{1,0:T(8,128)S(1)}, f32[240,768]{1,0:T(8,128)S(1)}, u32[]{:S(2)}, u32[]{:S(2)}) collective-permute-start(f32[240,768]{1,0:T(8,128)S(1)} %pad_maximum_fusion.5), channel_id=1, source_target_pairs={{0,16},{4,20},{8,24},{12,28},{16,0},{20,4},{24,8},{28,12},{1,17},{... | collective-permute-start | bytes 2211848 | tf_op jit(solution)/shard_map/ppermute | solution.py:529
  44.9 24.0 %collective-permute-start.11 = (f32[240,768]{1,0:T(8,128)S(1)}, f32[240,768]{1,0:T(8,128)S(1)}, u32[]{:S(2)}, u32[]{:S(2)}) collective-permute-start(f32[240,768]{1,0:T(8,128)S(1)} %pad_maximum_fusion.6), channel_id=1, source_target_pairs={{0,8},{4,12},{8,0},{12,4},{16,24},{20,28},{24,16},{28,20},{1,9},{5... | collective-permute-start | bytes 2211848 | tf_op jit(solution)/shard_map/ppermute | solution.py:529
  47.4 21.6 %collective-permute-start.9 = (f32[192,768]{1,0:T(8,128)S(1)}, f32[192,768]{1,0:T(8,128)S(1)}, u32[]{:S(2)}, u32[]{:S(2)}) collective-permute-start(f32[192,768]{1,0:T(8,128)S(1)} %collective-permute-done.4), channel_id=1, source_target_pairs={{1,2},{2,1},{5,6},{6,5},{9,10},{10,9},{13,14},{14,13},{17,18},{18,... | collective-permute-start | bytes 1769480 | tf_op jit(solution)/shard_map/ppermute | solution.py:941
  48.1 20.9 %collective-permute-start.8 = (f32[192,768]{1,0:T(8,128)S(1)}, f32[192,768]{1,0:T(8,128)S(1)}, u32[]{:S(2)}, u32[]{:S(2)}) collective-permute-start(f32[192,768]{1,0:T(8,128)S(1)} %collective-permute-done.5), channel_id=1, source_target_pairs={{1,0},{2,3},{5,4},{6,7},{9,8},{10,11},{13,12},{14,15},{17,16},{18,... | collective-permute-start | bytes 1769480 | tf_op jit(solution)/shard_map/ppermute | solution.py:944
  70.9 21.9 %collective-permute-start.14 = (f32[320,768]{1,0:T(8,128)S(1)}, f32[320,768]{1,0:T(8,128)S(1)}, u32[]{:S(2)}, u32[]{:S(2)}) collective-permute-start(f32[320,768]{1,0:T(8,128)S(1)} %pad_maximum_fusion), channel_id=1, source_target_pairs={{0,1},{1,0},{2,3},{3,2},{4,5},{5,4},{6,7},{7,6},{8,9},{9,8},{10,11... | collective-permute-start | bytes 2949128 | tf_op jit(solution)/shard_map/ppermute | solution.py:525
  74.6 15.8 %collective-permute-start.12 = (f32[2,96,768]{2,1,0:T(8,128)}, f32[2,96,768]{2,1,0:T(8,128)}, u32[]{:S(2)}, u32[]{:S(2)}) collective-permute-start(f32[2,96,768]{2,1,0:T(8,128)} %pad_maximum_fusion.8.u0_ref), channel_id=1, source_target_pairs={{0,16},{4,20},{8,24},{12,28},{16,0},{20,4},{24,8},{28,12},{1,17},{... | collective-permute-start | bytes 1769480 | tf_op jit(solution)/shard_map/ppermute | solution.py:529
  76.0 15.5 %collective-permute-start.13 = (f32[2,96,768]{2,1,0:T(8,128)}, f32[2,96,768]{2,1,0:T(8,128)}, u32[]{:S(2)}, u32[]{:S(2)}) collective-permute-start(f32[2,96,768]{2,1,0:T(8,128)} %pad_maximum_fusion.9.d0_ref), channel_id=1, source_target_pairs={{0,8},{4,12},{8,0},{12,4},{16,24},{20,28},{24,16},{28,20},{1,9},{5... | collective-permute-start | bytes 1769480 | tf_op jit(solution)/shard_map/ppermute | solution.py:529
  94.4 17.2 %collective-permute-start.17 = (f32[192,768]{1,0:T(8,128)S(1)}, f32[192,768]{1,0:T(8,128)S(1)}, u32[]{:S(2)}, u32[]{:S(2)}) collective-permute-start(f32[192,768]{1,0:T(8,128)S(1)} %pad_maximum_fusion.10), channel_id=1, source_target_pairs={{0,8},{4,12},{8,0},{12,4},{16,24},{20,28},{24,16},{28,20},{1,9},{5... | collective-permute-start | bytes 1769480 | tf_op jit(solution)/shard_map/ppermute | solution.py:529
  95.1 16.6 %collective-permute-start.18 = (f32[192,768]{1,0:T(8,128)S(1)}, f32[192,768]{1,0:T(8,128)S(1)}, u32[]{:S(2)}, u32[]{:S(2)}) collective-permute-start(f32[192,768]{1,0:T(8,128)S(1)} %pad_maximum_fusion.11), channel_id=1, source_target_pairs={{0,16},{4,20},{8,24},{12,28},{16,0},{20,4},{24,8},{28,12},{1,17},{... | collective-permute-start | bytes 1769480 | tf_op jit(solution)/shard_map/ppermute | solution.py:529
  111.9 15.8 %collective-permute-start.21 = (f32[2,96,768]{2,1,0:T(8,128)S(1)}, f32[2,96,768]{2,1,0:T(8,128)S(1)}, u32[]{:S(2)}, u32[]{:S(2)}) collective-permute-start(f32[2,96,768]{2,1,0:T(8,128)S(1)} %pad_maximum_fusion.12.u0_ref), channel_id=1, source_target_pairs={{0,16},{4,20},{8,24},{12,28},{16,0},{20,4},{24,8},{28,12},{1,17},{... | collective-permute-start | bytes 1769480 | tf_op jit(solution)/shard_map/ppermute | solution.py:529
  112.8 15.7 %collective-permute-start.22 = (f32[2,96,768]{2,1,0:T(8,128)S(1)}, f32[2,96,768]{2,1,0:T(8,128)S(1)}, u32[]{:S(2)}, u32[]{:S(2)}) collective-permute-start(f32[2,96,768]{2,1,0:T(8,128)S(1)} %pad_maximum_fusion.13.d0_ref), channel_id=1, source_target_pairs={{0,8},{4,12},{8,0},{12,4},{16,24},{20,28},{24,16},{28,20},{1,9},{5... | collective-permute-start | bytes 1769480 | tf_op jit(solution)/shard_map/ppermute | solution.py:529
  128.6 14.9 %collective-permute-start.23 = (f32[2,96,768]{2,1,0:T(8,128)S(1)}, f32[2,96,768]{2,1,0:T(8,128)S(1)}, u32[]{:S(2)}, u32[]{:S(2)}) collective-permute-start(f32[2,96,768]{2,1,0:T(8,128)S(1)} %pad_maximum_fusion.14.u0_ref), channel_id=1, source_target_pairs={{0,16},{4,20},{8,24},{12,28},{16,0},{20,4},{24,8},{28,12},{1,17},{... | collective-permute-start | bytes 1769480 | tf_op jit(solution)/shard_map/ppermute | solution.py:529
  129.8 14.4 %collective-permute-start.24 = (f32[2,96,768]{2,1,0:T(8,128)S(1)}, f32[2,96,768]{2,1,0:T(8,128)S(1)}, u32[]{:S(2)}, u32[]{:S(2)}) collective-permute-start(f32[2,96,768]{2,1,0:T(8,128)S(1)} %pad_maximum_fusion.15.d0_ref), channel_id=1, source_target_pairs={{0,8},{4,12},{8,0},{12,4},{16,24},{20,28},{24,16},{28,20},{1,9},{5... | collective-permute-start | bytes 1769480 | tf_op jit(solution)/shard_map/ppermute | solution.py:529
  186.2 18.8 %collective-permute-start.35 = (f32[2,512,768]{2,1,0:T(8,128)}, f32[2,512,768]{2,1,0:T(8,128)S(1)}, u32[]{:S(2)}, u32[]{:S(2)}) collective-permute-start(f32[2,512,768]{2,1,0:T(8,128)} %shard_map.314), channel_id=1, source_target_pairs={{0,4},{4,0},{8,12},{12,8},{16,20},{20,16},{24,28},{28,24},{1,5},{5... | collective-permute-start | bytes 9437192 | tf_op jit(solution)/shard_map/ppermute | solution.py:529
  186.2 15.7 %collective-permute-start.36 = (f32[192,768]{1,0:T(8,128)S(1)}, f32[192,768]{1,0:T(8,128)S(1)}, u32[]{:S(2)}, u32[]{:S(2)}) collective-permute-start(f32[192,768]{1,0:T(8,128)S(1)} %pad_maximum_fusion.16), channel_id=1, source_target_pairs={{0,1},{1,0},{2,3},{3,2},{4,5},{5,4},{6,7},{7,6},{8,9},{9,8},{10,11... | collective-permute-start | bytes 1769480 | tf_op jit(solution)/shard_map/ppermute | solution.py:525
  187.8 15.8 %collective-permute-start.37 = (f32[192,768]{1,0:T(8,128)}, f32[192,768]{1,0:T(8,128)}, u32[]{:S(2)}, u32[]{:S(2)}) collective-permute-start(f32[192,768]{1,0:T(8,128)} %get-tuple-element.1198), channel_id=1, source_target_pairs={{0,16},{4,20},{8,24},{12,28},{16,0},{20,4},{24,8},{28,12},{1,17},{... | collective-permute-start | bytes 1769480 | tf_op jit(solution)/shard_map/ppermute | solution.py:529
  189.5 15.5 %collective-permute-start.38 = (f32[192,768]{1,0:T(8,128)}, f32[192,768]{1,0:T(8,128)}, u32[]{:S(2)}, u32[]{:S(2)}) collective-permute-start(f32[192,768]{1,0:T(8,128)} %get-tuple-element.1202), channel_id=1, source_target_pairs={{0,8},{4,12},{8,0},{12,4},{16,24},{20,28},{24,16},{28,20},{1,9},{5... | collective-permute-start | bytes 1769480 | tf_op jit(solution)/shard_map/ppermute | solution.py:529
  229.7 20.4 %collective-permute-start.45 = (f32[192,512]{1,0:T(8,128)S(1)}, f32[192,512]{1,0:T(8,128)S(1)}, u32[]{:S(2)}, u32[]{:S(2)}) collective-permute-start(f32[192,512]{1,0:T(8,128)S(1)} %copy-done.72), channel_id=1, source_target_pairs={{0,1},{1,0},{2,3},{3,2},{4,5},{5,4},{6,7},{7,6},{8,9},{9,8},{10,11... | collective-permute-start | bytes 1179656 | tf_op jit(solution)/shard_map/ppermute | solution.py:525
  230.3 20.5 %collective-permute-start.48 = (f32[128,768]{1,0:T(8,128)S(1)}, f32[128,768]{1,0:T(8,128)S(1)}, u32[]{:S(2)}, u32[]{:S(2)}) collective-permute-start(f32[128,768]{1,0:T(8,128)S(1)} %pad_maximum_fusion.19), channel_id=1, source_target_pairs={{0,2},{1,3},{2,0},{3,1},{4,6},{5,7},{6,4},{7,5},{8,10},{9,11},{10,... | collective-permute-start | bytes 1179656 | tf_op jit(solution)/shard_map/ppermute | solution.py:525
  232.7 18.1 %collective-permute-start.47 = (f32[2,96,768]{2,1,0:T(8,128)S(1)}, f32[2,96,768]{2,1,0:T(8,128)S(1)}, u32[]{:S(2)}, u32[]{:S(2)}) collective-permute-start(f32[2,96,768]{2,1,0:T(8,128)S(1)} %get-tuple-element.1491), channel_id=1, source_target_pairs={{0,8},{4,12},{8,0},{12,4},{16,24},{20,28},{24,16},{28,20},{1,9},{5... | collective-permute-start | bytes 1769480 | tf_op jit(solution)/shard_map/ppermute | solution.py:529
  254.1 19.1 %collective-permute-start.50 = (f32[240,768]{1,0:T(8,128)S(1)}, f32[240,768]{1,0:T(8,128)S(1)}, u32[]{:S(2)}, u32[]{:S(2)}) collective-permute-start(f32[240,768]{1,0:T(8,128)S(1)} %pad_maximum_fusion.7), channel_id=1, source_target_pairs={{0,8},{4,12},{8,0},{12,4},{16,24},{20,28},{24,16},{28,20},{1,9},{5... | collective-permute-start | bytes 2211848 | tf_op jit(solution)/shard_map/ppermute | solution.py:529
  255.2 18.0 %collective-permute-start.51 = (f32[192,768]{1,0:T(8,128)S(1)}, f32[192,768]{1,0:T(8,128)S(1)}, u32[]{:S(2)}, u32[]{:S(2)}) collective-permute-start(f32[192,768]{1,0:T(8,128)S(1)} %pad_maximum_fusion.17), channel_id=1, source_target_pairs={{0,16},{4,20},{8,24},{12,28},{16,0},{20,4},{24,8},{28,12},{1,17},{... | collective-permute-start | bytes 1769480 | tf_op jit(solution)/shard_map/ppermute | solution.py:529
  275.3 22.7 %collective-permute-start.52 = (f32[304,768]{1,0:T(8,128)S(1)}, f32[304,768]{1,0:T(8,128)S(1)}, u32[]{:S(2)}, u32[]{:S(2)}) collective-permute-start(f32[304,768]{1,0:T(8,128)S(1)} %pad_maximum_fusion.1), channel_id=1, source_target_pairs={{0,1},{1,0},{2,3},{3,2},{4,5},{5,4},{6,7},{7,6},{8,9},{9,8},{10,11... | collective-permute-start | bytes 2801672 | tf_op jit(solution)/shard_map/ppermute | solution.py:525
  277.4 20.6 %collective-permute-start.55 = (f32[4,72,768]{2,1,0:T(8,128)S(1)}, f32[4,72,768]{2,1,0:T(8,128)S(1)}, u32[]{:S(2)}, u32[]{:S(2)}) collective-permute-start(f32[4,72,768]{2,1,0:T(8,128)S(1)} %copy-done.58), channel_id=1, source_target_pairs={{0,4},{4,0},{8,12},{12,8},{16,20},{20,16},{24,28},{28,24},{1,5},{5... | collective-permute-start | bytes 2654216 | tf_op jit(solution)/shard_map/ppermute | solution.py:529
  277.6 20.5 %collective-permute-start.54 = (f32[264,768]{1,0:T(8,128)S(1)}, f32[264,768]{1,0:T(8,128)S(1)}, u32[]{:S(2)}, u32[]{:S(2)}) collective-permute-start(f32[264,768]{1,0:T(8,128)S(1)} %pad_maximum_fusion.4.a_ref), channel_id=1, source_target_pairs={{0,16},{4,20},{8,24},{12,28},{16,0},{20,4},{24,8},{28,12},{1,17},{... | collective-permute-start | bytes 2433032 | tf_op jit(solution)/shard_map/ppermute | solution.py:529
  278.9 15.5 %collective-permute-start.53 = (f32[192,768]{1,0:T(8,128)S(1)}, f32[192,768]{1,0:T(8,128)S(1)}, u32[]{:S(2)}, u32[]{:S(2)}) collective-permute-start(f32[192,768]{1,0:T(8,128)S(1)} %pad_maximum_fusion.18.a_ref), channel_id=1, source_target_pairs={{0,8},{4,12},{8,0},{12,4},{16,24},{20,28},{24,16},{28,20},{1,9},{5... | collective-permute-start | bytes 1769480 | tf_op jit(solution)/shard_map/ppermute | solution.py:529
  298.2 17.5 %collective-permute-start.57 = (f32[2,72,768]{2,1,0:T(8,128)S(1)}, f32[2,72,768]{2,1,0:T(8,128)S(1)}, u32[]{:S(2)}, u32[]{:S(2)}) collective-permute-start(f32[2,72,768]{2,1,0:T(8,128)S(1)} %get-tuple-element.1493), channel_id=1, source_target_pairs={{0,8},{4,12},{8,0},{12,4},{16,24},{20,28},{24,16},{28,20},{1,9},{5... | collective-permute-start | bytes 1327112 | tf_op jit(solution)/shard_map/ppermute | solution.py:529
  299.6 16.2 %collective-permute-start.60 = (f32[96,768]{1,0:T(8,128)S(1)}, f32[96,768]{1,0:T(8,128)S(1)}, u32[]{:S(2)}, u32[]{:S(2)}) collective-permute-start(f32[96,768]{1,0:T(8,128)S(1)} %pad_maximum_fusion.20), channel_id=1, source_target_pairs={{0,2},{1,3},{2,0},{3,1},{4,6},{5,7},{6,4},{7,5},{8,10},{9,11},{10,... | collective-permute-start | bytes 884744 | tf_op jit(solution)/shard_map/ppermute | solution.py:525
  329.5 14.8 %collective-permute-start.71 = (f32[96,768]{1,0:T(8,128)S(1)}, f32[96,768]{1,0:T(8,128)S(1)}, u32[]{:S(2)}, u32[]{:S(2)}) collective-permute-start(f32[96,768]{1,0:T(8,128)S(1)} %maximum_add_fusion.1), channel_id=1, source_target_pairs={{0,16},{4,20},{8,24},{12,28},{16,0},{20,4},{24,8},{28,12},{1,17},{... | collective-permute-start | bytes 884744 | tf_op jit(solution)/shard_map/ppermute | solution.py:529
  (122 other events, 1051.8 us)

commit v2 on v1

--- a/solution.py
+++ b/solution.py
@@ -20,7 +20,8 @@
 BITS_A = (2, 4, 1)
 BITS_B = (4, 2, 1)
 MLP_KIND = ("a", "a", "b", "b")
-VMEM_LIMIT = 56 * 1024 * 1024
+VMEM_LIMIT = 26 * 1024 * 1024
+VMEM_LARGE = 56 * 1024 * 1024
 
 
 def mm(a, b):
@@ -35,11 +36,11 @@
     return lax.dot_general(a, b, (((0,), (0,)), ((), ())), preferred_element_type=F32)
 
 
-def call(kernel, out_shape, flops=0, bytes_accessed=0, **kw):
+def call(kernel, out_shape, flops=0, bytes_accessed=0, vmem_limit=VMEM_LIMIT, **kw):
     return pl.pallas_call(
         kernel,
         out_shape=out_shape,
-        compiler_params=pltpu.CompilerParams(vmem_limit_bytes=VMEM_LIMIT),
+        compiler_params=pltpu.CompilerParams(vmem_limit_bytes=vmem_limit),
         cost_estimate=pl.CostEstimate(
             flops=flops, bytes_accessed=bytes_accessed, transcendentals=0
         ),
@@ -361,13 +362,14 @@
 
 
 def attn_bwd_kernel(
-    first, idx_ref, x_ref, qpre_ref, kpre_ref, vt_ref, wt_ref, gmt_ref, gmtp_ref, mixf_ref, l_ref,
+    ncuts, idx_ref, x_ref, qpre_ref, kpre_ref, vt_ref, wt_ref, gmt_ref, gmtp_ref, mixf_ref, l_ref,
     hv_ref, kmask_ref, qhot_ref, *refs
 ):
-    if first:
-        gk_ref, gs_ref, gn_ref, st_ref, gb_ref, qaug_ref, kaug_ref, gpt_ref = refs
+    if ncuts:
+        gn_in, gk_ref, gs_ref, *gn_refs = refs[: 3 + ncuts]
     else:
-        gn_in, gk_ref, gs_ref, gn_ref, st_ref, gb_ref, qaug_ref, kaug_ref, gpt_ref = refs
+        gk_ref, gs_ref, gn_ref = refs[:3]
+    st_ref, gb_ref, qaug_ref, kaug_ref, gpt_ref = refs[-5:]
     part = 24
     e = PIECES * part
     full = x_ref.shape[0]
@@ -432,19 +434,24 @@
             put(gs_ref, at - PIECES // 2, p)
 
     gn = mm_tn(gp, wt_ref[...])
-    gn_ref[...] = gn if first else gn_in[...] + gn
+    if not ncuts:
+        gn_ref[...] = gn
+    else:
+        at = 0
+        for ref in gn_refs:
+            rows = slice(at, at + ref.shape[0])
+            ref[...] = gn_in[rows, :] + gn[rows]
+            at += ref.shape[0]
 
 
 def sums_kernel(
-    nslot, blk_ref, me_ref, x_ref, gn_ref, mst_ref, h0_ref, h2_ref, b0_ref, b2_ref, *refs
+    nslot, blk_ref, me_ref, x_ref, xf_ref, gn_ref, mst_ref, h0_ref, h2_ref, b0_ref, b2_ref, *refs
 ):
     ubs = refs[:nslot]
-    out_ref = refs[nslot]
-    n, _ = row_norm(x_ref[...].astype(F32))
-    e = gn_ref[...]
-
-    @pl.when(pl.program_id(0) == 0)
-    def _():
+    fars = refs[nslot:-1]
+    out_ref = refs[-1]
+
+    def fill():
         out_ref[...] = jnp.zeros_like(out_ref)
         out_ref[0:4, :] = mst_ref[0:4, :]
         heads = jnp.concatenate([h0_ref[i] + h2_ref[i] for i in range(3)], axis=0).T
@@ -463,8 +470,18 @@
                     piece = piece + jnp.where(here, mine[:, t * upart : (t + 1) * upart], 0.0)
                 out_ref[row + 1 : row + 2, p * upart : (p + 1) * upart] = piece
 
-    out_ref[4:5, :] += jnp.sum(e * n, axis=0, keepdims=True)
-    out_ref[5:6, :] += jnp.sum(e, axis=0, keepdims=True)
+    fill()
+
+    def add(x, e):
+        n, _ = row_norm(x.astype(F32))
+        out_ref[4:5, :] += jnp.sum(e * n, axis=0, keepdims=True)
+        out_ref[5:6, :] += jnp.sum(e, axis=0, keepdims=True)
+
+    add(x_ref[...], gn_ref[...])
+    at = 0
+    for ref in fars:
+        add(xf_ref[at : at + ref.shape[0], :], ref[...])
+        at += ref.shape[0]
 
 
 def small_out_kernel(a_ref, b_ref, qb_ref, h0_ref, h1_ref, h2_ref, *rows):
@@ -610,6 +627,7 @@
             *[sds((2, upart, width), BF16)] * 4,
         ),
         bytes_accessed=9_000_000,
+        vmem_limit=VMEM_LARGE,
         in_specs=[smem] + [vmem] * 6,
         out_specs=(vmem,) * 8,
         scratch_shapes=[pltpu.VMEM((units, width), F32), pltpu.VMEM((e, width), F32)],
@@ -617,7 +635,7 @@
         me1, qkv_t, out_weight, qkv_bias, up_bias, up_weight, down_weight
     )
 
-    n_gn = (256, 88, 80, 88)
+    n_gn = (256, 112, 144)
     n_z2 = 64
     numbers = jnp.arange(PIECES, dtype=jnp.int32)
     idx_a = storage_of(numbers ^ me, BITS_A).astype(jnp.int32)
@@ -836,28 +854,29 @@
             idx, v["normed"], st["qpre"], st["kpre"], st["vt"], st["wt"], v.pop(f"gmt{k}"),
             v.pop(got), st["mixf"], st["l"], hv, kmask, qhot,
         ]
-        alias = {}
+        cuts_now = (full,) if first else (share, *n_gn)
         if not first:
-            args.append(v["gn"])
-            alias = {len(args) - 1: 2}
-        keep, send, gn, hst, gb = call(
-            functools.partial(attn_bwd_kernel, first),
+            args.append(v.pop("gn"))
+        keep, send, *gn, hst, gb = call(
+            functools.partial(attn_bwd_kernel, 0 if first else len(cuts_now)),
             (
                 sds((half, 3 * part, width), F32),
                 sds((half, 3 * part, width), F32),
-                sds((full, width), F32),
+                *[sds((n, width), F32) for n in cuts_now],
                 sds((3, DH, 128), F32),
                 sds((3 * e, 128), F32),
             ),
             flops=2 * (full * width * e * 6 + full * full * e * 20),
             bytes_accessed=14_000_000,
             in_specs=[smem] + [vmem] * (len(args) - 1),
-            out_specs=(vmem,) * 5,
+            out_specs=(vmem,) * (4 + len(cuts_now)),
             scratch_shapes=scratch + [pltpu.VMEM((3 * e, full), BF16)],
-            input_output_aliases=alias,
         )(*args)
         v[f"q{k}"] = (keep, send)
-        v["gn"] = gn
+        if first:
+            v["gn"] = gn[0]
+        else:
+            v["gn_own"], v["gn_far"] = gn[0], tuple(gn[1:])
         v[f"hst{k}"] = hst
         v[f"qbg{k}"] = gb
 
@@ -1086,9 +1105,8 @@
     to_x = jnp.concatenate([ya[nmp * part :], yb[nmp * part :]], axis=0)
     v["gx"], v["gy"] = (to_x, swap(to_x, px)), (to_y, swap(to_y, py))
     o = v.pop("o") + yb[: nmp * part]
-    v["gn0"] = zswap(
-        jnp.concatenate([v["gn"][share : share + n_gn[0]], o[part : 2 * part], o[3 * part :]], axis=0), 1
-    )
+    v["gn0"] = zswap(v["gn_far"][0], 1)
+    v["oz"] = zswap(jnp.concatenate([o[part : 2 * part], o[3 * part :]], axis=0), 1)
     v["o0"], v["o2"] = o[:part], o[2 * part : 3 * part]
     v["small"] = call(
         functools.partial(sums_kernel, nmp),
@@ -1097,53 +1115,41 @@
         bytes_accessed=full * width * 6,
         grid_spec=pltpu.PrefetchScalarGridSpec(
             num_scalar_prefetch=2,
-            grid=(steps,),
+            grid=(1,),
             in_specs=[
-                pl.BlockSpec((block, width), lambda t, b, m: (b[t], 0)),
-                pl.BlockSpec((block, width), lambda t, b, m: (t, 0)),
+                pl.BlockSpec((share, width), lambda t, b, m: (b[0] // per, 0)),
+                pl.BlockSpec((share, width), lambda t, b, m: (b[per] // per, 0)),
+                pl.BlockSpec((share, width), lambda t, b, m: (0, 0)),
                 pl.BlockSpec((8, width), lambda t, b, m: (0, 0)),
                 *[pl.BlockSpec((3, DH, 128), lambda t, b, m: (0, 0, 0))] * 2,
                 *[pl.BlockSpec((3 * e, 128), lambda t, b, m: (0, 0))] * 2,
                 *[pl.BlockSpec((1, mine), lambda t, b, m: (0, 0))] * nmp,
+                *[pl.BlockSpec((n, width), lambda t, b, m: (0, 0)) for n in n_gn],
             ],
             out_specs=pl.BlockSpec((16, width), lambda t, b, m: (0, 0)),
         ),
     )(
-        blk, me1, tokens, v["gn"], v.pop("mst"), v.pop("hst0"), v.pop("hst2"), v.pop("qbg0"),
-        v.pop("qbg2"), *[v.pop(f"ubg{k}") for k in range(nmp)],
+        blk, me1, tokens, tokens, v["gn_own"], v.pop("mst"), v.pop("hst0"), v.pop("hst2"),
+        v.pop("qbg0"), v.pop("qbg2"), *[v.pop(f"ubg{k}") for k in range(nmp)], *v["gn_far"],
     )
+    v["small"] = v["small"] + swap(v["small"], core)
     v.fence()
     r2("q0", "b")
     (xa, xb), (ya, yb) = v["gx"], v["gy"]
-    gn0 = v.pop("gn0")
-    v["gn0"] = gn0
-    v["o0"] = v["o0"] + gn0[n_gn[0] : n_gn[0] + part]
-    o2 = v.pop("o2") + gn0[n_gn[0] + part :]
+    oz = v.pop("oz")
+    v["o0"] = v["o0"] + oz[:part]
     q2 = v.pop("q2") + yb[2 * upart :]
-    v["y2"] = zswap(jnp.concatenate([q2, o2], axis=0), 2)
-    at = share + n_gn[0]
-    v["gn1"] = zswap(v["gn"][at : at + n_gn[1]], 1)
-    small = v["small"] + swap(v["small"], core)
-    v["small"] = small + swap(small, px)
+    v["y2"] = zswap(jnp.concatenate([q2, v.pop("o2") + oz[part:]], axis=0), 2)
+    v["gn1"] = zswap(v["gn_far"][1], 1)
+    v["gu"] = (ya, yb, swap(ya, core), swap(yb, core))
+    v.pop("gy")
     v.fence()
     r3("q0", "b")
-    at = share + n_gn[0] + n_gn[1]
-    v["gn2"] = zswap(v["gn"][at : at + n_gn[2]], 1)
-    v["small"] = v["small"] + swap(v["small"], py)
-    ya, yb = v.pop("gy")
-    v["gu"] = (ya, yb, swap(ya, core), swap(yb, core))
-    v.fence()
-    r4("q0")
-    att_sum = high_bits(
-        jnp.concatenate([v.pop("q0"), v.pop("o0")], axis=0) + v.pop("y2")
-    )
-    v["w"] = (att_sum, swap(att_sum, px), swap(att_sum, py), swap(att_sum, px | py))
+    v["gn2"] = zswap(v.pop("gn_far")[2], 1)
+    small = v["small"] + swap(v["small"], px)
+    v["small"] = small + swap(small, py)
     xa, xb = v.pop("gx")
-    gd = (xa, xb, swap(xa, core), swap(xb, core))
-    small = high_bits(v.pop("small"))
-    got = zswap(jnp.concatenate([small[:8], small[12:]], axis=0), 1)
-    v["small"] = small[:12] + got
-
+    v["gd"] = (xa, xb, swap(xa, core), swap(xb, core))
     def unpack(kernel, arrays, idx, shape):
         pieces_spec = pl.BlockSpec((2 * upart, width), lambda t: (0, 0))
         return call(
@@ -1157,10 +1163,18 @@
         )(idx, *arrays)
 
     v["up_g"] = unpack(unpack_kernel, v.pop("gu"), idx_a, (width, units))
-    v["down_g"] = unpack(unpack_rows_kernel, gd, idx_b, (units, width))
-    v["gn3"] = zswap(v["gn"][full - n_gn[3] :], 1)
-    v.fence()
-    input_grad = call(
+    v.fence()
+    r4("q0")
+    att_sum = high_bits(
+        jnp.concatenate([v.pop("q0"), v.pop("o0")], axis=0) + v.pop("y2")
+    )
+    v["w"] = (att_sum, swap(att_sum, px), swap(att_sum, py), swap(att_sum, px | py))
+    small = high_bits(v.pop("small"))
+    got = zswap(jnp.concatenate([small[:8], small[12:]], axis=0), 1)
+    v["small"] = small[:12] + got
+
+    v["down_g"] = unpack(unpack_rows_kernel, v.pop("gd"), idx_b, (units, width))
+    v["input_grad"] = call(
         final_kernel,
         sds((share, width), BF16),
         flops=share * width * 20,
@@ -1177,7 +1191,8 @@
             ],
             out_specs=pl.BlockSpec((share, width), const2),
         ),
-    )(blk, tokens, v["gn"], *[v[f"gn{i}"] for i in range(4)], v["gm"], row1(norm1_gain))
+    )(blk, tokens, v["gn_own"], *[v[f"gn{i}"] for i in range(3)], v["gm"], row1(norm1_gain))
+    v.fence()
     w = jnp.concatenate(v.pop("w"), axis=0)
     small = v.pop("small")
     small_got = zswap(jnp.concatenate([small[:8], small[10:]], axis=0), 2)
@@ -1200,7 +1215,7 @@
     heads_of, rows_of = rows_of[:3], rows_of[3:]
     return (
         v["block_out"],
-        input_grad,
+        v["input_grad"],
         qkv_weight_grad,
         qkv_bias_grad,
         out_weight_grad,

time: 361 us -> 347 us (0.961)
  Pallas kernels: 147 us -> 89.4 us
  waiting for transfers between devices: 105 us -> 158 us
  local copies, waits for them, and re-layouts: 20 us -> 11.6 us
    ppermute x22, waiting for transfers between devices: 39.2 us -> 92.1 us  [swap_mp(): return lax.ppermute(a, 'mp', [(s, s ^ k) for s in range(size)])]
    pallas_call x4, Pallas kernels: 30.4 us -> 19.1 us  [run_mlp(): call(functools.partial(mlp_kernel, MLP_KIND[k], keeps), shapes, flops=2 *...]
    pallas_call x2, Pallas kernels: 15.1 us -> 5.22 us  [run_down(): call(functools.partial(down_kernel, nmp), sds((2, share, width), F32), fl...]
    pallas_call x2, Pallas kernels: 33.2 us -> 24.4 us  [run_attn_bwd(): call(functools.partial(attn_bwd_kernel, 0 if first else len(cuts_now)), (...]
    pallas_call x1, Pallas kernels: 7.51 us -> 3.05 us  [run_mid(): call(functools.partial(mid_kernel, nmp), shapes, flops=2 * share * width...]
    slice x5 -> x1, local copies, waits for them, and re-layouts: 4.11 us -> 0.02 us  [shards(): o[part:2 * part]]
    unnamed x155 -> x165, local copies, waits for them, and re-layouts: 9.35 us -> 7.91 us
  transfers between devices with their start and end apart: 75 -> 75, of which waited for: 37 -> 48; matrix products, arithmetic and copies ran while one was open for 6% -> 3% of each run, Pallas kernels for 39% -> 24%
where the time goes in v2:
time: 347 us; the launch traced here: 344 us
  waiting for transfers between devices  158 us (46%)
  Pallas kernels  89.4 us (26%)
  starting transfers between devices  70.8 us (20%)
  other arithmetic  11.8 us (3%)
  local copies, waits for them, and re-layouts  11.6 us (3%)
    ppermute x22, waiting for transfers between devices, swap_mp(): return lax.ppermute(a, 'mp', [(s, s ^ k) for s in range(size)])  92.1 us
    ppermute x50, waiting for transfers between devices, swap_plane(): return lax.ppermute(a, 'dp', [(d, d ^ bit) for d in range(size)])  52 us
    ppermute x50, starting transfers between devices, swap_plane(): return lax.ppermute(a, 'dp', [(d, d ^ bit) for d in range(size)])  40.9 us
    ppermute x22, starting transfers between devices, swap_mp(): return lax.ppermute(a, 'mp', [(s, s ^ k) for s in range(size)])  26.9 us
    pallas_call x2, Pallas kernels, run_attn_bwd(): call(functools.partial(attn_bwd_kernel, 0 if first else len(cuts_now)), (...  24.4 us
    pallas_call x4, Pallas kernels, run_mlp(): call(functools.partial(mlp_kernel, MLP_KIND[k], keeps), shapes, flops=2 *...  19.1 us
    ppermute x1, waiting for transfers between devices, pass_out(): return lax.ppermute(a, 'mp', [(1, 0), (2, 3)])  13.5 us
    unnamed x165, local copies, waits for them, and re-layouts  7.91 us
  transfers between devices with their start and end apart: 75, of which 48 were waited for; matrix products, arithmetic and copies ran while one was open for 3% of the time, Pallas kernels for 24%

profile of v2, /device:TPU:0, one launch (start us, length us, event | category | flops | bytes accessed | tf_op | source)
XLA Modules:
  0.0 343.7 jit_solution(16912730593774621623)
XLA Ops:
  0.7 4.2 %shard_map.305 = (f32[104,768]{1,0:T(8,128)}, f32[32,768]{1,0:T(8,128)}, f32[8,768]{1,0:T(8,128)}, f32[192,768]{1,0:T(8,128)}, bf16[2,96,768]{2,1,0:T(8,128)(2,1...) custom-call(s32[1]{0:T(128)} %bitcast.me_ref, ...), custom_call_target="tpu_custom_call" | custom-call | bytes 9000000 | tf_op jit(solution)/shard_map/pallas_call | solution.py:620
  4.9 4.0 %collective-permute-start.2 = (f32[104,768]{1,0:T(8,128)}, f32[104,768]{1,0:T(8,128)S(1)}, u32[]{:S(2)}, u32[]{:S(2)}) collective-permute-start(f32[104,768]{1,0:T(8,128)} %get-tuple-element.765), channel_id=1, source_target_pairs={{0,2},{1,3},{2,0},{3,1},{4,6},{5,7},{6,4},{7,5},{8,10},{9,11},{10,... | collective-permute-start | bytes 958472 | tf_op jit(solution)/shard_map/ppermute | solution.py:542
  12.4 3.3 fusion.7
  15.7 3.5 %collective-permute-done.b_ref = f32[32,768]{1,0:T(8,128)} collective-permute-done((f32[32,768]{1,0:T(8,128)}, f32[32,768]{1,0:T(8,128)}, u32[]{:S(2)}, u32[]{:S(2)}) %collective-permute-start) | collective-permute-done | bytes 98336 | tf_op jit(solution)/shard_map/ppermute | solution.py:542
  19.2 2.9 collective-permute-done.1.b_ref
  22.1 4.3 %collective-permute-done.2.b_ref = f32[104,768]{1,0:T(8,128)S(1)} collective-permute-done((f32[104,768]{1,0:T(8,128)}, f32[104,768]{1,0:T(8,128)S(1)}, u32[]{:S(2)}, u32[]{:S(2)}) %collective-permute-start.2) | collective-permute-done | bytes 319520 | tf_op jit(solution)/shard_map/ppermute | solution.py:542
  34.5 3.5 %collective-permute-done.6 = f32[72,768]{1,0:T(8,128)S(1)} collective-permute-done((f32[72,768]{1,0:T(8,128)S(1)}, f32[72,768]{1,0:T(8,128)S(1)}, u32[]{:S(2)}, u32[]{:S(2)}) %collective-permute-start.6) | collective-permute-done | bytes 221216 | tf_op jit(solution)/shard_map/ppermute | solution.py:546
  48.9 4.9 %shard_map.307 = (f32[192,1024]{1,0:T(8,128)S(1)}, f32[192,1024]{1,0:T(8,128)S(1)}, bf16[192,1024]{1,0:T(8,128)(2,1)S(1)}, bf16[192,512]{1,0:T(8,128)(2,1)S(1)},...) custom-call(bf16[1024,768]{1,0:T(8,128)(2,1)S(1)} %copy-done.4, ...), custom_call_target="tpu_custom_call" | custom-call | flops 4127195136 | bytes 10000000 | tf_op jit(solution)/shard_map/pallas_call | solution.py:704
  54.6 13.5 %collective-permute-done.8 = f32[192,768]{1,0:T(8,128)S(1)} collective-permute-done((f32[192,768]{1,0:T(8,128)S(1)}, f32[192,768]{1,0:T(8,128)S(1)}, u32[]{:S(2)}, u32[]{:S(2)}) %collective-permute-start.8) | collective-permute-done | bytes 589856 | tf_op jit(solution)/shard_map/ppermute | solution.py:963
  79.1 7.2 %shard_map.308 = (bf16[576,768]{1,0:T(8,128)(2,1)S(1)}, bf16[192,768]{1,0:T(8,128)(2,1)S(1)}, bf16[192,768]{1,0:T(8,128)(2,1)S(1)}, bf16[192,768]{1,0:T(8,128)(2...) custom-call(s32[8]{0:T(128)S(1)} %get-tuple-element.1555.ia_ref.idx_, ...), custom_call_target="tpu_custom_call" | custom-call | flops 4127195136 | bytes 10000000 | tf_op jit(solution)/shard_map/pallas_call | solution.py:724
  97.4 7.7 %collective-permute-done.19.refs_3_ = f32[128,768]{1,0:T(8,128)S(1)} collective-permute-done((f32[128,768]{1,0:T(8,128)S(1)}, f32[128,768]{1,0:T(8,128)S(1)}, u32[]{:S(2)}, u32[]{:S(2)}) %collective-permute-start.19) | collective-permute-done | bytes 393248 | tf_op jit(solution)/shard_map/ppermute | solution.py:542
  105.1 3.1 shard_map.309
  111.7 5.2 %shard_map.310 = (bf16[1024,384]{1,0:T(8,128)(2,1)S(1)}, bf16[1024,384]{1,0:T(8,128)(2,1)S(1)}, bf16[384,768]{1,0:T(8,128)(2,1)S(1)}, bf16[384,768]{1,0:T(8,128)...) custom-call(bf16[512,768]{1,0:T(8,128)(2,1)S(1)} %get-tuple-element., ...), custom_call_target="tpu_custom_call" | custom-call | flops 2415919104 | bytes 12000000 | tf_op jit(solution)/shard_map/pallas_call | solution.py:779
  117.0 7.3 %collective-permute-done.21.u1_ref = f32[2,96,768]{2,1,0:T(8,128)S(1)} collective-permute-done((f32[2,96,768]{2,1,0:T(8,128)S(1)}, f32[2,96,768]{2,1,0:T(8,128)S(1)}, u32[]{:S(2)}, u32[]{:S(2)}) %collective-permute-start.21) | collective-permute-done | bytes 589856 | tf_op jit(solution)/shard_map/ppermute | solution.py:546
  129.9 4.6 %shard_map.311 = (bf16[1024,384]{1,0:T(8,128)(2,1)S(1)}, bf16[1024,384]{1,0:T(8,128)(2,1)S(1)}, bf16[384,768]{1,0:T(8,128)(2,1)S(1)}, bf16[384,768]{1,0:T(8,128)...) custom-call(bf16[512,768]{1,0:T(8,128)(2,1)S(1)} %get-tuple-element., ...), custom_call_target="tpu_custom_call" | custom-call | flops 2415919104 | bytes 12000000 | tf_op jit(solution)/shard_map/pallas_call | solution.py:779
  134.5 6.0 %collective-permute-done.23.u1_ref = f32[2,96,768]{2,1,0:T(8,128)S(1)} collective-permute-done((f32[2,96,768]{2,1,0:T(8,128)S(1)}, f32[2,96,768]{2,1,0:T(8,128)S(1)}, u32[]{:S(2)}, u32[]{:S(2)}) %collective-permute-start.23) | collective-permute-done | bytes 589856 | tf_op jit(solution)/shard_map/ppermute | solution.py:546
  146.2 4.6 %shard_map.312 = (bf16[1024,384]{1,0:T(8,128)(2,1)S(1)}, bf16[1024,384]{1,0:T(8,128)(2,1)S(1)}, bf16[384,768]{1,0:T(8,128)(2,1)S(1)}, bf16[384,768]{1,0:T(8,128)...) custom-call(bf16[512,768]{1,0:T(8,128)(2,1)S(1)} %get-tuple-element., ...), custom_call_target="tpu_custom_call" | custom-call | flops 2415919104 | bytes 12000000 | tf_op jit(solution)/shard_map/pallas_call | solution.py:779
  150.8 4.7 %collective-permute-done.26.refs_0_ = f32[192,768]{1,0:T(8,128)S(1)} collective-permute-done((f32[192,768]{1,0:T(8,128)S(1)}, f32[192,768]{1,0:T(8,128)S(1)}, u32[]{:S(2)}, u32[]{:S(2)}) %collective-permute-start.26) | collective-permute-done | bytes 589856 | tf_op jit(solution)/shard_map/ppermute | solution.py:542
  160.2 4.7 %shard_map.313 = (bf16[1024,384]{1,0:T(8,128)(2,1)S(1)}, bf16[1024,384]{1,0:T(8,128)(2,1)S(1)}, bf16[384,768]{1,0:T(8,128)(2,1)S(1)}, bf16[384,768]{1,0:T(8,128)...) custom-call(bf16[512,768]{1,0:T(8,128)(2,1)S(1)} %get-tuple-element., ...), custom_call_target="tpu_custom_call" | custom-call | flops 2415919104 | bytes 12000000 | tf_op jit(solution)/shard_map/pallas_call | solution.py:779
  166.3 5.1 %collective-permute-done.29 = f32[192,768]{1,0:T(8,128)S(1)} collective-permute-done((f32[192,768]{1,0:T(8,128)S(1)}, f32[192,768]{1,0:T(8,128)S(1)}, u32[]{:S(2)}, u32[]{:S(2)}) %collective-permute-start.29) | collective-permute-done | bytes 589856 | tf_op jit(solution)/shard_map/ppermute | solution.py:542
  176.1 6.0 %collective-permute-done.32 = f32[192,768]{1,0:T(8,128)S(1)} collective-permute-done((f32[192,768]{1,0:T(8,128)S(1)}, f32[192,768]{1,0:T(8,128)S(1)}, u32[]{:S(2)}, u32[]{:S(2)}) %collective-permute-start.32) | collective-permute-done | bytes 589856 | tf_op jit(solution)/shard_map/ppermute | solution.py:542
  189.0 9.4 %collective-permute-done.36 = f32[192,768]{1,0:T(8,128)S(1)} collective-permute-done((f32[192,768]{1,0:T(8,128)S(1)}, f32[192,768]{1,0:T(8,128)S(1)}, u32[]{:S(2)}, u32[]{:S(2)}) %collective-permute-start.36) | collective-permute-done | bytes 589856 | tf_op jit(solution)/shard_map/ppermute | solution.py:542
  202.8 3.0 shard_map.316
  214.2 3.1 shard_map.317
  217.5 3.3 collective-permute-done.44
  226.9 12.3 %shard_map.318 = (f32[4,72,768]{2,1,0:T(8,128)S(1)}, f32[4,72,768]{2,1,0:T(8,128)S(1)}, f32[1024,768]{1,0:T(8,128)S(1)}, f32[3,64,128]{2,1,0:T(8,128)S(1)}, f32[576,128]{1,0:T(8,128)S(1)}) custom-call(s32[8]{0:T(128)S(1)} %get-tuple-element.1556.ib_ref.idx_ref, bf16[1024,768]{1,0:T(8,128)(2,1)S(1)} %copy-done.6, f32[192,1024]{1,0:T(8,128)S(1)} %copy-done.42, ...), custom_call_target="tpu_custom_call" | custom-call | flops 9865003008 | bytes 14000000 | tf_op jit(solution)/shard_map/pallas_call | solution.py:860
  249.8 12.1 %shard_map.319 = (f32[4,72,768]{2,1,0:T(8,128)S(1)}, f32[4,72,768]{2,1,0:T(8,128)S(1)}, f32[512,768]{1,0:T(8,128)S(1)}, f32[256,768]{1,0:T(8,128)S(1)}, f32[112,...) custom-call(s32[8]{0:T(128)S(1)} %get-tuple-element.1556.ib_ref.idx_ref, ...), custom_call_target="tpu_custom_call" | custom-call | flops 9865003008 | bytes 14000000 | tf_op jit(solution)/shard_map/pallas_call | solution.py:860
  274.8 13.1 %collective-permute-done.55 = f32[48,768]{1,0:T(8,128)S(1)} collective-permute-done((f32[48,768]{1,0:T(8,128)S(1)}, f32[48,768]{1,0:T(8,128)S(1)}, u32[]{:S(2)}, u32[]{:S(2)}) %collective-permute-start.55) | collective-permute-done | bytes 147488 | tf_op jit(solution)/shard_map/ppermute | solution.py:542
  292.4 13.5 %collective-permute-done.62 = f32[96,768]{1,0:T(8,128)S(1)} collective-permute-done((f32[96,768]{1,0:T(8,128)S(1)}, f32[96,768]{1,0:T(8,128)S(1)}, u32[]{:S(2)}, u32[]{:S(2)}) %collective-permute-start.62) | collective-permute-done | bytes 294944 | tf_op jit(solution)/shard_map/ppermute | solution.py:542
  308.8 3.3 collective-permute-done.67
  328.7 4.0 %collective-permute-done.71 = f32[96,768]{1,0:T(8,128)S(1)} collective-permute-done((f32[96,768]{1,0:T(8,128)S(1)}, f32[96,768]{1,0:T(8,128)S(1)}, u32[]{:S(2)}, u32[]{:S(2)}) %collective-permute-start.71) | collective-permute-done | bytes 294944 | tf_op jit(solution)/shard_map/ppermute | solution.py:546
  335.9 4.6 %collective-permute-done.74.b_ref = f32[10,768]{1,0:T(8,128)S(1)} collective-permute-done((f32[10,768]{1,0:T(8,128)S(1)}, f32[10,768]{1,0:T(8,128)S(1)}, u32[]{:S(2)}, u32[]{:S(2)}) %collective-permute-start.74) | collective-permute-done | bytes 30752 | tf_op jit(solution)/shard_map/ppermute | solution.py:542
  (406 shorter events, 149.2 us)
Async XLA Ops:
  4.9 21.6 %collective-permute-start.2 = (f32[104,768]{1,0:T(8,128)}, f32[104,768]{1,0:T(8,128)S(1)}, u32[]{:S(2)}, u32[]{:S(2)}) collective-permute-start(f32[104,768]{1,0:T(8,128)} %get-tuple-element.765), channel_id=1, source_target_pairs={{0,2},{1,3},{2,0},{3,1},{4,6},{5,7},{6,4},{7,5},{8,10},{9,11},{10,... | collective-permute-start | bytes 958472 | tf_op jit(solution)/shard_map/ppermute | solution.py:542
  26.4 16.5 %collective-permute-start.3 = (f32[512,768]{1,0:T(8,128)}, f32[512,768]{1,0:T(8,128)}, u32[]{:S(2)}, u32[]{:S(2)}) collective-permute-start(f32[512,768]{1,0:T(8,128)} %get-tuple-element.767), channel_id=1, source_target_pairs={{0,4},{4,0},{8,12},{12,8},{16,20},{20,16},{24,28},{28,24},{1,5},{5... | collective-permute-start | bytes 4718600 | tf_op jit(solution)/shard_map/ppermute | solution.py:546
  26.6 16.4 %collective-permute-start.4 = (f32[192,768]{1,0:T(8,128)}, f32[192,768]{1,0:T(8,128)S(1)}, u32[]{:S(2)}, u32[]{:S(2)}) collective-permute-start(f32[192,768]{1,0:T(8,128)} %get-tuple-element.768), channel_id=1, source_target_pairs={{0,1},{1,0},{2,3},{3,2},{4,5},{5,4},{6,7},{7,6},{8,9},{9,8},{10,11... | collective-permute-start | bytes 1769480 | tf_op jit(solution)/shard_map/ppermute | solution.py:542
  43.1 25.1 %collective-permute-start.10 = (f32[240,768]{1,0:T(8,128)S(1)}, f32[240,768]{1,0:T(8,128)S(1)}, u32[]{:S(2)}, u32[]{:S(2)}) collective-permute-start(f32[240,768]{1,0:T(8,128)S(1)} %pad_maximum_fusion.4), channel_id=1, source_target_pairs={{0,16},{4,20},{8,24},{12,28},{16,0},{20,4},{24,8},{28,12},{1,17},{... | collective-permute-start | bytes 2211848 | tf_op jit(solution)/shard_map/ppermute | solution.py:546
  44.7 23.4 %collective-permute-start.11 = (f32[240,768]{1,0:T(8,128)S(1)}, f32[240,768]{1,0:T(8,128)S(1)}, u32[]{:S(2)}, u32[]{:S(2)}) collective-permute-start(f32[240,768]{1,0:T(8,128)S(1)} %pad_maximum_fusion.5), channel_id=1, source_target_pairs={{0,8},{4,12},{8,0},{12,4},{16,24},{20,28},{24,16},{28,20},{1,9},{5... | collective-permute-start | bytes 2211848 | tf_op jit(solution)/shard_map/ppermute | solution.py:546
  46.5 21.7 %collective-permute-start.9 = (f32[192,768]{1,0:T(8,128)S(1)}, f32[192,768]{1,0:T(8,128)S(1)}, u32[]{:S(2)}, u32[]{:S(2)}) collective-permute-start(f32[192,768]{1,0:T(8,128)S(1)} %collective-permute-done.4), channel_id=1, source_target_pairs={{1,2},{2,1},{5,6},{6,5},{9,10},{10,9},{13,14},{14,13},{17,18},{18,... | collective-permute-start | bytes 1769480 | tf_op jit(solution)/shard_map/ppermute | solution.py:960
  47.2 20.9 %collective-permute-start.8 = (f32[192,768]{1,0:T(8,128)S(1)}, f32[192,768]{1,0:T(8,128)S(1)}, u32[]{:S(2)}, u32[]{:S(2)}) collective-permute-start(f32[192,768]{1,0:T(8,128)S(1)} %collective-permute-done.5), channel_id=1, source_target_pairs={{1,0},{2,3},{5,4},{6,7},{9,8},{10,11},{13,12},{14,15},{17,16},{18,... | collective-permute-start | bytes 1769480 | tf_op jit(solution)/shard_map/ppermute | solution.py:963
  69.3 22.2 %collective-permute-start.14 = (f32[320,768]{1,0:T(8,128)}, f32[320,768]{1,0:T(8,128)}, u32[]{:S(2)}, u32[]{:S(2)}) collective-permute-start(f32[320,768]{1,0:T(8,128)} %pad_maximum_fusion), channel_id=1, source_target_pairs={{0,1},{1,0},{2,3},{3,2},{4,5},{5,4},{6,7},{7,6},{8,9},{9,8},{10,11... | collective-permute-start | bytes 2949128 | tf_op jit(solution)/shard_map/ppermute | solution.py:542
  73.8 15.6 %collective-permute-start.12 = (f32[2,96,768]{2,1,0:T(8,128)}, f32[2,96,768]{2,1,0:T(8,128)}, u32[]{:S(2)}, u32[]{:S(2)}) collective-permute-start(f32[2,96,768]{2,1,0:T(8,128)} %pad_maximum_fusion.7.u0_ref), channel_id=1, source_target_pairs={{0,16},{4,20},{8,24},{12,28},{16,0},{20,4},{24,8},{28,12},{1,17},{... | collective-permute-start | bytes 1769480 | tf_op jit(solution)/shard_map/ppermute | solution.py:546
  75.2 15.3 %collective-permute-start.13 = (f32[2,96,768]{2,1,0:T(8,128)}, f32[2,96,768]{2,1,0:T(8,128)}, u32[]{:S(2)}, u32[]{:S(2)}) collective-permute-start(f32[2,96,768]{2,1,0:T(8,128)} %pad_maximum_fusion.8.d0_ref), channel_id=1, source_target_pairs={{0,8},{4,12},{8,0},{12,4},{16,24},{20,28},{24,16},{28,20},{1,9},{5... | collective-permute-start | bytes 1769480 | tf_op jit(solution)/shard_map/ppermute | solution.py:546
  108.5 15.8 %collective-permute-start.21 = (f32[2,96,768]{2,1,0:T(8,128)S(1)}, f32[2,96,768]{2,1,0:T(8,128)S(1)}, u32[]{:S(2)}, u32[]{:S(2)}) collective-permute-start(f32[2,96,768]{2,1,0:T(8,128)S(1)} %pad_maximum_fusion.11.u0_ref), channel_id=1, source_target_pairs={{0,16},{4,20},{8,24},{12,28},{16,0},{20,4},{24,8},{28,12},{1,17},{... | collective-permute-start | bytes 1769480 | tf_op jit(solution)/shard_map/ppermute | solution.py:546
  109.7 16.0 %collective-permute-start.22 = (f32[2,96,768]{2,1,0:T(8,128)S(1)}, f32[2,96,768]{2,1,0:T(8,128)S(1)}, u32[]{:S(2)}, u32[]{:S(2)}) collective-permute-start(f32[2,96,768]{2,1,0:T(8,128)S(1)} %pad_maximum_fusion.12.d0_ref), channel_id=1, source_target_pairs={{0,8},{4,12},{8,0},{12,4},{16,24},{20,28},{24,16},{28,20},{1,9},{5... | collective-permute-start | bytes 1769480 | tf_op jit(solution)/shard_map/ppermute | solution.py:546
  125.8 14.7 %collective-permute-start.23 = (f32[2,96,768]{2,1,0:T(8,128)S(1)}, f32[2,96,768]{2,1,0:T(8,128)S(1)}, u32[]{:S(2)}, u32[]{:S(2)}) collective-permute-start(f32[2,96,768]{2,1,0:T(8,128)S(1)} %pad_maximum_fusion.13.u0_ref), channel_id=1, source_target_pairs={{0,16},{4,20},{8,24},{12,28},{16,0},{20,4},{24,8},{28,12},{1,17},{... | collective-permute-start | bytes 1769480 | tf_op jit(solution)/shard_map/ppermute | solution.py:546
  182.5 18.1 %collective-permute-start.35 = (f32[2,512,768]{2,1,0:T(8,128)S(1)}, f32[2,512,768]{2,1,0:T(8,128)S(1)}, u32[]{:S(2)}, u32[]{:S(2)}) collective-permute-start(f32[2,512,768]{2,1,0:T(8,128)S(1)} %shard_map.314), channel_id=1, source_target_pairs={{0,4},{4,0},{8,12},{12,8},{16,20},{20,16},{24,28},{28,24},{1,5},{5... | collective-permute-start | bytes 9437192 | tf_op jit(solution)/shard_map/ppermute | solution.py:546
  182.5 16.0 %collective-permute-start.36 = (f32[192,768]{1,0:T(8,128)S(1)}, f32[192,768]{1,0:T(8,128)S(1)}, u32[]{:S(2)}, u32[]{:S(2)}) collective-permute-start(f32[192,768]{1,0:T(8,128)S(1)} %pad_maximum_fusion.15), channel_id=1, source_target_pairs={{0,1},{1,0},{2,3},{3,2},{4,5},{5,4},{6,7},{7,6},{8,9},{9,8},{10,11... | collective-permute-start | bytes 1769480 | tf_op jit(solution)/shard_map/ppermute | solution.py:542
  184.5 15.5 %collective-permute-start.37 = (f32[192,768]{1,0:T(8,128)S(1)}, f32[192,768]{1,0:T(8,128)S(1)}, u32[]{:S(2)}, u32[]{:S(2)}) collective-permute-start(f32[192,768]{1,0:T(8,128)S(1)} %get-tuple-element.1204), channel_id=1, source_target_pairs={{0,16},{4,20},{8,24},{12,28},{16,0},{20,4},{24,8},{28,12},{1,17},{... | collective-permute-start | bytes 1769480 | tf_op jit(solution)/shard_map/ppermute | solution.py:546
  185.4 15.2 %collective-permute-start.38 = (f32[192,768]{1,0:T(8,128)S(1)}, f32[192,768]{1,0:T(8,128)S(1)}, u32[]{:S(2)}, u32[]{:S(2)}) collective-permute-start(f32[192,768]{1,0:T(8,128)S(1)} %get-tuple-element.1208), channel_id=1, source_target_pairs={{0,8},{4,12},{8,0},{12,4},{16,24},{20,28},{24,16},{28,20},{1,9},{5... | collective-permute-start | bytes 1769480 | tf_op jit(solution)/shard_map/ppermute | solution.py:546
  222.7 19.0 %collective-permute-start.45 = (f32[192,512]{1,0:T(8,128)S(1)}, f32[192,512]{1,0:T(8,128)S(1)}, u32[]{:S(2)}, u32[]{:S(2)}) collective-permute-start(f32[192,512]{1,0:T(8,128)S(1)} %get-tuple-element.1315), channel_id=1, source_target_pairs={{0,1},{1,0},{2,3},{3,2},{4,5},{5,4},{6,7},{7,6},{8,9},{9,8},{10,11... | collective-permute-start | bytes 1179656 | tf_op jit(solution)/shard_map/ppermute | solution.py:542
  223.8 20.6 %collective-permute-start.48 = (f32[128,768]{1,0:T(8,128)S(1)}, f32[128,768]{1,0:T(8,128)S(1)}, u32[]{:S(2)}, u32[]{:S(2)}) collective-permute-start(f32[128,768]{1,0:T(8,128)S(1)} %pad_maximum_fusion.18), channel_id=1, source_target_pairs={{0,2},{1,3},{2,0},{3,1},{4,6},{5,7},{6,4},{7,5},{8,10},{9,11},{10,... | collective-permute-start | bytes 1179656 | tf_op jit(solution)/shard_map/ppermute | solution.py:542
  225.7 18.8 %collective-permute-start.47 = (f32[2,96,768]{2,1,0:T(8,128)S(1)}, f32[2,96,768]{2,1,0:T(8,128)S(1)}, u32[]{:S(2)}, u32[]{:S(2)}) collective-permute-start(f32[2,96,768]{2,1,0:T(8,128)S(1)} %get-tuple-element.1503), channel_id=1, source_target_pairs={{0,8},{4,12},{8,0},{12,4},{16,24},{20,28},{24,16},{28,20},{1,9},{5... | collective-permute-start | bytes 1769480 | tf_op jit(solution)/shard_map/ppermute | solution.py:546
  247.3 18.6 %collective-permute-start.50 = (f32[240,768]{1,0:T(8,128)S(1)}, f32[240,768]{1,0:T(8,128)S(1)}, u32[]{:S(2)}, u32[]{:S(2)}) collective-permute-start(f32[240,768]{1,0:T(8,128)S(1)} %pad_maximum_fusion.6), channel_id=1, source_target_pairs={{0,8},{4,12},{8,0},{12,4},{16,24},{20,28},{24,16},{28,20},{1,9},{5... | collective-permute-start | bytes 2211848 | tf_op jit(solution)/shard_map/ppermute | solution.py:546
  248.3 15.2 %collective-permute-start.51 = (f32[192,768]{1,0:T(8,128)S(1)}, f32[192,768]{1,0:T(8,128)S(1)}, u32[]{:S(2)}, u32[]{:S(2)}) collective-permute-start(f32[192,768]{1,0:T(8,128)S(1)} %pad_maximum_fusion.16), channel_id=1, source_target_pairs={{0,16},{4,20},{8,24},{12,28},{16,0},{20,4},{24,8},{28,12},{1,17},{... | collective-permute-start | bytes 1769480 | tf_op jit(solution)/shard_map/ppermute | solution.py:546
  265.9 22.0 %collective-permute-start.52 = (f32[256,768]{1,0:T(8,128)S(1)}, f32[256,768]{1,0:T(8,128)S(1)}, u32[]{:S(2)}, u32[]{:S(2)}) collective-permute-start(f32[256,768]{1,0:T(8,128)S(1)} %get-tuple-element.1408.refs_4_), channel_id=1, source_target_pairs={{0,1},{1,0},{2,3},{3,2},{4,5},{5,4},{6,7},{7,6},{8,9},{9,8},{10,11... | collective-permute-start | bytes 2359304 | tf_op jit(solution)/shard_map/ppermute | solution.py:542
  266.2 21.7 %collective-permute-start.54 = (f32[264,768]{1,0:T(8,128)S(1)}, f32[264,768]{1,0:T(8,128)S(1)}, u32[]{:S(2)}, u32[]{:S(2)}) collective-permute-start(f32[264,768]{1,0:T(8,128)S(1)} %pad_maximum_fusion.3.a_ref), channel_id=1, source_target_pairs={{0,16},{4,20},{8,24},{12,28},{16,0},{20,4},{24,8},{28,12},{1,17},{... | collective-permute-start | bytes 2433032 | tf_op jit(solution)/shard_map/ppermute | solution.py:546
  267.4 20.6 %collective-permute-start.56 = (f32[4,72,768]{2,1,0:T(8,128)S(1)}, f32[4,72,768]{2,1,0:T(8,128)S(1)}, u32[]{:S(2)}, u32[]{:S(2)}) collective-permute-start(f32[4,72,768]{2,1,0:T(8,128)S(1)} %get-tuple-element.1419), channel_id=1, source_target_pairs={{0,4},{4,0},{8,12},{12,8},{16,20},{20,16},{24,28},{28,24},{1,5},{5... | collective-permute-start | bytes 2654216 | tf_op jit(solution)/shard_map/ppermute | solution.py:546
  267.5 20.4 %collective-permute-start.53 = (f32[192,768]{1,0:T(8,128)S(1)}, f32[192,768]{1,0:T(8,128)S(1)}, u32[]{:S(2)}, u32[]{:S(2)}) collective-permute-start(f32[192,768]{1,0:T(8,128)S(1)} %pad_maximum_fusion.17.a_ref), channel_id=1, source_target_pairs={{0,8},{4,12},{8,0},{12,4},{16,24},{20,28},{24,16},{28,20},{1,9},{5... | collective-permute-start | bytes 1769480 | tf_op jit(solution)/shard_map/ppermute | solution.py:546
  272.9 15.0 %collective-permute-start.55 = (f32[48,768]{1,0:T(8,128)S(1)}, f32[48,768]{1,0:T(8,128)S(1)}, u32[]{:S(2)}, u32[]{:S(2)}) collective-permute-start(f32[48,768]{1,0:T(8,128)S(1)} %pad_maximum_fusion.22), channel_id=1, source_target_pairs={{0,1},{1,0},{2,3},{3,2},{4,5},{5,4},{6,7},{7,6},{8,9},{9,8},{10,11... | collective-permute-start | bytes 442376 | tf_op jit(solution)/shard_map/ppermute | solution.py:542
  287.9 18.0 %collective-permute-start.58 = (f32[112,768]{1,0:T(8,128)S(1)}, f32[112,768]{1,0:T(8,128)S(1)}, u32[]{:S(2)}, u32[]{:S(2)}) collective-permute-start(f32[112,768]{1,0:T(8,128)S(1)} %get-tuple-element.1432.refs_5_), channel_id=1, source_target_pairs={{0,1},{1,0},{2,3},{3,2},{4,5},{5,4},{6,7},{7,6},{8,9},{9,8},{10,11... | collective-permute-start | bytes 1032200 | tf_op jit(solution)/shard_map/ppermute | solution.py:542
  288.3 17.6 %collective-permute-start.59 = (f32[264,768]{1,0:T(8,128)S(1)}, f32[264,768]{1,0:T(8,128)S(1)}, u32[]{:S(2)}, u32[]{:S(2)}) collective-permute-start(f32[264,768]{1,0:T(8,128)S(1)} %pad_maximum_fusion.3.a_ref), channel_id=1, source_target_pairs={{0,4},{4,0},{8,12},{12,8},{16,20},{20,16},{24,28},{28,24},{1,5},{5... | collective-permute-start | bytes 2433032 | tf_op jit(solution)/shard_map/ppermute | solution.py:546
  288.3 17.6 %collective-permute-start.60 = (f32[264,768]{1,0:T(8,128)S(1)}, f32[264,768]{1,0:T(8,128)S(1)}, u32[]{:S(2)}, u32[]{:S(2)}) collective-permute-start(f32[264,768]{1,0:T(8,128)S(1)} %collective-permute-done.54.b_ref), channel_id=1, source_target_pairs={{0,4},{4,0},{8,12},{12,8},{16,20},{20,16},{24,28},{28,24},{1,5},{5... | collective-permute-start | bytes 2433032 | tf_op jit(solution)/shard_map/ppermute | solution.py:546
  288.9 17.0 %collective-permute-start.61 = (f32[2,72,768]{2,1,0:T(8,128)S(1)}, f32[2,72,768]{2,1,0:T(8,128)S(1)}, u32[]{:S(2)}, u32[]{:S(2)}) collective-permute-start(f32[2,72,768]{2,1,0:T(8,128)S(1)} %get-tuple-element.1505), channel_id=1, source_target_pairs={{0,8},{4,12},{8,0},{12,4},{16,24},{20,28},{24,16},{28,20},{1,9},{5... | collective-permute-start | bytes 1327112 | tf_op jit(solution)/shard_map/ppermute | solution.py:546
  289.9 16.0 %collective-permute-start.62 = (f32[96,768]{1,0:T(8,128)S(1)}, f32[96,768]{1,0:T(8,128)S(1)}, u32[]{:S(2)}, u32[]{:S(2)}) collective-permute-start(f32[96,768]{1,0:T(8,128)S(1)} %pad_maximum_fusion.19), channel_id=1, source_target_pairs={{0,2},{1,3},{2,0},{3,1},{4,6},{5,7},{6,4},{7,5},{8,10},{9,11},{10,... | collective-permute-start | bytes 884744 | tf_op jit(solution)/shard_map/ppermute | solution.py:542
  (125 other events, 1174.4 us)

commit v3 on v2

--- a/solution.py
+++ b/solution.py
@@ -313,10 +313,14 @@
     gps = refs[nslot : 2 * nslot]
     ubs = refs[2 * nslot : 3 * nslot]
     dbs = refs[3 * nslot : 4 * nslot]
-    out_ref = refs[4 * nslot]
+    outs = refs[4 * nslot :]
     cat = lambda refs, axis: jnp.concatenate([r[...] for r in refs], axis=axis)
-    out_ref[0] = mm(cat(hids, 1), cat(dbs, 0))
-    out_ref[1] = mm(cat(gps, 1), cat(ubs, 0))
+    share = outs[0].shape[1]
+    for i, (rows_of, w_of) in enumerate(((hids, dbs), (gps, ubs))):
+        w = cat(w_of, 0)
+        for r, out_ref in enumerate(outs):
+            rows = slice(r * share, (r + 1) * share)
+            out_ref[i] = mm(jnp.concatenate([a[rows, :] for a in rows_of], axis=1), w)
 
 
 def mid_kernel(nslot, mid_ref, own_ref, got_ref, cot_ref, db_ref, g_ref, *refs):
@@ -506,24 +510,17 @@
         at += ref.shape[0]
 
 
-def lay_out(refs, to_ref):
-    part = to_ref.shape[1]
-    for i, ref in enumerate(refs):
-        for j in range(2):
-            to_ref[2 * i + j] = ref[j * part : (j + 1) * part, :]
-
-
-def unpack_kernel(idx_ref, a_ref, b_ref, c_ref, d_ref, out_ref, s_ref):
-    lay_out((a_ref, b_ref, c_ref, d_ref), s_ref)
-    whole = jnp.concatenate([s_ref[idx_ref[p]] for p in range(PIECES)], axis=0)
-    out_ref[...] = whole.T
-
-
-def unpack_rows_kernel(idx_ref, a_ref, b_ref, c_ref, d_ref, out_ref, s_ref):
-    part = s_ref.shape[1]
-    lay_out((a_ref, b_ref, c_ref, d_ref), s_ref)
+def unpack_mlp_kernel(ia_ref, ib_ref, a_ref, b_ref, up_ref, down_ref, s_ref):
+    part = s_ref.shape[2]
+    half = PIECES // 2
+    for w in range(2):
+        for j in range(half):
+            rows = slice((w * half + j) * part, (w * half + j + 1) * part)
+            s_ref[w, j] = a_ref[rows, :]
+            s_ref[w, half + j] = b_ref[rows, :]
+    up_ref[...] = jnp.concatenate([s_ref[0, ia_ref[p]] for p in range(PIECES)], axis=0).T
     for p in range(PIECES):
-        out_ref[p * part : (p + 1) * part, :] = s_ref[idx_ref[p]]
+        down_ref[p * part : (p + 1) * part, :] = s_ref[1, ib_ref[p]]
 
 
 def unpack_att_kernel(i_ref, a_ref, b_ref, qkv_ref, out_ref, s_ref):
@@ -635,8 +632,8 @@
         me1, qkv_t, out_weight, qkv_bias, up_bias, up_weight, down_weight
     )
 
-    n_gn = (256, 112, 144)
-    n_z2 = 64
+    n_gn = (224, 208, 80)
+    n_q0 = 40
     numbers = jnp.arange(PIECES, dtype=jnp.int32)
     idx_a = storage_of(numbers ^ me, BITS_A).astype(jnp.int32)
     idx_b = storage_of(numbers ^ me, BITS_B).astype(jnp.int32)
@@ -793,17 +790,15 @@
             v[f"p{k}"], v[f"q{k}u"] = res[4], res[5]
             v[f"w{k}"] = res[6:9]
 
-    def run_down(r):
-        row_spec = pl.BlockSpec((share, mine), lambda t: (r, 0))
-        w_spec = pl.BlockSpec((mine, width), lambda t: (0, 0))
+    def run_down():
         return call(
             functools.partial(down_kernel, nmp),
-            sds((2, share, width), F32),
-            flops=4 * share * width * mine * nmp,
-            bytes_accessed=11_000_000,
-            grid=(1,),
-            in_specs=[row_spec] * (2 * nmp) + [w_spec] * (2 * nmp),
-            out_specs=pl.BlockSpec((2, share, width), lambda t: (0, 0, 0)),
+            (sds((2, share, width), F32),) * 2,
+            flops=4 * full * width * mine * nmp,
+            bytes_accessed=17_000_000,
+            vmem_limit=40 * 1024 * 1024,
+            in_specs=[vmem] * (4 * nmp),
+            out_specs=(vmem,) * 2,
         )(*[v[f"h{k}"][i] for i in range(4) for k in range(nmp)])
 
     def run_mid():
@@ -846,7 +841,7 @@
             grid=(1,),
             in_specs=[smem] + specs,
             out_specs=tuple(whole(a) for a in shapes),
-        )(idx_b, *args)
+        )(idx_a, *args)
 
     def run_attn_bwd(k, got, idx, first):
         st = v.pop(f"st{k}")
@@ -1051,63 +1046,49 @@
     v["q3u"] = zswap(v["q3u"], 1)
     c1(0)
     c1(2)
-    v["send"] = run_down(1)
+    v["acc_own"], v["acc_far"] = run_down()
     v.fence()
     c0(0)
     c0(2)
     v["d13"] = zswap(v["d13"], 1)
-    v["acc_got"] = swap(v.pop("send"), core)
-    v["acc_own"] = run_down(0)
+    v["acc_got"] = swap(v.pop("acc_far"), core)
+    v["low"] = run_mid()
     v.fence()
     d13 = v.pop("d13")
     v["d1"], v["d3"] = d13[:upart], d13[upart:]
     c2u(0)
     c2u(2)
-    v["low"] = run_mid()
+    v["gp2"] = zswap(v.pop("gmt3"), 1)
+    run_out_grad(v.pop("low"))
     v.fence()
     c2d(0)
     c2d(2)
-    v["gp2"] = zswap(v.pop("gmt3"), 1)
-    v["z2x"] = zswap(v["w2"][0][:n_z2], 2)
-    run_out_grad(v.pop("low"))
+    v["gp0"] = zswap(v.pop("gmt1"), 1)
+    v["z2x"] = zswap(v["w2"][0], 2)
+    run_attn_bwd(2, "gp2", idx_b, True)
+    v.fence()
+    r1("q2")
+    r1("o")
     v.fence()
     c3(0)
     c3(2)
-    up_sum, down_sum = v.pop("w2")
-    v["z2y"] = zswap(jnp.concatenate([up_sum[n_z2:], down_sum], axis=0), 2)
-    v["gp0"] = zswap(v.pop("gmt1"), 1)
-    r1("o")
-    r2("o", "b")
-    run_attn_bwd(2, "gp2", idx_b, True)
-    v.fence()
-    r1("q2")
-    v.fence()
-    mlp_sum = high_bits(
-        jnp.concatenate(v.pop("w0"), axis=0)
-        + jnp.concatenate([v.pop("z2x"), v.pop("z2y")], axis=0)
-    )
-    ma, mb = mlp_sum[:upart], mlp_sum[upart:]
+    v["z2y"] = zswap(v.pop("w2")[1], 2)
+    r2("q2", "b")
+    r2("o", "a")
+    run_attn_bwd(0, "gp0", idx_b, False)
+    v.fence()
+    up_sum, down_sum = v.pop("w0")
+    ma = high_bits(up_sum + v.pop("z2x"))
+    mb = high_bits(down_sum + v.pop("z2y"))
+    r1("q0")
+    keep, got = v["o"]
+    to_x = jnp.concatenate([ma, keep[1] + got[1]], axis=0)
+    v["o"] = keep[0] + got[0]
     keep, got = v["q2"]
-    to_x = jnp.concatenate([(keep[2:] + got[2:]).reshape(-1, width), ma], axis=0)
-    v["q2"] = keep[:2] + got[:2]
-    keep, got = v["o"]
-    to_y = jnp.concatenate([keep[1] + got[1], mb], axis=0)
-    v["o"] = keep[0] + got[0]
+    to_y = jnp.concatenate([mb, keep[1] + got[1]], axis=0)
+    v["q2"] = keep[0] + got[0]
     v["gx"], v["gy"] = (to_x, swap(to_x, px)), (to_y, swap(to_y, py))
-    run_attn_bwd(0, "gp0", idx_b, False)
-    v.fence()
-    nq = 2 * 3 * part
-    (xa, xb), (ya, yb) = v.pop("gx"), v.pop("gy")
-    r1("q0")
-    q2 = v["q2"] + xb[:nq].reshape(2, 3 * part, width)
-    v["q2"] = q2[0]
-    to_y = jnp.concatenate([xa[nq:], xb[nq:], q2[1]], axis=0)
-    to_x = jnp.concatenate([ya[nmp * part :], yb[nmp * part :]], axis=0)
-    v["gx"], v["gy"] = (to_x, swap(to_x, px)), (to_y, swap(to_y, py))
-    o = v.pop("o") + yb[: nmp * part]
     v["gn0"] = zswap(v["gn_far"][0], 1)
-    v["oz"] = zswap(jnp.concatenate([o[part : 2 * part], o[3 * part :]], axis=0), 1)
-    v["o0"], v["o2"] = o[:part], o[2 * part : 3 * part]
     v["small"] = call(
         functools.partial(sums_kernel, nmp),
         sds((16, width), F32),
@@ -1134,46 +1115,53 @@
     )
     v["small"] = v["small"] + swap(v["small"], core)
     v.fence()
-    r2("q0", "b")
-    (xa, xb), (ya, yb) = v["gx"], v["gy"]
+    (xa, xb), (ya, yb) = v.pop("gx"), v.pop("gy")
+    o = v.pop("o") + xb[upart:]
+    v["q2"] = v["q2"] + yb[upart:]
+    keep, got = v.pop("q0")
+    q0 = keep + got
+    v["q0b"], v["q0a"] = q0[:2, :n_q0], (q0[0, n_q0:], q0[2, n_q0:])
+    to_y = jnp.concatenate([xa[:upart], xb[:upart], q0[1, n_q0:], q0[3, n_q0:]], axis=0)
+    to_x = jnp.concatenate([ya[:upart], yb[:upart], q0[2, :n_q0], q0[3, :n_q0]], axis=0)
+    v["gx"], v["gy"] = (to_x, swap(to_x, px)), (to_y, swap(to_y, py))
+    v["oz"] = zswap(jnp.concatenate([o[part : 2 * part], o[3 * part :]], axis=0), 1)
+    v["o0"], v["o2"] = o[:part], o[2 * part : 3 * part]
+    v["gn1"] = zswap(v["gn_far"][1], 1)
+    v["small"] = v["small"] + swap(v["small"], px)
+    v.fence()
+    (xa, xb), (ya, yb) = v.pop("gx"), v.pop("gy")
+    q0b = v.pop("q0b") + xb[2 * upart :].reshape(2, n_q0, width)
+    n_rest = 3 * part - n_q0
+    q0a = [
+        a + yb[2 * upart + i * n_rest : 2 * upart + (i + 1) * n_rest]
+        for i, a in enumerate(v.pop("q0a"))
+    ]
+    v["q0b"] = (q0b[0], swap(q0b[1], py))
+    v["q0a"] = (q0a[0], swap(q0a[1], px))
     oz = v.pop("oz")
     v["o0"] = v["o0"] + oz[:part]
-    q2 = v.pop("q2") + yb[2 * upart :]
-    v["y2"] = zswap(jnp.concatenate([q2, v.pop("o2") + oz[part:]], axis=0), 2)
-    v["gn1"] = zswap(v["gn_far"][1], 1)
-    v["gu"] = (ya, yb, swap(ya, core), swap(yb, core))
-    v.pop("gy")
-    v.fence()
-    r3("q0", "b")
+    v["y2"] = zswap(jnp.concatenate([v.pop("q2"), v.pop("o2") + oz[part:]], axis=0), 2)
     v["gn2"] = zswap(v.pop("gn_far")[2], 1)
-    small = v["small"] + swap(v["small"], px)
-    v["small"] = small + swap(small, py)
-    xa, xb = v.pop("gx")
-    v["gd"] = (xa, xb, swap(xa, core), swap(xb, core))
-    def unpack(kernel, arrays, idx, shape):
-        pieces_spec = pl.BlockSpec((2 * upart, width), lambda t: (0, 0))
-        return call(
-            kernel,
-            sds(shape, F32),
-            bytes_accessed=2 * 4 * math.prod(shape),
-            grid=(1,),
-            in_specs=[smem] + [pieces_spec] * 4,
-            out_specs=pl.BlockSpec(shape, lambda t: (0, 0)),
-            scratch_shapes=[pltpu.VMEM((PIECES, upart, width), F32)],
-        )(idx, *arrays)
-
-    v["up_g"] = unpack(unpack_kernel, v.pop("gu"), idx_a, (width, units))
-    v.fence()
-    r4("q0")
-    att_sum = high_bits(
-        jnp.concatenate([v.pop("q0"), v.pop("o0")], axis=0) + v.pop("y2")
-    )
+    v["small"] = v["small"] + swap(v["small"], py)
+    n2 = 2 * upart
+    v["mlp"] = jnp.concatenate([ya[:n2], yb[:n2], xa[:n2], xb[:n2]], axis=0)
+    v.fence()
+    q0 = jnp.concatenate([a + b for a, b in (v.pop("q0b"), v.pop("q0a"))], axis=0)
+    att_sum = high_bits(jnp.concatenate([q0, v.pop("o0")], axis=0) + v.pop("y2"))
     v["w"] = (att_sum, swap(att_sum, px), swap(att_sum, py), swap(att_sum, px | py))
     small = high_bits(v.pop("small"))
     got = zswap(jnp.concatenate([small[:8], small[12:]], axis=0), 1)
     v["small"] = small[:12] + got
 
-    v["down_g"] = unpack(unpack_rows_kernel, v.pop("gd"), idx_b, (units, width))
+    mlp = v.pop("mlp")
+    v["up_g"], v["down_g"] = call(
+        unpack_mlp_kernel,
+        (sds((width, units), F32), sds((units, width), F32)),
+        bytes_accessed=10_000_000,
+        in_specs=[smem, smem] + [vmem] * 2,
+        out_specs=(vmem,) * 2,
+        scratch_shapes=[pltpu.VMEM((2, PIECES, upart, width), F32)],
+    )(idx_a, idx_b, mlp, swap(mlp, core))
     v["input_grad"] = call(
         final_kernel,
         sds((share, width), BF16),
@@ -1205,6 +1193,9 @@
         scratch_shapes=[pltpu.VMEM((PIECES, 4 * part, width), F32)],
     )(idx_a, w, swap(w, core))
     qkv_weight_grad = jnp.swapaxes(qkv_weight_grad, 1, 2)
+    qkv_weight_grad, out_weight_grad, small, small_got = lax.optimization_barrier(
+        (qkv_weight_grad, out_weight_grad, small, small_got)
+    )
     qkv_bias_grad, *rows_of = call(
         small_out_kernel,
         (sds((3, e), F32), *[sds((DH,), F32)] * 3, *[sds((width,), F32)] * 7),

time: 347 us -> 339 us (0.977)
  waiting for transfers between devices: 158 us -> 149 us
  other arithmetic: 11.8 us -> 15.6 us
    ppermute x22, waiting for transfers between devices: 92.1 us -> 59.5 us  [swap_mp(): return lax.ppermute(a, 'mp', [(s, s ^ k) for s in range(size)])]
    ppermute x50 -> x48, waiting for transfers between devices: 52 us -> 75.2 us  [swap_plane(): return lax.ppermute(a, 'dp', [(d, d ^ bit) for d in range(size)])]
    pallas_call x4 -> x2, Pallas kernels: 10.2 us -> 10.5 us  [the longest x1 6.72 us: run_down(): call(functools.partial(down_kernel, nmp), (sds((2, share, width), F32),)...]
    ppermute x50 -> x48, starting transfers between devices: 40.9 us -> 40.7 us  [swap_plane(): return lax.ppermute(a, 'dp', [(d, d ^ bit) for d in range(size)])]
  transfers between devices with their start and end apart: 75 -> 73, of which waited for: 48 -> 47; matrix products, arithmetic and copies ran while one was open for 3% -> 4% of each run, Pallas kernels for 24% -> 26%
where the time goes in v3:
time: 339 us; the launch traced here: 336 us
  waiting for transfers between devices  149 us (44%)
  Pallas kernels  92.6 us (27%)
  starting transfers between devices  67.8 us (20%)
  other arithmetic  15.6 us (5%)
  local copies, waits for them, and re-layouts  8.33 us (2%)
    ppermute x48, waiting for transfers between devices, swap_plane(): return lax.ppermute(a, 'dp', [(d, d ^ bit) for d in range(size)])  75.2 us
    ppermute x22, waiting for transfers between devices, swap_mp(): return lax.ppermute(a, 'mp', [(s, s ^ k) for s in range(size)])  59.5 us
    ppermute x48, starting transfers between devices, swap_plane(): return lax.ppermute(a, 'dp', [(d, d ^ bit) for d in range(size)])  40.7 us
    pallas_call x2, Pallas kernels, run_attn_bwd(): call(functools.partial(attn_bwd_kernel, 0 if first else len(cuts_now)), (...  24.3 us
    ppermute x22, starting transfers between devices, swap_mp(): return lax.ppermute(a, 'mp', [(s, s ^ k) for s in range(size)])  24.2 us
    pallas_call x4, Pallas kernels, run_mlp(): call(functools.partial(mlp_kernel, MLP_KIND[k], keeps), shapes, flops=2 *...  22.1 us
    ppermute x1, waiting for transfers between devices, pass_out(): return lax.ppermute(a, 'mp', [(1, 0), (2, 3)])  14.2 us
    pallas_call x1, Pallas kernels, run_attn_far(): call(attn_fwd_kernel, tuple(shapes), flops=2 * (full * width * e * 3 + fu...  7.12 us
  transfers between devices with their start and end apart: 73, of which 47 were waited for; matrix products, arithmetic and copies ran while one was open for 4% of the time, Pallas kernels for 26%

profile of v3, /device:TPU:0, one launch (start us, length us, event | category | flops | bytes accessed | tf_op | source)
XLA Modules:
  0.0 335.7 jit_solution(17807193009652466620)
XLA Ops:
  0.7 4.2 %shard_map.305 = (f32[104,768]{1,0:T(8,128)}, f32[32,768]{1,0:T(8,128)}, f32[8,768]{1,0:T(8,128)}, f32[192,768]{1,0:T(8,128)}, bf16[2,96,768]{2,1,0:T(8,128)(2,1...) custom-call(s32[1]{0:T(128)} %bitcast.me_ref, ...), custom_call_target="tpu_custom_call" | custom-call | bytes 9000000 | tf_op jit(solution)/shard_map/pallas_call | solution.py:617
  4.9 4.0 %collective-permute-start.2 = (f32[104,768]{1,0:T(8,128)}, f32[104,768]{1,0:T(8,128)S(1)}, u32[]{:S(2)}, u32[]{:S(2)}) collective-permute-start(f32[104,768]{1,0:T(8,128)} %get-tuple-element.729), channel_id=1, source_target_pairs={{0,2},{1,3},{2,0},{3,1},{4,6},{5,7},{6,4},{7,5},{8,10},{9,11},{10,... | collective-permute-start | bytes 958472 | tf_op jit(solution)/shard_map/ppermute | solution.py:539
  12.5 3.3 fusion.7
  15.8 3.5 %collective-permute-done.b_ref = f32[32,768]{1,0:T(8,128)} collective-permute-done((f32[32,768]{1,0:T(8,128)}, f32[32,768]{1,0:T(8,128)}, u32[]{:S(2)}, u32[]{:S(2)}) %collective-permute-start) | collective-permute-done | bytes 98336 | tf_op jit(solution)/shard_map/ppermute | solution.py:539
  22.1 4.3 %collective-permute-done.2.b_ref = f32[104,768]{1,0:T(8,128)S(1)} collective-permute-done((f32[104,768]{1,0:T(8,128)}, f32[104,768]{1,0:T(8,128)S(1)}, u32[]{:S(2)}, u32[]{:S(2)}) %collective-permute-start.2) | collective-permute-done | bytes 319520 | tf_op jit(solution)/shard_map/ppermute | solution.py:539
  34.5 3.5 %collective-permute-done.7 = f32[72,768]{1,0:T(8,128)S(1)} collective-permute-done((f32[72,768]{1,0:T(8,128)S(1)}, f32[72,768]{1,0:T(8,128)S(1)}, u32[]{:S(2)}, u32[]{:S(2)}) %collective-permute-start.7) | collective-permute-done | bytes 221216 | tf_op jit(solution)/shard_map/ppermute | solution.py:543
  48.8 4.9 %shard_map.307 = (f32[192,1024]{1,0:T(8,128)S(1)}, f32[192,1024]{1,0:T(8,128)S(1)}, bf16[192,1024]{1,0:T(8,128)(2,1)S(1)}, bf16[192,512]{1,0:T(8,128)(2,1)S(1)},...) custom-call(bf16[1024,768]{1,0:T(8,128)(2,1)S(1)} %copy-done.4, ...), custom_call_target="tpu_custom_call" | custom-call | flops 4127195136 | bytes 10000000 | tf_op jit(solution)/shard_map/pallas_call | solution.py:701
  53.8 14.2 %collective-permute-done.8 = f32[192,768]{1,0:T(8,128)S(1)} collective-permute-done((f32[192,768]{1,0:T(8,128)S(1)}, f32[192,768]{1,0:T(8,128)S(1)}, u32[]{:S(2)}, u32[]{:S(2)}) %collective-permute-start.8) | collective-permute-done | bytes 589856 | tf_op jit(solution)/shard_map/ppermute | solution.py:958
  79.2 7.1 %shard_map.308 = (bf16[576,768]{1,0:T(8,128)(2,1)S(1)}, bf16[192,768]{1,0:T(8,128)(2,1)S(1)}, bf16[192,768]{1,0:T(8,128)(2,1)S(1)}, bf16[192,768]{1,0:T(8,128)(2...) custom-call(s32[8]{0:T(128)S(1)} %get-tuple-element.1487.ia_ref.idx_, ...), custom_call_target="tpu_custom_call" | custom-call | flops 4127195136 | bytes 10000000 | tf_op jit(solution)/shard_map/pallas_call | solution.py:721
  89.5 6.4 %collective-permute-done.14.refs_1_ = f32[320,768]{1,0:T(8,128)} collective-permute-done((f32[320,768]{1,0:T(8,128)}, f32[320,768]{1,0:T(8,128)}, u32[]{:S(2)}, u32[]{:S(2)}) %collective-permute-start.14) | collective-permute-done | bytes 983072 | tf_op jit(solution)/shard_map/ppermute | solution.py:539
  99.1 9.3 %collective-permute-done.19.refs_3_ = f32[128,768]{1,0:T(8,128)S(1)} collective-permute-done((f32[128,768]{1,0:T(8,128)S(1)}, f32[128,768]{1,0:T(8,128)S(1)}, u32[]{:S(2)}, u32[]{:S(2)}) %collective-permute-start.19) | collective-permute-done | bytes 393248 | tf_op jit(solution)/shard_map/ppermute | solution.py:539
  115.6 5.2 %shard_map.310 = (bf16[1024,384]{1,0:T(8,128)(2,1)S(1)}, bf16[1024,384]{1,0:T(8,128)(2,1)S(1)}, bf16[384,768]{1,0:T(8,128)(2,1)S(1)}, bf16[384,768]{1,0:T(8,128)...) custom-call(bf16[512,768]{1,0:T(8,128)(2,1)S(1)} %get-tuple-element., ...), custom_call_target="tpu_custom_call" | custom-call | flops 2415919104 | bytes 12000000 | tf_op jit(solution)/shard_map/pallas_call | solution.py:776
  121.7 6.5 %collective-permute-done.22.d1_ref = f32[2,96,768]{2,1,0:T(8,128)S(1)} collective-permute-done((f32[2,96,768]{2,1,0:T(8,128)S(1)}, f32[2,96,768]{2,1,0:T(8,128)S(1)}, u32[]{:S(2)}, u32[]{:S(2)}) %collective-permute-start.22) | collective-permute-done | bytes 589856 | tf_op jit(solution)/shard_map/ppermute | solution.py:543
  132.8 5.4 %shard_map.311 = (bf16[1024,384]{1,0:T(8,128)(2,1)S(1)}, bf16[1024,384]{1,0:T(8,128)(2,1)S(1)}, bf16[384,768]{1,0:T(8,128)(2,1)S(1)}, bf16[384,768]{1,0:T(8,128)...) custom-call(bf16[512,768]{1,0:T(8,128)(2,1)S(1)} %get-tuple-element., ...), custom_call_target="tpu_custom_call" | custom-call | flops 2415919104 | bytes 12000000 | tf_op jit(solution)/shard_map/pallas_call | solution.py:776
  138.2 5.6 %collective-permute-done.24.d1_ref = f32[2,96,768]{2,1,0:T(8,128)S(1)} collective-permute-done((f32[2,96,768]{2,1,0:T(8,128)S(1)}, f32[2,96,768]{2,1,0:T(8,128)S(1)}, u32[]{:S(2)}, u32[]{:S(2)}) %collective-permute-start.24) | collective-permute-done | bytes 589856 | tf_op jit(solution)/shard_map/ppermute | solution.py:543
  148.1 5.6 %shard_map.312 = (bf16[1024,384]{1,0:T(8,128)(2,1)S(1)}, bf16[1024,384]{1,0:T(8,128)(2,1)S(1)}, bf16[384,768]{1,0:T(8,128)(2,1)S(1)}, bf16[384,768]{1,0:T(8,128)...) custom-call(bf16[512,768]{1,0:T(8,128)(2,1)S(1)} %get-tuple-element., ...), custom_call_target="tpu_custom_call" | custom-call | flops 2415919104 | bytes 12000000 | tf_op jit(solution)/shard_map/pallas_call | solution.py:776
  153.7 6.0 %collective-permute-done.26.refs_0_ = f32[192,768]{1,0:T(8,128)S(1)} collective-permute-done((f32[192,768]{1,0:T(8,128)S(1)}, f32[192,768]{1,0:T(8,128)S(1)}, u32[]{:S(2)}, u32[]{:S(2)}) %collective-permute-start.26) | collective-permute-done | bytes 589856 | tf_op jit(solution)/shard_map/ppermute | solution.py:539
  163.9 5.9 %shard_map.313 = (bf16[1024,384]{1,0:T(8,128)(2,1)S(1)}, bf16[1024,384]{1,0:T(8,128)(2,1)S(1)}, bf16[384,768]{1,0:T(8,128)(2,1)S(1)}, bf16[384,768]{1,0:T(8,128)...) custom-call(bf16[512,768]{1,0:T(8,128)(2,1)S(1)} %get-tuple-element., ...), custom_call_target="tpu_custom_call" | custom-call | flops 2415919104 | bytes 12000000 | tf_op jit(solution)/shard_map/pallas_call | solution.py:776
  169.9 3.3 collective-permute-done.29
  177.9 6.7 %shard_map.314 = (f32[2,512,768]{2,1,0:T(8,128)S(1)}, f32[2,512,768]{2,1,0:T(8,128)}) custom-call(bf16[1024,384]{1,0:T(8,128)(2,1)S(1)} %copy-done.38, bf16[1024,384]{1,0:T(8,128)(2,1)S(1)} %copy-done.30, bf16[1024,384]{1,0:T(8,128)(2,1)S(1)} %get-tuple-element.1063.refs_2_, bf16[1024,384]{1,0:T(8,128)(2,1)S(1)} %get-tuple-element.1064.refs_3_, ...), custom_call_target="tpu_custom_call" | custom-call | flops 4831838208 | bytes 17000000 | tf_op jit(solution)/shard_map/pallas_call | solution.py:794
  188.2 3.7 %collective-permute-done.35.got_ref = f32[2,512,768]{2,1,0:T(8,128)S(1)} collective-permute-done((f32[2,512,768]{2,1,0:T(8,128)}, f32[2,512,768]{2,1,0:T(8,128)S(1)}, u32[]{:S(2)}, u32[]{:S(2)}) %collective-permute-start.35) | collective-permute-done | bytes 3145760 | tf_op jit(solution)/shard_map/ppermute | solution.py:543
  192.0 3.2 shard_map.315
  195.2 6.9 %collective-permute-done.36 = f32[192,768]{1,0:T(8,128)S(1)} collective-permute-done((f32[192,768]{1,0:T(8,128)}, f32[192,768]{1,0:T(8,128)S(1)}, u32[]{:S(2)}, u32[]{:S(2)}) %collective-permute-start.36) | collective-permute-done | bytes 589856 | tf_op jit(solution)/shard_map/ppermute | solution.py:539
  207.5 3.2 shard_map.316
  220.1 12.1 %shard_map.317 = (f32[4,72,768]{2,1,0:T(8,128)S(1)}, f32[4,72,768]{2,1,0:T(8,128)S(1)}, f32[1024,768]{1,0:T(8,128)S(1)}, f32[3,64,128]{2,1,0:T(8,128)S(1)}, f32[576,128]{1,0:T(8,128)S(1)}) custom-call(s32[8]{0:T(128)S(1)} %get-tuple-element.1488.ib_ref.idx_ref, bf16[1024,768]{1,0:T(8,128)(2,1)S(1)} %copy-done.6, f32[192,1024]{1,0:T(8,128)S(1)} %copy-done.42, ...), custom_call_target="tpu_custom_call" | custom-call | flops 9865003008 | bytes 14000000 | tf_op jit(solution)/shard_map/pallas_call | solution.py:855
  233.6 3.6 %collective-permute-done.47 = f32[4,72,768]{2,1,0:T(8,128)S(1)} collective-permute-done((f32[4,72,768]{2,1,0:T(8,128)S(1)}, f32[4,72,768]{2,1,0:T(8,128)S(1)}, u32[]{:S(2)}, u32[]{:S(2)}) %collective-permute-start.47) | collective-permute-done | bytes 884768 | tf_op jit(solution)/shard_map/ppermute | solution.py:543
  242.1 12.2 %shard_map.318 = (f32[4,72,768]{2,1,0:T(8,128)S(1)}, f32[4,72,768]{2,1,0:T(8,128)S(1)}, f32[512,768]{1,0:T(8,128)S(1)}, f32[224,768]{1,0:T(8,128)S(1)}, f32[208,...) custom-call(s32[8]{0:T(128)S(1)} %get-tuple-element.1488.ib_ref.idx_ref, ...), custom_call_target="tpu_custom_call" | custom-call | flops 9865003008 | bytes 14000000 | tf_op jit(solution)/shard_map/pallas_call | solution.py:855
  263.3 8.8 %collective-permute-done.53 = f32[168,768]{1,0:T(8,128)S(1)} collective-permute-done((f32[168,768]{1,0:T(8,128)S(1)}, f32[168,768]{1,0:T(8,128)S(1)}, u32[]{:S(2)}, u32[]{:S(2)}) %collective-permute-start.53) | collective-permute-done | bytes 516128 | tf_op jit(solution)/shard_map/ppermute | solution.py:543
  280.4 15.8 %collective-permute-done.60 = f32[16,768]{1,0:T(8,128)S(1)} collective-permute-done((f32[16,768]{1,0:T(8,128)S(1)}, f32[16,768]{1,0:T(8,128)S(1)}, u32[]{:S(2)}, u32[]{:S(2)}) %collective-permute-start.60) | collective-permute-done | bytes 49184 | tf_op jit(solution)/shard_map/ppermute | solution.py:543
  308.1 3.3 collective-permute-done.65
  319.3 3.7 %shard_map.320 = (f32[768,768]{1,0:T(8,128)}, f32[768,768]{1,0:T(8,128)}) custom-call(s32[8]{0:T(128)S(1)} %get-tuple-element.1487.ia_ref.idx_ref.i_ref, s32[8]{0:T(128)S(1)} %get-tuple-element.1488.ib_ref.idx_ref, f32[768,768]{1,0:T(8,128)S(1)} %pad_maximum_fusion.a_ref, f32[768,768]{1,0:T(8,128)S(1)} %collective-permute-done.66.b_ref), custom_call_target="tpu_custom_call" | custom-call | bytes 10000000 | tf_op jit(solution)/shard_map/pallas_call | solution.py:1157
  323.0 5.4 %collective-permute-done.69 = f32[96,768]{1,0:T(8,128)S(1)} collective-permute-done((f32[96,768]{1,0:T(8,128)S(1)}, f32[96,768]{1,0:T(8,128)S(1)}, u32[]{:S(2)}, u32[]{:S(2)}) %collective-permute-start.69) | collective-permute-done | bytes 294944 | tf_op jit(solution)/shard_map/ppermute | solution.py:543
  (408 shorter events, 136.4 us)
Async XLA Ops:
  4.9 21.6 %collective-permute-start.2 = (f32[104,768]{1,0:T(8,128)}, f32[104,768]{1,0:T(8,128)S(1)}, u32[]{:S(2)}, u32[]{:S(2)}) collective-permute-start(f32[104,768]{1,0:T(8,128)} %get-tuple-element.729), channel_id=1, source_target_pairs={{0,2},{1,3},{2,0},{3,1},{4,6},{5,7},{6,4},{7,5},{8,10},{9,11},{10,... | collective-permute-start | bytes 958472 | tf_op jit(solution)/shard_map/ppermute | solution.py:539
  26.4 16.5 %collective-permute-start.3 = (f32[512,768]{1,0:T(8,128)}, f32[512,768]{1,0:T(8,128)}, u32[]{:S(2)}, u32[]{:S(2)}) collective-permute-start(f32[512,768]{1,0:T(8,128)} %get-tuple-element.731), channel_id=1, source_target_pairs={{0,4},{4,0},{8,12},{12,8},{16,20},{20,16},{24,28},{28,24},{1,5},{5... | collective-permute-start | bytes 4718600 | tf_op jit(solution)/shard_map/ppermute | solution.py:543
  26.6 16.3 %collective-permute-start.4 = (f32[192,768]{1,0:T(8,128)}, f32[192,768]{1,0:T(8,128)S(1)}, u32[]{:S(2)}, u32[]{:S(2)}) collective-permute-start(f32[192,768]{1,0:T(8,128)} %get-tuple-element.732), channel_id=1, source_target_pairs={{0,1},{1,0},{2,3},{3,2},{4,5},{5,4},{6,7},{7,6},{8,9},{9,8},{10,11... | collective-permute-start | bytes 1769480 | tf_op jit(solution)/shard_map/ppermute | solution.py:539
  43.1 24.9 %collective-permute-start.11 = (f32[240,768]{1,0:T(8,128)S(1)}, f32[240,768]{1,0:T(8,128)S(1)}, u32[]{:S(2)}, u32[]{:S(2)}) collective-permute-start(f32[240,768]{1,0:T(8,128)S(1)} %pad_maximum_fusion.7), channel_id=1, source_target_pairs={{0,8},{4,12},{8,0},{12,4},{16,24},{20,28},{24,16},{28,20},{1,9},{5... | collective-permute-start | bytes 2211848 | tf_op jit(solution)/shard_map/ppermute | solution.py:543
  44.7 23.3 %collective-permute-start.10 = (f32[240,768]{1,0:T(8,128)S(1)}, f32[240,768]{1,0:T(8,128)S(1)}, u32[]{:S(2)}, u32[]{:S(2)}) collective-permute-start(f32[240,768]{1,0:T(8,128)S(1)} %pad_maximum_fusion.6), channel_id=1, source_target_pairs={{0,16},{4,20},{8,24},{12,28},{16,0},{20,4},{24,8},{28,12},{1,17},{... | collective-permute-start | bytes 2211848 | tf_op jit(solution)/shard_map/ppermute | solution.py:543
  46.3 21.7 %collective-permute-start.9 = (f32[192,768]{1,0:T(8,128)S(1)}, f32[192,768]{1,0:T(8,128)S(1)}, u32[]{:S(2)}, u32[]{:S(2)}) collective-permute-start(f32[192,768]{1,0:T(8,128)S(1)} %collective-permute-done.4), channel_id=1, source_target_pairs={{1,2},{2,1},{5,6},{6,5},{9,10},{10,9},{13,14},{14,13},{17,18},{18,... | collective-permute-start | bytes 1769480 | tf_op jit(solution)/shard_map/ppermute | solution.py:955
  47.0 20.9 %collective-permute-start.8 = (f32[192,768]{1,0:T(8,128)S(1)}, f32[192,768]{1,0:T(8,128)S(1)}, u32[]{:S(2)}, u32[]{:S(2)}) collective-permute-start(f32[192,768]{1,0:T(8,128)S(1)} %collective-permute-done.5), channel_id=1, source_target_pairs={{1,0},{2,3},{5,4},{6,7},{9,8},{10,11},{13,12},{14,15},{17,16},{18,... | collective-permute-start | bytes 1769480 | tf_op jit(solution)/shard_map/ppermute | solution.py:958
  71.9 24.0 %collective-permute-start.14 = (f32[320,768]{1,0:T(8,128)}, f32[320,768]{1,0:T(8,128)}, u32[]{:S(2)}, u32[]{:S(2)}) collective-permute-start(f32[320,768]{1,0:T(8,128)} %pad_maximum_fusion.1), channel_id=1, source_target_pairs={{0,1},{1,0},{2,3},{3,2},{4,5},{5,4},{6,7},{7,6},{8,9},{9,8},{10,11... | collective-permute-start | bytes 2949128 | tf_op jit(solution)/shard_map/ppermute | solution.py:539
  72.8 15.6 %collective-permute-start.13 = (f32[2,96,768]{2,1,0:T(8,128)}, f32[2,96,768]{2,1,0:T(8,128)}, u32[]{:S(2)}, u32[]{:S(2)}) collective-permute-start(f32[2,96,768]{2,1,0:T(8,128)} %pad_maximum_fusion.9.d0_ref), channel_id=1, source_target_pairs={{0,8},{4,12},{8,0},{12,4},{16,24},{20,28},{24,16},{28,20},{1,9},{5... | collective-permute-start | bytes 1769480 | tf_op jit(solution)/shard_map/ppermute | solution.py:543
  74.3 15.3 %collective-permute-start.12 = (f32[2,96,768]{2,1,0:T(8,128)}, f32[2,96,768]{2,1,0:T(8,128)}, u32[]{:S(2)}, u32[]{:S(2)}) collective-permute-start(f32[2,96,768]{2,1,0:T(8,128)} %pad_maximum_fusion.8.u0_ref), channel_id=1, source_target_pairs={{0,16},{4,20},{8,24},{12,28},{16,0},{20,4},{24,8},{28,12},{1,17},{... | collective-permute-start | bytes 1769480 | tf_op jit(solution)/shard_map/ppermute | solution.py:543
  97.4 14.5 %collective-permute-start.18 = (f32[192,768]{1,0:T(8,128)S(1)}, f32[192,768]{1,0:T(8,128)S(1)}, u32[]{:S(2)}, u32[]{:S(2)}) collective-permute-start(f32[192,768]{1,0:T(8,128)S(1)} %pad_maximum_fusion.11), channel_id=1, source_target_pairs={{0,16},{4,20},{8,24},{12,28},{16,0},{20,4},{24,8},{28,12},{1,17},{... | collective-permute-start | bytes 1769480 | tf_op jit(solution)/shard_map/ppermute | solution.py:543
  112.4 15.8 %collective-permute-start.22 = (f32[2,96,768]{2,1,0:T(8,128)S(1)}, f32[2,96,768]{2,1,0:T(8,128)S(1)}, u32[]{:S(2)}, u32[]{:S(2)}) collective-permute-start(f32[2,96,768]{2,1,0:T(8,128)S(1)} %pad_maximum_fusion.13.d0_ref), channel_id=1, source_target_pairs={{0,8},{4,12},{8,0},{12,4},{16,24},{20,28},{24,16},{28,20},{1,9},{5... | collective-permute-start | bytes 1769480 | tf_op jit(solution)/shard_map/ppermute | solution.py:543
  113.5 15.5 %collective-permute-start.21 = (f32[2,96,768]{2,1,0:T(8,128)S(1)}, f32[2,96,768]{2,1,0:T(8,128)S(1)}, u32[]{:S(2)}, u32[]{:S(2)}) collective-permute-start(f32[2,96,768]{2,1,0:T(8,128)S(1)} %pad_maximum_fusion.12.u0_ref), channel_id=1, source_target_pairs={{0,16},{4,20},{8,24},{12,28},{16,0},{20,4},{24,8},{28,12},{1,17},{... | collective-permute-start | bytes 1769480 | tf_op jit(solution)/shard_map/ppermute | solution.py:543
  129.1 14.7 %collective-permute-start.24 = (f32[2,96,768]{2,1,0:T(8,128)S(1)}, f32[2,96,768]{2,1,0:T(8,128)S(1)}, u32[]{:S(2)}, u32[]{:S(2)}) collective-permute-start(f32[2,96,768]{2,1,0:T(8,128)S(1)} %pad_maximum_fusion.15.d0_ref), channel_id=1, source_target_pairs={{0,8},{4,12},{8,0},{12,4},{16,24},{20,28},{24,16},{28,20},{1,9},{5... | collective-permute-start | bytes 1769480 | tf_op jit(solution)/shard_map/ppermute | solution.py:543
  186.1 16.0 %collective-permute-start.36 = (f32[192,768]{1,0:T(8,128)}, f32[192,768]{1,0:T(8,128)S(1)}, u32[]{:S(2)}, u32[]{:S(2)}) collective-permute-start(f32[192,768]{1,0:T(8,128)} %pad_maximum_fusion.16), channel_id=1, source_target_pairs={{0,1},{1,0},{2,3},{3,2},{4,5},{5,4},{6,7},{7,6},{8,9},{9,8},{10,11... | collective-permute-start | bytes 1769480 | tf_op jit(solution)/shard_map/ppermute | solution.py:539
  186.7 15.7 %collective-permute-start.37 = (f32[192,768]{1,0:T(8,128)}, f32[192,768]{1,0:T(8,128)S(1)}, u32[]{:S(2)}, u32[]{:S(2)}) collective-permute-start(f32[192,768]{1,0:T(8,128)} %get-tuple-element.1163), channel_id=1, source_target_pairs={{0,16},{4,20},{8,24},{12,28},{16,0},{20,4},{24,8},{28,12},{1,17},{... | collective-permute-start | bytes 1769480 | tf_op jit(solution)/shard_map/ppermute | solution.py:543
  187.5 15.3 %collective-permute-start.38 = (f32[192,768]{1,0:T(8,128)}, f32[192,768]{1,0:T(8,128)S(1)}, u32[]{:S(2)}, u32[]{:S(2)}) collective-permute-start(f32[192,768]{1,0:T(8,128)} %get-tuple-element.1167), channel_id=1, source_target_pairs={{0,8},{4,12},{8,0},{12,4},{16,24},{20,28},{24,16},{28,20},{1,9},{5... | collective-permute-start | bytes 1769480 | tf_op jit(solution)/shard_map/ppermute | solution.py:543
  215.1 17.3 %collective-permute-start.44 = (f32[96,768]{1,0:T(8,128)S(1)}, f32[96,768]{1,0:T(8,128)S(1)}, u32[]{:S(2)}, u32[]{:S(2)}) collective-permute-start(f32[96,768]{1,0:T(8,128)S(1)} %slice_add_fusion.5), channel_id=1, source_target_pairs={{0,16},{4,20},{8,24},{12,28},{16,0},{20,4},{24,8},{28,12},{1,17},{... | collective-permute-start | bytes 884744 | tf_op jit(solution)/shard_map/ppermute | solution.py:543
  217.4 15.0 %collective-permute-start.45 = (f32[96,768]{1,0:T(8,128)S(1)}, f32[96,768]{1,0:T(8,128)S(1)}, u32[]{:S(2)}, u32[]{:S(2)}) collective-permute-start(f32[96,768]{1,0:T(8,128)S(1)} %get-tuple-element.1450), channel_id=1, source_target_pairs={{0,2},{1,3},{2,0},{3,1},{4,6},{5,7},{6,4},{7,5},{8,10},{9,11},{10,... | collective-permute-start | bytes 884744 | tf_op jit(solution)/shard_map/ppermute | solution.py:539
  237.3 17.1 %collective-permute-start.50 = (f32[96,768]{1,0:T(8,128)S(1)}, f32[96,768]{1,0:T(8,128)S(1)}, u32[]{:S(2)}, u32[]{:S(2)}) collective-permute-start(f32[96,768]{1,0:T(8,128)S(1)} %add_add_fusion), channel_id=1, source_target_pairs={{0,2},{1,3},{2,0},{3,1},{4,6},{5,7},{6,4},{7,5},{8,10},{9,11},{10,... | collective-permute-start | bytes 884744 | tf_op jit(solution)/shard_map/ppermute | solution.py:539
  239.3 15.0 %collective-permute-start.49 = (f32[2,72,768]{2,1,0:T(8,128)S(1)}, f32[2,72,768]{2,1,0:T(8,128)S(1)}, u32[]{:S(2)}, u32[]{:S(2)}) collective-permute-start(f32[2,72,768]{2,1,0:T(8,128)S(1)} %get-tuple-element.1433), channel_id=1, source_target_pairs={{0,8},{4,12},{8,0},{12,4},{16,24},{20,28},{24,16},{28,20},{1,9},{5... | collective-permute-start | bytes 1327112 | tf_op jit(solution)/shard_map/ppermute | solution.py:543
  240.9 14.9 %collective-permute-start.48 = (f32[2,96,768]{2,1,0:T(8,128)S(1)}, f32[2,96,768]{2,1,0:T(8,128)S(1)}, u32[]{:S(2)}, u32[]{:S(2)}) collective-permute-start(f32[2,96,768]{2,1,0:T(8,128)S(1)} %get-tuple-element.1431), channel_id=1, source_target_pairs={{0,16},{4,20},{8,24},{12,28},{16,0},{20,4},{24,8},{28,12},{1,17},{... | collective-permute-start | bytes 1769480 | tf_op jit(solution)/shard_map/ppermute | solution.py:543
  256.0 16.1 %collective-permute-start.52 = (f32[192,768]{1,0:T(8,128)S(1)}, f32[192,768]{1,0:T(8,128)S(1)}, u32[]{:S(2)}, u32[]{:S(2)}) collective-permute-start(f32[192,768]{1,0:T(8,128)S(1)} %pad_maximum_fusion.17), channel_id=1, source_target_pairs={{0,8},{4,12},{8,0},{12,4},{16,24},{20,28},{24,16},{28,20},{1,9},{5... | collective-permute-start | bytes 1769480 | tf_op jit(solution)/shard_map/ppermute | solution.py:543
  256.7 17.9 %collective-permute-start.54 = (f32[4,72,768]{2,1,0:T(8,128)S(1)}, f32[4,72,768]{2,1,0:T(8,128)S(1)}, u32[]{:S(2)}, u32[]{:S(2)}) collective-permute-start(f32[4,72,768]{2,1,0:T(8,128)S(1)} %get-tuple-element.1344), channel_id=1, source_target_pairs={{0,4},{4,0},{8,12},{12,8},{16,20},{20,16},{24,28},{28,24},{1,5},{5... | collective-permute-start | bytes 2654216 | tf_op jit(solution)/shard_map/ppermute | solution.py:543
  256.7 17.8 %collective-permute-start.51 = (f32[224,768]{1,0:T(8,128)S(1)}, f32[224,768]{1,0:T(8,128)S(1)}, u32[]{:S(2)}, u32[]{:S(2)}) collective-permute-start(f32[224,768]{1,0:T(8,128)S(1)} %get-tuple-element.1331.refs_4_), channel_id=1, source_target_pairs={{0,1},{1,0},{2,3},{3,2},{4,5},{5,4},{6,7},{7,6},{8,9},{9,8},{10,11... | collective-permute-start | bytes 2064392 | tf_op jit(solution)/shard_map/ppermute | solution.py:539
  274.9 21.4 %collective-permute-start.57 = (f32[272,768]{1,0:T(8,128)S(1)}, f32[272,768]{1,0:T(8,128)S(1)}, u32[]{:S(2)}, u32[]{:S(2)}) collective-permute-start(f32[272,768]{1,0:T(8,128)S(1)} %pad_maximum_fusion.4), channel_id=1, source_target_pairs={{0,8},{4,12},{8,0},{12,4},{16,24},{20,28},{24,16},{28,20},{1,9},{5... | collective-permute-start | bytes 2506760 | tf_op jit(solution)/shard_map/ppermute | solution.py:543
  276.4 19.9 %collective-permute-start.58 = (f32[256,768]{1,0:T(8,128)S(1)}, f32[256,768]{1,0:T(8,128)S(1)}, u32[]{:S(2)}, u32[]{:S(2)}) collective-permute-start(f32[256,768]{1,0:T(8,128)S(1)} %pad_maximum_fusion.5), channel_id=1, source_target_pairs={{0,16},{4,20},{8,24},{12,28},{16,0},{20,4},{24,8},{28,12},{1,17},{... | collective-permute-start | bytes 2359304 | tf_op jit(solution)/shard_map/ppermute | solution.py:543
  277.6 18.7 %collective-permute-start.56 = (f32[208,768]{1,0:T(8,128)S(1)}, f32[208,768]{1,0:T(8,128)S(1)}, u32[]{:S(2)}, u32[]{:S(2)}) collective-permute-start(f32[208,768]{1,0:T(8,128)S(1)} %get-tuple-element.1357.refs_5_), channel_id=1, source_target_pairs={{0,1},{1,0},{2,3},{3,2},{4,5},{5,4},{6,7},{7,6},{8,9},{9,8},{10,11... | collective-permute-start | bytes 1916936 | tf_op jit(solution)/shard_map/ppermute | solution.py:539
  278.8 17.5 %collective-permute-start.60 = (f32[16,768]{1,0:T(8,128)S(1)}, f32[16,768]{1,0:T(8,128)S(1)}, u32[]{:S(2)}, u32[]{:S(2)}) collective-permute-start(f32[16,768]{1,0:T(8,128)S(1)} %add.244), channel_id=1, source_target_pairs={{0,8},{4,12},{8,0},{12,4},{16,24},{20,28},{24,16},{28,20},{1,9},{5... | collective-permute-start | bytes 147464 | tf_op jit(solution)/shard_map/ppermute | solution.py:543
  279.5 16.8 %collective-permute-start.59 = (f32[48,768]{1,0:T(8,128)S(1)}, f32[48,768]{1,0:T(8,128)S(1)}, u32[]{:S(2)}, u32[]{:S(2)}) collective-permute-start(f32[48,768]{1,0:T(8,128)S(1)} %pad_maximum_fusion.22), channel_id=1, source_target_pairs={{0,1},{1,0},{2,3},{3,2},{4,5},{5,4},{6,7},{7,6},{8,9},{9,8},{10,11... | collective-permute-start | bytes 442376 | tf_op jit(solution)/shard_map/ppermute | solution.py:539
  296.4 15.0 %collective-permute-start.65 = (f32[96,768]{1,0:T(8,128)S(1)}, f32[96,768]{1,0:T(8,128)S(1)}, u32[]{:S(2)}, u32[]{:S(2)}) collective-permute-start(f32[96,768]{1,0:T(8,128)S(1)} %pad_maximum_fusion.19), channel_id=1, source_target_pairs={{0,2},{1,3},{2,0},{3,1},{4,6},{5,7},{6,4},{7,5},{8,10},{9,11},{10,... | collective-permute-start | bytes 884744 | tf_op jit(solution)/shard_map/ppermute | solution.py:539
  312.9 15.5 %collective-permute-start.69 = (f32[96,768]{1,0:T(8,128)S(1)}, f32[96,768]{1,0:T(8,128)S(1)}, u32[]{:S(2)}, u32[]{:S(2)}) collective-permute-start(f32[96,768]{1,0:T(8,128)S(1)} %maximum_add_fusion), channel_id=1, source_target_pairs={{0,16},{4,20},{8,24},{12,28},{16,0},{20,4},{24,8},{28,12},{1,17},{... | collective-permute-start | bytes 884744 | tf_op jit(solution)/shard_map/ppermute | solution.py:543
  (124 other events, 1055.6 us)

commit v4 on v3

--- a/solution.py
+++ b/solution.py
@@ -632,7 +632,7 @@
         me1, qkv_t, out_weight, qkv_bias, up_bias, up_weight, down_weight
     )
 
-    n_gn = (224, 208, 80)
+    n_gn = (176, 136, 120, 80)
     n_q0 = 40
     numbers = jnp.arange(PIECES, dtype=jnp.int32)
     idx_a = storage_of(numbers ^ me, BITS_A).astype(jnp.int32)
@@ -923,13 +923,13 @@
 
     def c2u(k):
         k0, k1, g1, g0 = v[f"w{k}"]
-        q = v.pop(f"q{k + 1}u")
-        sent = k1[:upart] + q[upart:] + g1[:upart]
-        v[f"w{k}"] = (k0, k1, g1, g0, q, swap(sent, second_link(k)))
+        q0, q1 = v.pop(f"q{k + 1}u")
+        sent = k1[:upart] + q1 + g1[:upart]
+        v[f"w{k}"] = (k0, k1, g1, g0, q0, swap(sent, second_link(k)))
 
     def c2d(k):
         k0, k1, g1, g0, q, gu = v[f"w{k}"]
-        up_sum = k0[:upart] + g0[:upart] + q[:upart] + gu
+        up_sum = k0[:upart] + g0[:upart] + q + gu
         sent = k1[upart:] + g1[upart:]
         v[f"w{k}"] = (up_sum, k0[upart:], g0[upart:], swap(sent, second_link(k)))
 
@@ -983,6 +983,7 @@
     v["cot_p"] = swap(v.pop("cot_f"), core)
     v["m1"] = zswap(v["piece"], 1)
     v["mid_a"] = middle_swap(v.pop("piece"))
+    run_attn_own()
     v.fence()
     m1 = v["m1"]
     to_y = jnp.concatenate([*v["ta"], m1[upart:]], axis=0)
@@ -990,8 +991,7 @@
     v["ta"] = (to_y, swap(to_y, py))
     v["tb"] = (to_x, swap(to_x, px))
     v["mid_b"] = middle_swap(v.pop("m1"))
-    v["end_a"] = pass_out(v["mid_a"])
-    run_attn_own()
+    v["mix0"] = zswap(jnp.concatenate([v["st0"].pop("mixs"), v["mid_a"]], axis=0), 1)
     v.fence()
     nt = 2 * 3 * part
     ya, yb = v.pop("ta")
@@ -1008,12 +1008,12 @@
     )
     run_attn_far()
     g2("m1")
-    v["mix0"] = zswap(jnp.concatenate([v["st0"].pop("mixs"), v["mid_b"]], axis=0), 1)
+    v["end_b"] = pass_out(v["mid_b"])
     v.fence()
     v["mix2"] = zswap(v["st2"].pop("mixs"), 1)
     run_out()
-    m3 = jnp.where(inner, v.pop("mid_a"), v["mix0"][mix_rows:])
-    m2 = jnp.where(inner, v.pop("mid_b"), v.pop("end_a"))
+    m3 = jnp.where(inner, v.pop("mid_a"), v.pop("end_b"))
+    m2 = jnp.where(inner, v.pop("mid_b"), v["mix0"][mix_rows:])
     to_x = jnp.concatenate([m3[:upart], m2[:upart]], axis=0)
     to_y = jnp.concatenate([m3[upart:], m2[upart:]], axis=0)
     v["ma"], v["mb"] = (to_x, swap(to_x, px)), (to_y, swap(to_y, py))
@@ -1038,24 +1038,29 @@
     run_mlp(2, v.pop("m2a"), v.pop("m2b"), v["t2"], 4 * part // 8)
     e2(1)
     e2(3)
-    v["q1u"] = zswap(v["q1u"], 1)
+    q1u = v.pop("q1u")
+    v["q1x"] = zswap(q1u[:upart], 1)
+    v["q1r"] = q1u[upart:]
     v.fence()
     e3(1)
     e3(3)
-    v["d13"] = jnp.concatenate([v.pop("w1"), v.pop("w3")], axis=0)
-    v["q3u"] = zswap(v["q3u"], 1)
+    q3u = v.pop("q3u")
+    v["qm"] = zswap(jnp.concatenate([v.pop("q1r"), q3u[:upart]], axis=0), 1)
+    v["q3r"] = q3u[upart:]
     c1(0)
     c1(2)
     v["acc_own"], v["acc_far"] = run_down()
     v.fence()
     c0(0)
     c0(2)
-    v["d13"] = zswap(v["d13"], 1)
+    v["q3y"] = zswap(jnp.concatenate([v.pop("q3r"), v.pop("w3")], axis=0), 1)
     v["acc_got"] = swap(v.pop("acc_far"), core)
     v["low"] = run_mid()
     v.fence()
-    d13 = v.pop("d13")
-    v["d1"], v["d3"] = d13[:upart], d13[upart:]
+    qm = v.pop("qm")
+    q3y = v.pop("q3y")
+    v["q1u"], v["q3u"] = (v.pop("q1x"), qm[:upart]), (qm[upart:], q3y[:upart])
+    v["d3"] = q3y[upart:]
     c2u(0)
     c2u(2)
     v["gp2"] = zswap(v.pop("gmt3"), 1)
@@ -1070,13 +1075,14 @@
     r1("q2")
     r1("o")
     v.fence()
-    c3(0)
     c3(2)
+    v["d1"] = zswap(v.pop("w1"), 1)
     v["z2y"] = zswap(v.pop("w2")[1], 2)
     r2("q2", "b")
     r2("o", "a")
     run_attn_bwd(0, "gp0", idx_b, False)
     v.fence()
+    c3(0)
     up_sum, down_sum = v.pop("w0")
     ma = high_bits(up_sum + v.pop("z2x"))
     mb = high_bits(down_sum + v.pop("z2y"))
@@ -1124,9 +1130,11 @@
     to_y = jnp.concatenate([xa[:upart], xb[:upart], q0[1, n_q0:], q0[3, n_q0:]], axis=0)
     to_x = jnp.concatenate([ya[:upart], yb[:upart], q0[2, :n_q0], q0[3, :n_q0]], axis=0)
     v["gx"], v["gy"] = (to_x, swap(to_x, px)), (to_y, swap(to_y, py))
-    v["oz"] = zswap(jnp.concatenate([o[part : 2 * part], o[3 * part :]], axis=0), 1)
     v["o0"], v["o2"] = o[:part], o[2 * part : 3 * part]
-    v["gn1"] = zswap(v["gn_far"][1], 1)
+    v["gn1"] = zswap(
+        jnp.concatenate([v["gn_far"][1], o[part : 2 * part], o[3 * part :]], axis=0), 1
+    )
+    v["yq"] = zswap(v.pop("q2"), 2)
     v["small"] = v["small"] + swap(v["small"], px)
     v.fence()
     (xa, xb), (ya, yb) = v.pop("gx"), v.pop("gy")
@@ -1138,20 +1146,22 @@
     ]
     v["q0b"] = (q0b[0], swap(q0b[1], py))
     v["q0a"] = (q0a[0], swap(q0a[1], px))
-    oz = v.pop("oz")
+    oz = v["gn1"][n_gn[1] :]
     v["o0"] = v["o0"] + oz[:part]
-    v["y2"] = zswap(jnp.concatenate([v.pop("q2"), v.pop("o2") + oz[part:]], axis=0), 2)
-    v["gn2"] = zswap(v.pop("gn_far")[2], 1)
+    v["yo"] = zswap(v.pop("o2") + oz[part:], 2)
+    v["gn2"] = zswap(v["gn_far"][2], 1)
     v["small"] = v["small"] + swap(v["small"], py)
     n2 = 2 * upart
     v["mlp"] = jnp.concatenate([ya[:n2], yb[:n2], xa[:n2], xb[:n2]], axis=0)
     v.fence()
     q0 = jnp.concatenate([a + b for a, b in (v.pop("q0b"), v.pop("q0a"))], axis=0)
-    att_sum = high_bits(jnp.concatenate([q0, v.pop("o0")], axis=0) + v.pop("y2"))
+    att_sum = high_bits(
+        jnp.concatenate([q0 + v.pop("yq"), v.pop("o0") + v.pop("yo")], axis=0)
+    )
     v["w"] = (att_sum, swap(att_sum, px), swap(att_sum, py), swap(att_sum, px | py))
     small = high_bits(v.pop("small"))
-    got = zswap(jnp.concatenate([small[:8], small[12:]], axis=0), 1)
-    v["small"] = small[:12] + got
+    v["gn3"] = zswap(jnp.concatenate([v.pop("gn_far")[3], small[:8], small[12:]], axis=0), 1)
+    v["small"] = small[:12] + v["gn3"][n_gn[3] :]
 
     mlp = v.pop("mlp")
     v["up_g"], v["down_g"] = call(
@@ -1162,7 +1172,8 @@
         out_specs=(vmem,) * 2,
         scratch_shapes=[pltpu.VMEM((2, PIECES, upart, width), F32)],
     )(idx_a, idx_b, mlp, swap(mlp, core))
-    v["input_grad"] = call(
+    v.fence()
+    input_grad = call(
         final_kernel,
         sds((share, width), BF16),
         flops=share * width * 20,
@@ -1179,8 +1190,7 @@
             ],
             out_specs=pl.BlockSpec((share, width), const2),
         ),
-    )(blk, tokens, v["gn_own"], *[v[f"gn{i}"] for i in range(3)], v["gm"], row1(norm1_gain))
-    v.fence()
+    )(blk, tokens, v["gn_own"], *[v[f"gn{i}"] for i in range(4)], v["gm"], row1(norm1_gain))
     w = jnp.concatenate(v.pop("w"), axis=0)
     small = v.pop("small")
     small_got = zswap(jnp.concatenate([small[:8], small[10:]], axis=0), 2)
@@ -1193,8 +1203,8 @@
         scratch_shapes=[pltpu.VMEM((PIECES, 4 * part, width), F32)],
     )(idx_a, w, swap(w, core))
     qkv_weight_grad = jnp.swapaxes(qkv_weight_grad, 1, 2)
-    qkv_weight_grad, out_weight_grad, small, small_got = lax.optimization_barrier(
-        (qkv_weight_grad, out_weight_grad, small, small_got)
+    qkv_weight_grad, out_weight_grad, input_grad, small, small_got = lax.optimization_barrier(
+        (qkv_weight_grad, out_weight_grad, input_grad, small, small_got)
     )
     qkv_bias_grad, *rows_of = call(
         small_out_kernel,
@@ -1206,7 +1216,7 @@
     heads_of, rows_of = rows_of[:3], rows_of[3:]
     return (
         v["block_out"],
-        v["input_grad"],
+        input_grad,
         qkv_weight_grad,
         qkv_bias_grad,
         out_weight_grad,

time: 339 us -> 337 us (level)
  waiting for transfers between devices: 149 us -> 129 us
  starting transfers between devices: 67.8 us -> 82.8 us
    ppermute x1, waiting for transfers between devices: 14.2 us -> 3.12 us  [pass_out(): return lax.ppermute(a, 'mp', [(1, 0), (2, 3)])]
    ppermute x22 -> x23, starting transfers between devices: 24.2 us -> 34.9 us  [swap_mp(): return lax.ppermute(a, 'mp', [(s, s ^ k) for s in range(size)])]
    ppermute x22 -> x23, waiting for transfers between devices: 59.5 us -> 50.7 us  [swap_mp(): return lax.ppermute(a, 'mp', [(s, s ^ k) for s in range(size)])]
    ppermute x48, starting transfers between devices: 40.7 us -> 44.2 us  [swap_plane(): return lax.ppermute(a, 'dp', [(d, d ^ bit) for d in range(size)])]
    unnamed x165 -> x171, local copies, waits for them, and re-layouts: 5.5 us -> 7.42 us
  transfers between devices with their start and end apart: 73 -> 74, of which waited for: 47 -> 43; matrix products, arithmetic and copies ran while one was open for 4% -> 4% of each run, Pallas kernels for 26% -> 26%
where the time goes in v4:
time: 337 us; the launch traced here: 331 us
  waiting for transfers between devices  129 us (38%)
  Pallas kernels  90.4 us (27%)
  starting transfers between devices  82.8 us (25%)
  other arithmetic  15.8 us (5%)
  local copies, waits for them, and re-layouts  10.3 us (3%)
    ppermute x48, waiting for transfers between devices, swap_plane(): return lax.ppermute(a, 'dp', [(d, d ^ bit) for d in range(size)])  74.9 us
    ppermute x23, waiting for transfers between devices, swap_mp(): return lax.ppermute(a, 'mp', [(s, s ^ k) for s in range(size)])  50.7 us
    ppermute x48, starting transfers between devices, swap_plane(): return lax.ppermute(a, 'dp', [(d, d ^ bit) for d in range(size)])  44.2 us
    ppermute x23, starting transfers between devices, swap_mp(): return lax.ppermute(a, 'mp', [(s, s ^ k) for s in range(size)])  34.9 us
    pallas_call x2, Pallas kernels, run_attn_bwd(): call(functools.partial(attn_bwd_kernel, 0 if first else len(cuts_now)), (...  24.3 us
    pallas_call x4, Pallas kernels, run_mlp(): call(functools.partial(mlp_kernel, MLP_KIND[k], keeps), shapes, flops=2 *...  21.3 us
    unnamed x171, local copies, waits for them, and re-layouts  7.42 us
    pallas_call x1, Pallas kernels, run_attn_far(): call(attn_fwd_kernel, tuple(shapes), flops=2 * (full * width * e * 3 + fu...  7.12 us
  transfers between devices with their start and end apart: 74, of which 43 were waited for; matrix products, arithmetic and copies ran while one was open for 4% of the time, Pallas kernels for 26%

profile of v4, /device:TPU:0, one launch (start us, length us, event | category | flops | bytes accessed | tf_op | source)
XLA Modules:
  0.0 330.7 jit_solution(13239569749203209829)
XLA Ops:
  0.7 4.2 %shard_map.305 = (f32[104,768]{1,0:T(8,128)}, f32[32,768]{1,0:T(8,128)}, f32[8,768]{1,0:T(8,128)}, f32[192,768]{1,0:T(8,128)}, bf16[2,96,768]{2,1,0:T(8,128)(2,1...) custom-call(s32[1]{0:T(128)} %bitcast.me_ref, ...), custom_call_target="tpu_custom_call" | custom-call | bytes 9000000 | tf_op jit(solution)/shard_map/pallas_call | solution.py:617
  4.9 4.0 %collective-permute-start.2 = (f32[104,768]{1,0:T(8,128)}, f32[104,768]{1,0:T(8,128)S(1)}, u32[]{:S(2)}, u32[]{:S(2)}) collective-permute-start(f32[104,768]{1,0:T(8,128)} %get-tuple-element.755), channel_id=1, source_target_pairs={{0,2},{1,3},{2,0},{3,1},{4,6},{5,7},{6,4},{7,5},{8,10},{9,11},{10,... | collective-permute-start | bytes 958472 | tf_op jit(solution)/shard_map/ppermute | solution.py:539
  12.5 3.3 fusion.7
  15.8 3.5 %collective-permute-done.b_ref = f32[32,768]{1,0:T(8,128)} collective-permute-done((f32[32,768]{1,0:T(8,128)}, f32[32,768]{1,0:T(8,128)}, u32[]{:S(2)}, u32[]{:S(2)}) %collective-permute-start) | collective-permute-done | bytes 98336 | tf_op jit(solution)/shard_map/ppermute | solution.py:539
  19.2 2.9 collective-permute-done.1.b_ref
  22.1 4.3 %collective-permute-done.2.b_ref = f32[104,768]{1,0:T(8,128)S(1)} collective-permute-done((f32[104,768]{1,0:T(8,128)}, f32[104,768]{1,0:T(8,128)S(1)}, u32[]{:S(2)}, u32[]{:S(2)}) %collective-permute-start.2) | collective-permute-done | bytes 319520 | tf_op jit(solution)/shard_map/ppermute | solution.py:539
  36.0 4.9 %shard_map.307 = (f32[192,1024]{1,0:T(8,128)S(1)}, f32[192,1024]{1,0:T(8,128)S(1)}, bf16[192,1024]{1,0:T(8,128)(2,1)S(1)}, bf16[192,512]{1,0:T(8,128)(2,1)S(1)},...) custom-call(bf16[1024,768]{1,0:T(8,128)(2,1)S(1)} %copy-done.6, ...), custom_call_target="tpu_custom_call" | custom-call | flops 4127195136 | bytes 10000000 | tf_op jit(solution)/shard_map/pallas_call | solution.py:701
  43.5 4.6 %collective-permute-start.9 = (f32[320,768]{1,0:T(8,128)S(1)}, f32[320,768]{1,0:T(8,128)S(1)}, u32[]{:S(2)}, u32[]{:S(2)}) collective-permute-start(f32[320,768]{1,0:T(8,128)S(1)} %pad_maximum_fusion.1), channel_id=1, source_target_pairs={{0,1},{1,0},{2,3},{3,2},{4,5},{5,4},{6,7},{7,6},{8,9},{9,8},{10,11... | collective-permute-start | bytes 2949128 | tf_op jit(solution)/shard_map/ppermute | solution.py:539
  52.8 13.4 %collective-permute-done.11 = f32[240,768]{1,0:T(8,128)S(1)} collective-permute-done((f32[240,768]{1,0:T(8,128)S(1)}, f32[240,768]{1,0:T(8,128)S(1)}, u32[]{:S(2)}, u32[]{:S(2)}) %collective-permute-start.11) | collective-permute-done | bytes 737312 | tf_op jit(solution)/shard_map/ppermute | solution.py:543
  83.3 7.1 %shard_map.308 = (bf16[576,768]{1,0:T(8,128)(2,1)S(1)}, bf16[192,768]{1,0:T(8,128)(2,1)S(1)}, bf16[192,768]{1,0:T(8,128)(2,1)S(1)}, bf16[192,768]{1,0:T(8,128)(2...) custom-call(s32[8]{0:T(128)S(1)} %get-tuple-element.1545.ia_ref.idx_, ...), custom_call_target="tpu_custom_call" | custom-call | flops 4127195136 | bytes 10000000 | tf_op jit(solution)/shard_map/pallas_call | solution.py:721
  91.3 3.1 collective-permute-done.12
  98.5 7.8 %collective-permute-done.19.refs_3_ = f32[128,768]{1,0:T(8,128)S(1)} collective-permute-done((f32[128,768]{1,0:T(8,128)S(1)}, f32[128,768]{1,0:T(8,128)S(1)}, u32[]{:S(2)}, u32[]{:S(2)}) %collective-permute-start.19) | collective-permute-done | bytes 393248 | tf_op jit(solution)/shard_map/ppermute | solution.py:539
  113.4 5.3 %shard_map.310 = (bf16[1024,384]{1,0:T(8,128)(2,1)S(1)}, bf16[1024,384]{1,0:T(8,128)(2,1)S(1)}, bf16[384,768]{1,0:T(8,128)(2,1)S(1)}, bf16[384,768]{1,0:T(8,128)...) custom-call(bf16[512,768]{1,0:T(8,128)(2,1)S(1)} %get-tuple-element., ...), custom_call_target="tpu_custom_call" | custom-call | flops 2415919104 | bytes 12000000 | tf_op jit(solution)/shard_map/pallas_call | solution.py:776
  119.5 6.5 %collective-permute-done.22.d1_ref = f32[2,96,768]{2,1,0:T(8,128)S(1)} collective-permute-done((f32[2,96,768]{2,1,0:T(8,128)S(1)}, f32[2,96,768]{2,1,0:T(8,128)S(1)}, u32[]{:S(2)}, u32[]{:S(2)}) %collective-permute-start.22) | collective-permute-done | bytes 589856 | tf_op jit(solution)/shard_map/ppermute | solution.py:543
  131.8 5.1 %shard_map.311 = (bf16[1024,384]{1,0:T(8,128)(2,1)S(1)}, bf16[1024,384]{1,0:T(8,128)(2,1)S(1)}, bf16[384,768]{1,0:T(8,128)(2,1)S(1)}, bf16[384,768]{1,0:T(8,128)...) custom-call(bf16[512,768]{1,0:T(8,128)(2,1)S(1)} %get-tuple-element., ...), custom_call_target="tpu_custom_call" | custom-call | flops 2415919104 | bytes 12000000 | tf_op jit(solution)/shard_map/pallas_call | solution.py:776
  136.9 4.3 %collective-permute-done.24.d1_ref = f32[2,96,768]{2,1,0:T(8,128)S(1)} collective-permute-done((f32[2,96,768]{2,1,0:T(8,128)S(1)}, f32[2,96,768]{2,1,0:T(8,128)S(1)}, u32[]{:S(2)}, u32[]{:S(2)}) %collective-permute-start.24) | collective-permute-done | bytes 589856 | tf_op jit(solution)/shard_map/ppermute | solution.py:543
  147.0 5.6 %shard_map.312 = (bf16[1024,384]{1,0:T(8,128)(2,1)S(1)}, bf16[1024,384]{1,0:T(8,128)(2,1)S(1)}, bf16[384,768]{1,0:T(8,128)(2,1)S(1)}, bf16[384,768]{1,0:T(8,128)...) custom-call(bf16[512,768]{1,0:T(8,128)(2,1)S(1)} %get-tuple-element., ...), custom_call_target="tpu_custom_call" | custom-call | flops 2415919104 | bytes 12000000 | tf_op jit(solution)/shard_map/pallas_call | solution.py:776
  152.6 5.1 %collective-permute-done.26.refs_0_ = f32[192,768]{1,0:T(8,128)S(1)} collective-permute-done((f32[192,768]{1,0:T(8,128)S(1)}, f32[192,768]{1,0:T(8,128)S(1)}, u32[]{:S(2)}, u32[]{:S(2)}) %collective-permute-start.26) | collective-permute-done | bytes 589856 | tf_op jit(solution)/shard_map/ppermute | solution.py:539
  162.1 5.4 %shard_map.313 = (bf16[1024,384]{1,0:T(8,128)(2,1)S(1)}, bf16[1024,384]{1,0:T(8,128)(2,1)S(1)}, bf16[384,768]{1,0:T(8,128)(2,1)S(1)}, bf16[384,768]{1,0:T(8,128)...) custom-call(bf16[512,768]{1,0:T(8,128)(2,1)S(1)} %get-tuple-element., ...), custom_call_target="tpu_custom_call" | custom-call | flops 2415919104 | bytes 12000000 | tf_op jit(solution)/shard_map/pallas_call | solution.py:776
  173.8 6.7 %shard_map.314 = (f32[2,512,768]{2,1,0:T(8,128)S(1)}, f32[2,512,768]{2,1,0:T(8,128)}) custom-call(bf16[1024,384]{1,0:T(8,128)(2,1)S(1)} %copy-done.42, bf16[1024,384]{1,0:T(8,128)(2,1)S(1)} %copy-done.34, bf16[1024,384]{1,0:T(8,128)(2,1)S(1)} %get-tuple-element.1097.refs_2_, bf16[1024,384]{1,0:T(8,128)(2,1)S(1)} %get-tuple-element.1098.refs_3_, ...), custom_call_target="tpu_custom_call" | custom-call | flops 4831838208 | bytes 17000000 | tf_op jit(solution)/shard_map/pallas_call | solution.py:794
  187.6 3.4 %shard_map.315 = (bf16[192,512]{1,0:T(8,128)(2,1)S(1)}, f32[192,512]{1,0:T(8,128)S(1)}, bf16[192,512]{1,0:T(8,128)(2,1)S(1)}, f32[192,512]{1,0:T(8,128)S(1)}, bf...) custom-call(f32[512,768]{1,0:T(8,128)S(1)} %get-tuple-element.1155.mid_ref, ...), custom_call_target="tpu_custom_call" | custom-call | flops 603979776 | bytes 12000000 | tf_op jit(solution)/shard_map/pallas_call | solution.py:813
  190.9 6.6 %collective-permute-done.36 = f32[192,768]{1,0:T(8,128)S(1)} collective-permute-done((f32[192,768]{1,0:T(8,128)S(1)}, f32[192,768]{1,0:T(8,128)S(1)}, u32[]{:S(2)}, u32[]{:S(2)}) %collective-permute-start.36) | collective-permute-done | bytes 589856 | tf_op jit(solution)/shard_map/ppermute | solution.py:539
  218.4 12.1 %shard_map.317 = (f32[4,72,768]{2,1,0:T(8,128)S(1)}, f32[4,72,768]{2,1,0:T(8,128)S(1)}, f32[1024,768]{1,0:T(8,128)S(1)}, f32[3,64,128]{2,1,0:T(8,128)S(1)}, f32[576,128]{1,0:T(8,128)S(1)}) custom-call(s32[8]{0:T(128)S(1)} %get-tuple-element.1546.ib_ref.idx_ref, bf16[1024,768]{1,0:T(8,128)(2,1)S(1)} %copy-done.8, f32[192,1024]{1,0:T(8,128)S(1)} %copy-done.50, ...), custom_call_target="tpu_custom_call" | custom-call | flops 9865003008 | bytes 14000000 | tf_op jit(solution)/shard_map/pallas_call | solution.py:855
  231.9 3.6 %collective-permute-done.47 = f32[4,72,768]{2,1,0:T(8,128)S(1)} collective-permute-done((f32[4,72,768]{2,1,0:T(8,128)S(1)}, f32[4,72,768]{2,1,0:T(8,128)S(1)}, u32[]{:S(2)}, u32[]{:S(2)}) %collective-permute-start.47) | collective-permute-done | bytes 884768 | tf_op jit(solution)/shard_map/ppermute | solution.py:543
  240.8 12.2 %shard_map.318 = (f32[4,72,768]{2,1,0:T(8,128)S(1)}, f32[4,72,768]{2,1,0:T(8,128)S(1)}, f32[512,768]{1,0:T(8,128)S(1)}, f32[176,768]{1,0:T(8,128)S(1)}, f32[136,...) custom-call(s32[8]{0:T(128)S(1)} %get-tuple-element.1546.ib_ref.idx_, ...), custom_call_target="tpu_custom_call" | custom-call | flops 9865003008 | bytes 14000000 | tf_op jit(solution)/shard_map/pallas_call | solution.py:855
  256.7 2.8 shard_map.319
  260.8 8.5 %collective-permute-done.54 = f32[168,768]{1,0:T(8,128)S(1)} collective-permute-done((f32[168,768]{1,0:T(8,128)S(1)}, f32[168,768]{1,0:T(8,128)S(1)}, u32[]{:S(2)}, u32[]{:S(2)}) %collective-permute-start.54) | collective-permute-done | bytes 516128 | tf_op jit(solution)/shard_map/ppermute | solution.py:543
  276.3 15.5 %collective-permute-done.60 = f32[16,768]{1,0:T(8,128)S(1)} collective-permute-done((f32[16,768]{1,0:T(8,128)S(1)}, f32[16,768]{1,0:T(8,128)S(1)}, u32[]{:S(2)}, u32[]{:S(2)}) %collective-permute-start.60) | collective-permute-done | bytes 49184 | tf_op jit(solution)/shard_map/ppermute | solution.py:543
  299.0 4.5 %collective-permute-done.66 = f32[24,768]{1,0:T(8,128)S(1)} collective-permute-done((f32[24,768]{1,0:T(8,128)S(1)}, f32[24,768]{1,0:T(8,128)S(1)}, u32[]{:S(2)}, u32[]{:S(2)}) %collective-permute-start.66) | collective-permute-done | bytes 73760 | tf_op jit(solution)/shard_map/ppermute | solution.py:539
  310.9 4.0 %collective-permute-done.68.refs_3_ = f32[92,768]{1,0:T(8,128)S(1)} collective-permute-done((f32[92,768]{1,0:T(8,128)S(1)}, f32[92,768]{1,0:T(8,128)S(1)}, u32[]{:S(2)}, u32[]{:S(2)}) %collective-permute-start.68) | collective-permute-done | bytes 282656 | tf_op jit(solution)/shard_map/ppermute | solution.py:539
  314.9 3.7 %shard_map.320 = (f32[768,768]{1,0:T(8,128)}, f32[768,768]{1,0:T(8,128)}) custom-call(s32[8]{0:T(128)S(1)} %get-tuple-element.1545.ia_ref.idx_ref.i_ref, s32[8]{0:T(128)S(1)} %get-tuple-element.1546.ib_ref.idx_ref, f32[768,768]{1,0:T(8,128)S(1)} %pad_maximum_fusion.a_ref, f32[768,768]{1,0:T(8,128)S(1)} %collective-permute-done.67.b_ref), custom_call_target="tpu_custom_call" | custom-call | bytes 10000000 | tf_op jit(solution)/shard_map/pallas_call | solution.py:1167
  318.6 4.8 %collective-permute-done.71 = f32[96,768]{1,0:T(8,128)S(1)} collective-permute-done((f32[96,768]{1,0:T(8,128)S(1)}, f32[96,768]{1,0:T(8,128)S(1)}, u32[]{:S(2)}, u32[]{:S(2)}) %collective-permute-start.71) | collective-permute-done | bytes 294944 | tf_op jit(solution)/shard_map/ppermute | solution.py:543
  (418 shorter events, 139.2 us)
Async XLA Ops:
  4.9 21.6 %collective-permute-start.2 = (f32[104,768]{1,0:T(8,128)}, f32[104,768]{1,0:T(8,128)S(1)}, u32[]{:S(2)}, u32[]{:S(2)}) collective-permute-start(f32[104,768]{1,0:T(8,128)} %get-tuple-element.755), channel_id=1, source_target_pairs={{0,2},{1,3},{2,0},{3,1},{4,6},{5,7},{6,4},{7,5},{8,10},{9,11},{10,... | collective-permute-start | bytes 958472 | tf_op jit(solution)/shard_map/ppermute | solution.py:539
  26.4 16.9 %collective-permute-start.3 = (f32[512,768]{1,0:T(8,128)}, f32[512,768]{1,0:T(8,128)}, u32[]{:S(2)}, u32[]{:S(2)}) collective-permute-start(f32[512,768]{1,0:T(8,128)} %get-tuple-element.757), channel_id=1, source_target_pairs={{0,4},{4,0},{8,12},{12,8},{16,20},{20,16},{24,28},{28,24},{1,5},{5... | collective-permute-start | bytes 4718600 | tf_op jit(solution)/shard_map/ppermute | solution.py:543
  27.0 16.4 %collective-permute-start.4 = (f32[192,768]{1,0:T(8,128)}, f32[192,768]{1,0:T(8,128)S(1)}, u32[]{:S(2)}, u32[]{:S(2)}) collective-permute-start(f32[192,768]{1,0:T(8,128)} %get-tuple-element.758), channel_id=1, source_target_pairs={{0,1},{1,0},{2,3},{3,2},{4,5},{5,4},{6,7},{7,6},{8,9},{9,8},{10,11... | collective-permute-start | bytes 1769480 | tf_op jit(solution)/shard_map/ppermute | solution.py:539
  43.5 26.4 %collective-permute-start.9 = (f32[320,768]{1,0:T(8,128)S(1)}, f32[320,768]{1,0:T(8,128)S(1)}, u32[]{:S(2)}, u32[]{:S(2)}) collective-permute-start(f32[320,768]{1,0:T(8,128)S(1)} %pad_maximum_fusion.1), channel_id=1, source_target_pairs={{0,1},{1,0},{2,3},{3,2},{4,5},{5,4},{6,7},{7,6},{8,9},{9,8},{10,11... | collective-permute-start | bytes 2949128 | tf_op jit(solution)/shard_map/ppermute | solution.py:539
  48.1 18.1 %collective-permute-start.11 = (f32[240,768]{1,0:T(8,128)S(1)}, f32[240,768]{1,0:T(8,128)S(1)}, u32[]{:S(2)}, u32[]{:S(2)}) collective-permute-start(f32[240,768]{1,0:T(8,128)S(1)} %pad_maximum_fusion.7), channel_id=1, source_target_pairs={{0,8},{4,12},{8,0},{12,4},{16,24},{20,28},{24,16},{28,20},{1,9},{5... | collective-permute-start | bytes 2211848 | tf_op jit(solution)/shard_map/ppermute | solution.py:543
  49.8 17.8 %collective-permute-start.10 = (f32[240,768]{1,0:T(8,128)S(1)}, f32[240,768]{1,0:T(8,128)S(1)}, u32[]{:S(2)}, u32[]{:S(2)}) collective-permute-start(f32[240,768]{1,0:T(8,128)S(1)} %pad_maximum_fusion.6), channel_id=1, source_target_pairs={{0,16},{4,20},{8,24},{12,28},{16,0},{20,4},{24,8},{28,12},{1,17},{... | collective-permute-start | bytes 2211848 | tf_op jit(solution)/shard_map/ppermute | solution.py:543
  73.6 16.9 %collective-permute-start.14 = (f32[2,96,768]{2,1,0:T(8,128)}, f32[2,96,768]{2,1,0:T(8,128)}, u32[]{:S(2)}, u32[]{:S(2)}) collective-permute-start(f32[2,96,768]{2,1,0:T(8,128)} %pad_maximum_fusion.9.d0_ref), channel_id=1, source_target_pairs={{0,8},{4,12},{8,0},{12,4},{16,24},{20,28},{24,16},{28,20},{1,9},{5... | collective-permute-start | bytes 1769480 | tf_op jit(solution)/shard_map/ppermute | solution.py:543
  76.0 15.3 %collective-permute-start.13 = (f32[2,96,768]{2,1,0:T(8,128)}, f32[2,96,768]{2,1,0:T(8,128)}, u32[]{:S(2)}, u32[]{:S(2)}) collective-permute-start(f32[2,96,768]{2,1,0:T(8,128)} %pad_maximum_fusion.8.u0_ref), channel_id=1, source_target_pairs={{0,16},{4,20},{8,24},{12,28},{16,0},{20,4},{24,8},{28,12},{1,17},{... | collective-permute-start | bytes 1769480 | tf_op jit(solution)/shard_map/ppermute | solution.py:543
  77.5 16.9 %collective-permute-start.12 = (f32[192,768]{1,0:T(8,128)}, f32[192,768]{1,0:T(8,128)}, u32[]{:S(2)}, u32[]{:S(2)}) collective-permute-start(f32[192,768]{1,0:T(8,128)} %collective-permute-done.8), channel_id=1, source_target_pairs={{1,0},{2,3},{5,4},{6,7},{9,8},{10,11},{13,12},{14,15},{17,16},{18,... | collective-permute-start | bytes 1769480 | tf_op jit(solution)/shard_map/ppermute | solution.py:958
  110.2 15.8 %collective-permute-start.22 = (f32[2,96,768]{2,1,0:T(8,128)S(1)}, f32[2,96,768]{2,1,0:T(8,128)S(1)}, u32[]{:S(2)}, u32[]{:S(2)}) collective-permute-start(f32[2,96,768]{2,1,0:T(8,128)S(1)} %pad_maximum_fusion.13.d0_ref), channel_id=1, source_target_pairs={{0,8},{4,12},{8,0},{12,4},{16,24},{20,28},{24,16},{28,20},{1,9},{5... | collective-permute-start | bytes 1769480 | tf_op jit(solution)/shard_map/ppermute | solution.py:543
  110.9 15.5 %collective-permute-start.21 = (f32[2,96,768]{2,1,0:T(8,128)S(1)}, f32[2,96,768]{2,1,0:T(8,128)S(1)}, u32[]{:S(2)}, u32[]{:S(2)}) collective-permute-start(f32[2,96,768]{2,1,0:T(8,128)S(1)} %pad_maximum_fusion.12.u0_ref), channel_id=1, source_target_pairs={{0,16},{4,20},{8,24},{12,28},{16,0},{20,4},{24,8},{28,12},{1,17},{... | collective-permute-start | bytes 1769480 | tf_op jit(solution)/shard_map/ppermute | solution.py:543
  126.5 14.7 %collective-permute-start.24 = (f32[2,96,768]{2,1,0:T(8,128)S(1)}, f32[2,96,768]{2,1,0:T(8,128)S(1)}, u32[]{:S(2)}, u32[]{:S(2)}) collective-permute-start(f32[2,96,768]{2,1,0:T(8,128)S(1)} %pad_maximum_fusion.15.d0_ref), channel_id=1, source_target_pairs={{0,8},{4,12},{8,0},{12,4},{16,24},{20,28},{24,16},{28,20},{1,9},{5... | collective-permute-start | bytes 1769480 | tf_op jit(solution)/shard_map/ppermute | solution.py:543
  128.1 14.4 %collective-permute-start.23 = (f32[2,96,768]{2,1,0:T(8,128)S(1)}, f32[2,96,768]{2,1,0:T(8,128)S(1)}, u32[]{:S(2)}, u32[]{:S(2)}) collective-permute-start(f32[2,96,768]{2,1,0:T(8,128)S(1)} %pad_maximum_fusion.14.u0_ref), channel_id=1, source_target_pairs={{0,16},{4,20},{8,24},{12,28},{16,0},{20,4},{24,8},{28,12},{1,17},{... | collective-permute-start | bytes 1769480 | tf_op jit(solution)/shard_map/ppermute | solution.py:543
  129.7 14.5 %collective-permute-start.25 = (f32[192,768]{1,0:T(8,128)S(1)}, f32[192,768]{1,0:T(8,128)S(1)}, u32[]{:S(2)}, u32[]{:S(2)}) collective-permute-start(f32[192,768]{1,0:T(8,128)S(1)} %get-tuple-element.932), channel_id=1, source_target_pairs={{0,1},{1,0},{2,3},{3,2},{4,5},{5,4},{6,7},{7,6},{8,9},{9,8},{10,11... | collective-permute-start | bytes 1769480 | tf_op jit(solution)/shard_map/ppermute | solution.py:539
  181.7 15.8 %collective-permute-start.36 = (f32[192,768]{1,0:T(8,128)S(1)}, f32[192,768]{1,0:T(8,128)S(1)}, u32[]{:S(2)}, u32[]{:S(2)}) collective-permute-start(f32[192,768]{1,0:T(8,128)S(1)} %pad_maximum_fusion.17), channel_id=1, source_target_pairs={{0,1},{1,0},{2,3},{3,2},{4,5},{5,4},{6,7},{7,6},{8,9},{9,8},{10,11... | collective-permute-start | bytes 1769480 | tf_op jit(solution)/shard_map/ppermute | solution.py:539
  183.2 15.7 %collective-permute-start.37 = (f32[192,768]{1,0:T(8,128)}, f32[192,768]{1,0:T(8,128)S(1)}, u32[]{:S(2)}, u32[]{:S(2)}) collective-permute-start(f32[192,768]{1,0:T(8,128)} %get-tuple-element.1199), channel_id=1, source_target_pairs={{0,16},{4,20},{8,24},{12,28},{16,0},{20,4},{24,8},{28,12},{1,17},{... | collective-permute-start | bytes 1769480 | tf_op jit(solution)/shard_map/ppermute | solution.py:543
  184.8 15.4 %collective-permute-start.38 = (f32[192,768]{1,0:T(8,128)}, f32[192,768]{1,0:T(8,128)S(1)}, u32[]{:S(2)}, u32[]{:S(2)}) collective-permute-start(f32[192,768]{1,0:T(8,128)} %get-tuple-element.1204), channel_id=1, source_target_pairs={{0,8},{4,12},{8,0},{12,4},{16,24},{20,28},{24,16},{28,20},{1,9},{5... | collective-permute-start | bytes 1769480 | tf_op jit(solution)/shard_map/ppermute | solution.py:543
  213.9 16.8 %collective-permute-start.44 = (f32[96,768]{1,0:T(8,128)S(1)}, f32[96,768]{1,0:T(8,128)S(1)}, u32[]{:S(2)}, u32[]{:S(2)}) collective-permute-start(f32[96,768]{1,0:T(8,128)S(1)} %slice_add_fusion.5), channel_id=1, source_target_pairs={{0,16},{4,20},{8,24},{12,28},{16,0},{20,4},{24,8},{28,12},{1,17},{... | collective-permute-start | bytes 884744 | tf_op jit(solution)/shard_map/ppermute | solution.py:543
  214.7 16.1 %collective-permute-start.45 = (f32[96,768]{1,0:T(8,128)S(1)}, f32[96,768]{1,0:T(8,128)S(1)}, u32[]{:S(2)}, u32[]{:S(2)}) collective-permute-start(f32[96,768]{1,0:T(8,128)S(1)} %get-tuple-element.1502), channel_id=1, source_target_pairs={{0,2},{1,3},{2,0},{3,1},{4,6},{5,7},{6,4},{7,5},{8,10},{9,11},{10,... | collective-permute-start | bytes 884744 | tf_op jit(solution)/shard_map/ppermute | solution.py:539
  235.6 17.4 %collective-permute-start.51 = (f32[96,768]{1,0:T(8,128)S(1)}, f32[96,768]{1,0:T(8,128)S(1)}, u32[]{:S(2)}, u32[]{:S(2)}) collective-permute-start(f32[96,768]{1,0:T(8,128)S(1)} %add_add_fusion.1), channel_id=1, source_target_pairs={{0,2},{1,3},{2,0},{3,1},{4,6},{5,7},{6,4},{7,5},{8,10},{9,11},{10,... | collective-permute-start | bytes 884744 | tf_op jit(solution)/shard_map/ppermute | solution.py:539
  236.0 17.6 %collective-permute-start.50 = (f32[2,72,768]{2,1,0:T(8,128)S(1)}, f32[2,72,768]{2,1,0:T(8,128)S(1)}, u32[]{:S(2)}, u32[]{:S(2)}) collective-permute-start(f32[2,72,768]{2,1,0:T(8,128)S(1)} %get-tuple-element.1485), channel_id=1, source_target_pairs={{0,8},{4,12},{8,0},{12,4},{16,24},{20,28},{24,16},{28,20},{1,9},{5... | collective-permute-start | bytes 1327112 | tf_op jit(solution)/shard_map/ppermute | solution.py:543
  237.7 15.9 %collective-permute-start.49 = (f32[2,96,768]{2,1,0:T(8,128)S(1)}, f32[2,96,768]{2,1,0:T(8,128)S(1)}, u32[]{:S(2)}, u32[]{:S(2)}) collective-permute-start(f32[2,96,768]{2,1,0:T(8,128)S(1)} %get-tuple-element.1483), channel_id=1, source_target_pairs={{0,16},{4,20},{8,24},{12,28},{16,0},{20,4},{24,8},{28,12},{1,17},{... | collective-permute-start | bytes 1769480 | tf_op jit(solution)/shard_map/ppermute | solution.py:543
  239.1 14.4 %collective-permute-start.48 = (f32[96,768]{1,0:T(8,128)S(1)}, f32[96,768]{1,0:T(8,128)S(1)}, u32[]{:S(2)}, u32[]{:S(2)}) collective-permute-start(f32[96,768]{1,0:T(8,128)S(1)} %copy-done.71), channel_id=1, source_target_pairs={{0,1},{1,0},{2,3},{3,2},{4,5},{5,4},{6,7},{7,6},{8,9},{9,8},{10,11... | collective-permute-start | bytes 884744 | tf_op jit(solution)/shard_map/ppermute | solution.py:539
  253.7 15.6 %collective-permute-start.53 = (f32[192,768]{1,0:T(8,128)S(1)}, f32[192,768]{1,0:T(8,128)S(1)}, u32[]{:S(2)}, u32[]{:S(2)}) collective-permute-start(f32[192,768]{1,0:T(8,128)S(1)} %pad_maximum_fusion.18), channel_id=1, source_target_pairs={{0,8},{4,12},{8,0},{12,4},{16,24},{20,28},{24,16},{28,20},{1,9},{5... | collective-permute-start | bytes 1769480 | tf_op jit(solution)/shard_map/ppermute | solution.py:543
  254.4 15.0 %collective-permute-start.55 = (f32[4,72,768]{2,1,0:T(8,128)S(1)}, f32[4,72,768]{2,1,0:T(8,128)S(1)}, u32[]{:S(2)}, u32[]{:S(2)}) collective-permute-start(f32[4,72,768]{2,1,0:T(8,128)S(1)} %get-tuple-element.1387), channel_id=1, source_target_pairs={{0,4},{4,0},{8,12},{12,8},{16,20},{20,16},{24,28},{28,24},{1,5},{5... | collective-permute-start | bytes 2654216 | tf_op jit(solution)/shard_map/ppermute | solution.py:543
  254.4 15.0 %collective-permute-start.52 = (f32[176,768]{1,0:T(8,128)S(1)}, f32[176,768]{1,0:T(8,128)S(1)}, u32[]{:S(2)}, u32[]{:S(2)}) collective-permute-start(f32[176,768]{1,0:T(8,128)S(1)} %get-tuple-element.1370.refs_4_), channel_id=1, source_target_pairs={{0,1},{1,0},{2,3},{3,2},{4,5},{5,4},{6,7},{7,6},{8,9},{9,8},{10,11... | collective-permute-start | bytes 1622024 | tf_op jit(solution)/shard_map/ppermute | solution.py:539
  269.7 22.1 %collective-permute-start.59 = (f32[256,768]{1,0:T(8,128)S(1)}, f32[256,768]{1,0:T(8,128)S(1)}, u32[]{:S(2)}, u32[]{:S(2)}) collective-permute-start(f32[256,768]{1,0:T(8,128)S(1)} %pad_maximum_fusion.5), channel_id=1, source_target_pairs={{0,16},{4,20},{8,24},{12,28},{16,0},{20,4},{24,8},{28,12},{1,17},{... | collective-permute-start | bytes 2359304 | tf_op jit(solution)/shard_map/ppermute | solution.py:543
  271.1 20.8 %collective-permute-start.58 = (f32[272,768]{1,0:T(8,128)S(1)}, f32[272,768]{1,0:T(8,128)S(1)}, u32[]{:S(2)}, u32[]{:S(2)}) collective-permute-start(f32[272,768]{1,0:T(8,128)S(1)} %pad_maximum_fusion.4), channel_id=1, source_target_pairs={{0,8},{4,12},{8,0},{12,4},{16,24},{20,28},{24,16},{28,20},{1,9},{5... | collective-permute-start | bytes 2506760 | tf_op jit(solution)/shard_map/ppermute | solution.py:543
  272.6 19.2 %collective-permute-start.57 = (f32[184,768]{1,0:T(8,128)S(1)}, f32[184,768]{1,0:T(8,128)S(1)}, u32[]{:S(2)}, u32[]{:S(2)}) collective-permute-start(f32[184,768]{1,0:T(8,128)S(1)} %pad_maximum_fusion.19), channel_id=1, source_target_pairs={{0,1},{1,0},{2,3},{3,2},{4,5},{5,4},{6,7},{7,6},{8,9},{9,8},{10,11... | collective-permute-start | bytes 1695752 | tf_op jit(solution)/shard_map/ppermute | solution.py:539
  273.5 18.3 %collective-permute-start.61 = (f32[72,768]{1,0:T(8,128)S(1)}, f32[72,768]{1,0:T(8,128)S(1)}, u32[]{:S(2)}, u32[]{:S(2)}) collective-permute-start(f32[72,768]{1,0:T(8,128)S(1)} %slice_add_fusion.13), channel_id=1, source_target_pairs={{0,2},{1,3},{2,0},{3,1},{4,6},{5,7},{6,4},{7,5},{8,10},{9,11},{10,... | collective-permute-start | bytes 663560 | tf_op jit(solution)/shard_map/ppermute | solution.py:539
  275.8 16.1 %collective-permute-start.60 = (f32[16,768]{1,0:T(8,128)S(1)}, f32[16,768]{1,0:T(8,128)S(1)}, u32[]{:S(2)}, u32[]{:S(2)}) collective-permute-start(f32[16,768]{1,0:T(8,128)S(1)} %add.247), channel_id=1, source_target_pairs={{0,8},{4,12},{8,0},{12,4},{16,24},{20,28},{24,16},{28,20},{1,9},{5... | collective-permute-start | bytes 147464 | tf_op jit(solution)/shard_map/ppermute | solution.py:543
  309.1 14.3 %collective-permute-start.71 = (f32[96,768]{1,0:T(8,128)S(1)}, f32[96,768]{1,0:T(8,128)S(1)}, u32[]{:S(2)}, u32[]{:S(2)}) collective-permute-start(f32[96,768]{1,0:T(8,128)S(1)} %pad_maximum_fusion.22), channel_id=1, source_target_pairs={{0,24},{4,28},{8,16},{12,20},{16,8},{20,12},{24,0},{28,4},{1,25},{... | collective-permute-start | bytes 884744 | tf_op jit(solution)/shard_map/ppermute | solution.py:543
  (128 other events, 1033.5 us)
